TPU v7x, 32 devices: a whole 2x2x4 slice. The times are simulated.
32 devices in a mesh: parts: 2 (over y), gx: 4 (over z), gy: 4 (over x, core).
Axes of the slice: x: 2, y: 2, z: 4, core: 2. Of those that a mesh axis runs over, the one named last changes fastest.
Arguments:
- cell_x: int32 [131072], P(('parts', 'gx', 'gy')), parts along dimension 0, may hold values from 0 to 63
- cell_y: int32 [131072], P(('parts', 'gx', 'gy')), parts along dimension 0, may hold values from 0 to 63
- cell_z: int32 [131072], P(('parts', 'gx', 'gy')), parts along dimension 0, may hold values from 0 to 255
- fraction: float32 [3, 131072], P(None, ('parts', 'gx', 'gy')), parts along dimension 1, may hold values from 0 to 1
- charge: float32 [131072], P(('parts', 'gx', 'gy')), parts along dimension 0, may hold values from -6 to 6
Outputs:
- charge_potential: float32 [131072], P(('parts', 'gx', 'gy')), parts along dimension 0
- forces: float32 [3, 131072], P(None, ('parts', 'gx', 'gy')), parts along dimension 1
There are 2 independent parts, one for each index of `parts`. A program takes and returns all parts, laid end to end along the dimension named above; each array names one. Nothing has to cross between parts.
Inputs may be any that keep to these rules, and one draw needn't show every extreme that they name: `cell_x`: a charge's cell along the first dimension, local to its device. `cell_y`: a charge's cell along the second dimension, local to its device.
All inputs are finite; a program needn't handle non-finite values.
Results may differ from a plain program's by a relative error of at most 0.0003.
Values sent between devices are 32-bit elements; how exact they have to be, the bound alone decides.
No kernel may reach another device: no remote copies, remote signals or barrier semaphores. Data moves between devices by JAX's collectives and lax.ppermute only.
A program may use at most 384 MiB of HBM per device.

v0:
```python
import jax
import jax.numpy as jnp
from jax import lax
from jax.sharding import PartitionSpec as P

N = 256


def with_halo(value, sides, width):
    for axis, dim in sides:
        devices, length = (lax.axis_size(axis), value.shape[dim])
        up = [(i, (i + 1) % devices) for i in range(devices)]
        down = [(j, i) for i, j in up]
        last = lax.slice_in_dim(value, length - width, length, axis=dim)
        leading = lax.slice_in_dim(value, 0, width, axis=dim)
        before = lax.ppermute(last, axis, up)
        after = lax.ppermute(leading, axis, down)
        value = jnp.concatenate([before, value, after], axis=dim)
    return value


def table_part(rows, columns, size):
    product = rows[:, None] * columns[None, :] % size
    angle = product.astype(jnp.float32) * (2.0 * jnp.pi / size)
    return jnp.cos(angle) + jnp.sin(angle)


def spline(param):
    rest = 1.0 - param
    square = param * param
    cube = square * param
    weights = [
        rest * rest * rest / 6.0,
        (3.0 * cube - 6.0 * square + 4.0) / 6.0,
        (-3.0 * cube + 3.0 * square + 3.0 * param + 1.0) / 6.0,
        cube / 6.0,
    ]
    slopes = [
        -rest * rest / 2.0,
        1.5 * square - 2.0 * param,
        -1.5 * square + param + 0.5,
        square / 2.0,
    ]
    return (weights, slopes)


def place(first, weights, length, wrap):
    places = jnp.arange(length, dtype=jnp.int32)
    result = jnp.zeros((first.shape[0], length), jnp.float32)
    for offset in range(4):
        target = first + offset
        if wrap:
            target = target % length
        result = result + weights[offset][:, None] * (places[None, :] == target[:, None]).astype(
            jnp.float32
        )
    return result


def symbol(index, size):
    sines = 2.0 * jnp.sin(jnp.pi * index.astype(jnp.float32) / size)
    return sines * sines


def green_of(freq_a, freq_b, freq_c, grid_size):
    total = (
        symbol(freq_a, grid_size)[:, None, None]
        + symbol(freq_b, grid_size)[None, :, None]
        + symbol(freq_c, grid_size)[None, None, :]
    )
    safe = jnp.where(total > 0, total, jnp.float32(1.0))
    return jnp.where(total > 0, jnp.exp(-0.5 * total) / safe, jnp.float32(0.0)) / float(
        grid_size * grid_size * grid_size
    )


def apply_y(field, grid_size):
    high = lax.Precision.HIGHEST
    rows_here = field.shape[0]
    flat = field.reshape(rows_here, -1)
    own = lax.axis_index("gy") * rows_here + jnp.arange(rows_here, dtype=jnp.int32)
    wanted = jnp.arange(lax.axis_size("gy") * rows_here, dtype=jnp.int32)
    summed = lax.psum_scatter(
        jnp.dot(table_part(wanted, own, grid_size), flat, precision=high),
        "gy",
        scatter_dimension=0,
        tiled=True,
    )
    return summed.reshape(field.shape)


def fold_rims(padded, axis_dim, inner):
    middle = lax.slice_in_dim(padded, 4, 4 + inner, axis=axis_dim)
    lower = lax.slice_in_dim(padded, 0, 2, axis=axis_dim)
    upper = lax.slice_in_dim(padded, inner + 6, inner + 8, axis=axis_dim)
    widths_low = [(0, 0)] * 3
    widths_high = [(0, 0)] * 3
    widths_low[axis_dim] = (0, inner - 2)
    widths_high[axis_dim] = (inner - 2, 0)
    return middle + jnp.pad(lower, widths_low) + jnp.pad(upper, widths_high)


def shards(cell_x, cell_y, cell_z, fraction, charge):
    high = lax.Precision.HIGHEST
    grid_size = N
    planes_x = grid_size // lax.axis_size("gx")
    planes_y = grid_size // lax.axis_size("gy")
    weight_x, slope_x = spline(fraction[0])
    weight_y, slope_y = spline(fraction[1])
    weight_z, slope_z = spline(fraction[2])
    along_x = place(cell_x + 1, weight_x, planes_x + 4, False)
    along_y = place(cell_y + 1, weight_y, planes_y + 4, False)
    along_z = place(cell_z - 1, weight_z, grid_size, True)
    plane = (charge[:, None] * along_y)[:, :, None] * along_x[:, None, :]
    plane = plane.reshape(charge.shape[0], -1)
    spread = lax.dot_general(plane, along_z, (((0,), (0,)), ((), ())), precision=high)
    spread = spread.reshape(planes_y + 4, planes_x + 4, grid_size)
    padded = with_halo(spread, (("gx", 1), ("gy", 0)), 2)
    density = fold_rims(fold_rims(padded, 1, planes_x), 0, planes_y)
    full_index = jnp.arange(grid_size, dtype=jnp.int32)
    table = table_part(full_index, full_index, grid_size)
    spectrum = jnp.dot(density.reshape(-1, grid_size), table, precision=high).reshape(density.shape)
    spectrum = apply_y(spectrum, grid_size)
    pencil = lax.all_to_all(spectrum, "gx", split_axis=2, concat_axis=1, tiled=True)
    pencil = jnp.einsum("kx,yxz->ykz", table, pencil, precision=high)
    depth = pencil.shape[2]
    freq_y = lax.axis_index("gy") * planes_y + jnp.arange(planes_y, dtype=jnp.int32)
    freq_z = lax.axis_index("gx") * depth + jnp.arange(depth, dtype=jnp.int32)
    green = green_of(freq_y, full_index, freq_z, grid_size)
    pencil = jnp.einsum("kx,yxz->ykz", table, pencil * green, precision=high)
    spectrum = lax.all_to_all(pencil, "gx", split_axis=1, concat_axis=2, tiled=True)
    spectrum = apply_y(spectrum, grid_size)
    potential = jnp.dot(spectrum.reshape(-1, grid_size), table, precision=high).reshape(
        spectrum.shape
    )
    nearby = with_halo(potential, (("gx", 1), ("gy", 0)), 2)
    slope_along_z = place(cell_z - 1, slope_z, grid_size, True)
    both_z = jnp.concatenate([along_z, slope_along_z], axis=0)
    sampled = lax.dot_general(
        nearby.reshape(-1, grid_size), both_z, (((1,), (1,)), ((), ())), precision=high
    )
    sampled = sampled.reshape(planes_y + 4, planes_x + 4, 2 * charge.shape[0])
    count = charge.shape[0]
    value_part = sampled[:, :, :count]
    slope_part = sampled[:, :, count:]
    slope_along_x = place(cell_x + 1, slope_x, planes_x + 4, False)
    slope_along_y = place(cell_y + 1, slope_y, planes_y + 4, False)
    value = jnp.einsum("yxc,cy,cx->c", value_part, along_y, along_x, precision=high)
    grad_x = jnp.einsum("yxc,cy,cx->c", value_part, along_y, slope_along_x, precision=high)
    grad_y = jnp.einsum("yxc,cy,cx->c", value_part, slope_along_y, along_x, precision=high)
    grad_z = jnp.einsum("yxc,cy,cx->c", slope_part, along_y, along_x, precision=high)
    forces = -charge[None, :] * jnp.stack([grad_x, grad_y, grad_z], axis=0)
    return (charge * value, forces)


def solution(mesh):
    placed = (
        P(("parts", "gx", "gy")),
        P(("parts", "gx", "gy")),
        P(("parts", "gx", "gy")),
        P(None, ("parts", "gx", "gy")),
        P(("parts", "gx", "gy")),
    )
    return jax.shard_map(
        shards,
        mesh=mesh,
        in_specs=placed,
        out_specs=(P(("parts", "gx", "gy")), P(None, ("parts", "gx", "gy"))),
        check_vma=False,
    )
```

profile of v0, /device:TPU:0, one launch (start us, length us, event | category | flops | bytes accessed | tf_op | source)
XLA Modules:
  0.0 1162.2 jit_solution(14551360954450162519)
XLA Ops:
  14.4 25.2 %broadcast_multiply_fusion = f32[4096,68,68]{0,2,1:T(8,128)} fusion(f32[4096,68]{0,1:T(8,128)S(1)} %get-tuple-element.23, f32[4096,68]{0,1:T(8,128)S(1)} %get-tuple-element.18), kind=kLoop, calls=%fused_computation.6 | loop fusion | flops 18939904 | bytes 77987840 | tf_op jit(solution)/shard_map/mul | solution.py:114
  39.5 61.5 %mul.748 = f32[4096,4624]{0,1:T(8,128)} reshape(f32[4096,68,68]{0,2,1:T(8,128)} %broadcast_multiply_fusion) | data formatting | bytes 151519232 | tf_op jit(solution)/shard_map/mul | solution.py:114
  101.0 61.8 %dot_general.53 = f32[68,68,4096]{2,1,0:T(8,128)} reshape(f32[4624,4096]{1,0:T(8,128)} %bitcast.5) | data formatting | bytes 151519232 | tf_op jit(solution)/shard_map/dot_general | solution.py:116
  169.5 75.1 %fusion.32 = f32[68,68,256]{2,1,0:T(8,128)S(1)} fusion(f32[68,68,4096]{2,1,0:T(8,128)} %dot_general.53, f32[4096,256,1]{1,0,2:T(8,128)} %fusion.152), kind=kOutput, calls=%fused_computation.47 | convolution fusion | flops 58183385088 | bytes 84688896 | tf_op jit(solution)/shard_map/dot_general | solution.py:116
  277.8 18.9 %fusion.62 = f32[256,16384]{1,0:T(8,128)} fusion(f32[64,16384]{1,0:T(8,128)} %reshape_reshape.4, s32[64]{0:T(128)S(1)} %iota_add_fusion), kind=kOutput, calls=%fused_computation.113 | convolution fusion | flops 3221471232 | bytes 20971776 | tf_op jit(solution)/shard_map/dot_general | solution.py:84
  296.7 126.4 %reduce-scatter.3.cloned.1.call-done = f32[64,16384]{1,0:T(8,128)} async-done(((f32[256,16384]{1,0:T(8,128)}), f32[64,16384]{1,0:T(8,128)}) %reduce-scatter.3.cloned.1.call-update) | async-done | bytes 4194320 | tf_op jit(solution)/shard_map/reduce_scatter | solution.py:83
  428.6 9.2 copy.10
  437.7 8.6 reshape.610
  451.5 93.2 %all-to-all-done = f32[4,1,262144]{2,1,0:T(1,128)} async-done(((f32[4,1,262144]{2,1,0:T(1,128)}), f32[4,1,262144]{2,1,0:T(1,128)}, u32[]{:S(2)}, u32[]{:S(2)}) %all-to-all-start) | async-done | bytes 4194336 | tf_op jit(solution)/shard_map/all_to_all | solution.py:124
  545.2 24.6 %reduce.14 = f32[4,262144]{1,0:T(4,128)} reduce(f32[4,1,262144]{2,1,0:T(1,128)} %all-to-all-done, f32[]{:T(128)} %broadcast.808), dimensions={1}, to_apply=%all_to_all.24.reduce_sub_computation | reduce | bytes 8388612 | tf_op jit(solution)/shard_map/all_to_all | solution.py:124
  569.9 9.3 reshape.611
  579.1 12.0 %copy.58 = f32[64,64,4,64]{1,2,3,0:T(4,128)} copy(f32[64,64,4,64]{1,0,3,2:T(8,128)} %bitcast.84) | data formatting | bytes 8388608 | tf_op jit(solution)/shard_map/all_to_all | solution.py:124
  591.1 8.9 all_to_all.27
  614.5 9.2 copy.13
  623.7 8.8 reshape.612
  632.5 98.4 %all_to_all.33 = f32[4,1,262144]{2,1,0:T(1,128)} all-to-all(f32[4,1,262144]{2,1,0:T(1,128)} %reshape.612), channel_id=1, replica_groups=mesh['parts'=2,'gx'=4,'gy'=4] {'gx'}, dimensions={0} | all-to-all | bytes 8388608 | tf_op jit(solution)/shard_map/all_to_all | solution.py:131
  730.9 15.2 %reduce.15 = f32[4,262144]{1,0:T(4,128)} reduce(f32[4,1,262144]{2,1,0:T(1,128)} %all_to_all.33, f32[]{:T(128)} %broadcast.808), dimensions={1}, to_apply=%all_to_all.28.reduce_sub_computation | reduce | bytes 8388612 | tf_op jit(solution)/shard_map/all_to_all | solution.py:131
  746.1 9.3 reshape.613
  755.4 12.0 %copy.59 = f32[64,4,64,64]{3,1,2,0:T(4,128)} copy(f32[64,4,64,64]{3,0,2,1:T(8,128)} %bitcast.86) | data formatting | bytes 8388608 | tf_op jit(solution)/shard_map/all_to_all | solution.py:131
  767.4 9.2 reshape.588
  776.5 19.3 %fusion.61 = f32[256,16384]{1,0:T(8,128)} fusion(f32[64,16384]{1,0:T(8,128)} %reshape.588, s32[64]{0:T(128)S(1)} %iota_add_fusion), kind=kOutput, calls=%fused_computation.112 | convolution fusion | flops 3221471232 | bytes 20971776 | tf_op jit(solution)/shard_map/dot_general | solution.py:84
  795.8 124.4 %reduce-scatter.5.cloned.1.call-done = f32[64,16384]{1,0:T(8,128)} async-done(((f32[256,16384]{1,0:T(8,128)}), f32[64,16384]{1,0:T(8,128)}) %reduce-scatter.5.cloned.1.call-update) | async-done | bytes 4194320 | tf_op jit(solution)/shard_map/reduce_scatter | solution.py:83
  949.2 139.4 %fusion.2 = f32[68,68,8192]{2,1,0:T(8,128)} fusion(f32[2,68,256]{2,1,0:T(8,128)} %collective-permute-done.7, f32[64,2,256]{2,1,0:T(2,128)S(1)} %collective-permute-done.5, f32[64,64,256]{2,1,0:T(8,128)} %copy-done.1, f32[64,2,256]{2,1,0:T(2,128)S(1)} %collective-permute-done.4, f32[2,68,256]{2,1,0:T(8,128)} %collective-permute-done.6, ...), kind=kOutput, calls=%fused_computation.8 | convolution fusion | flops 116371505152 | bytes 164642816 | tf_op jit(solution)/shard_map/dot_general | solution.py:139
  1088.6 51.9 %fusion.1 = (f32[4096,68]{0,1:T(8,128)}, f32[4096,68]{0,1:T(8,128)}, f32[4096,68]{0,1:T(8,128)}) fusion(f32[68,68,8192]{2,1,0:T(8,128)} %fusion.2, f32[4096,68]{0,1:T(8,128)S(1)} %copy-done.4, f32[4096,68]{0,1:T(8,128)} %get-tuple-element.19), kind=kLoop, calls=%fused_computation.2 | loop fusion | flops 112803840 | bytes 157089792
  (85 shorter events, 115.8 us)
Async XLA Ops:
  7.2 416.0 %reduce-scatter.3.cloned.1.call-start = ((), (), s32[]{:S(2)}) async-start(), calls=%async_computation.4 | async-start | bytes 20971520 | tf_op jit(solution)/shard_map/reduce_scatter | solution.py:83
  11.5 2.9 copy-start.2
  101.0 61.9 %copy-start.7 = (s32[4096]{0:T(1024)S(1)}, s32[4096]{0:T(1024)}, u32[]{:S(2)}) copy-start(s32[4096]{0:T(1024)} %param.7) | copy-start | bytes 49156
  244.7 11.5 copy-start
  244.8 9.6 collective-permute-start
  247.8 8.4 collective-permute-start.1
  256.2 4.6 collective-permute-start.2
  256.3 5.2 collective-permute-start.3
  258.0 6.3 slice-start
  258.0 6.3 slice-start.1
  258.0 6.3 copy-start.8
  446.4 98.3 %all-to-all-start = ((f32[4,1,262144]{2,1,0:T(1,128)}), f32[4,1,262144]{2,1,0:T(1,128)}, u32[]{:S(2)}, u32[]{:S(2)}) async-start(f32[4,1,262144]{2,1,0:T(1,128)} %reshape.610), calls=%async_computation.1 | async-start | bytes 8388608 | tf_op jit(solution)/shard_map/all_to_all | solution.py:124
  451.2 469.1 %reduce-scatter.5.cloned.1.call-start = ((), (), s32[]{:S(2)}) async-start(), calls=%async_computation.5 | async-start | bytes 20971520 | tf_op jit(solution)/shard_map/reduce_scatter | solution.py:83
  928.4 10.6 copy-start.1
  928.6 10.5 collective-permute-start.4
  930.1 9.0 collective-permute-start.5
  939.8 9.3 collective-permute-start.6
  939.8 9.3 collective-permute-start.7
  941.6 3.8 copy-start.3
  949.2 139.4 %copy-start.4 = (f32[4096,68]{0,1:T(8,128)S(1)}, f32[4096,68]{0,1:T(8,128)}, u32[]{:S(2)}) copy-start(f32[4096,68]{0,1:T(8,128)} %get-tuple-element.17) | copy-start | bytes 3342340
  1140.6 5.7 copy-start.5
  1148.1 5.7 copy-start.6
Sparse Core Ops, SparseCore 0:
  296.9 126.2 reduce-scatter.2
  796.0 124.2 reduce-scatter.4
where the time goes:
time: 1170 us; the launch traced here: 1160 us
  waiting for transfers between devices  354 us (30%)
  matrix products  278 us (24%)
  local copies, waits for them, and re-layouts  247 us (21%)
  other arithmetic  153 us (13%)
  blocking collectives  98.4 us (8%)
  starting transfers between devices  17.7 us (2%)
  between operations  14.6 us (1%)
    reduce_scatter x2, waiting for transfers between devices, apply_y(): lax.psum_scatter(jnp.dot(table_part(wanted, own, grid_size), flat, precis...  251 us
    dot_general x1, matrix products, shards(): lax.dot_general(nearby.reshape(-1, grid_size), both_z, (((1,), (1,)), (()...  139 us
    all_to_all x1, blocking collectives, shards(): lax.all_to_all(pencil, 'gx', split_axis=1, concat_axis=2, tiled=True)  98.4 us
    all_to_all x1, waiting for transfers between devices, shards(): lax.all_to_all(spectrum, 'gx', split_axis=2, concat_axis=1, tiled=True)  93.2 us
    dot_general x1, matrix products, shards(): lax.dot_general(plane, along_z, (((0,), (0,)), ((), ())), precision=high)  75.1 us
    dot_general x1, local copies, waits for them, and re-layouts, shards(): lax.dot_general(plane, along_z, (((0,), (0,)), ((), ())), precision=high)  61.8 us
    mul x1, local copies, waits for them, and re-layouts, shards(): plane = (charge[:, None] * along_y)[:, :, None] * along_x[:, None, :]  61.5 us
    unnamed x2, other arithmetic  51.9 us
  transfers between devices with their start and end apart: 11, of which 7 were waited for; matrix products, arithmetic and copies ran while one was open for 1% of the time, Pallas kernels for 0%

commit v1 on v0

v1 whole, which is shorter than its diff:
```python
import functools

import jax
import jax.numpy as jnp
import numpy as np
from jax import lax
from jax.experimental import pallas as pl
from jax.experimental.pallas import tpu as pltpu
from jax.sharding import PartitionSpec as P

N = 256
LANES = 128
ROWS = 16
PLANES = 8
PAD = 16
F32 = jnp.float32
BF16 = jnp.bfloat16

SIN_PI = (3.141592640130707, -5.167710083507877, 2.550077523214437, -0.5982912856197345, 0.07765766030450941)
COS_PI = (
    0.9999999997799038,
    -4.934802137078749,
    4.058709159554242,
    -1.335212003029471,
    0.23493731372678894,
    -0.024396324214549327,
)


def poly(coefficients, x):
    result = coefficients[-1]
    for value in coefficients[-2::-1]:
        result = result * x + F32(value)
    return result


def spline(param):
    rest = 1.0 - param
    square = param * param
    cube = square * param
    return [
        rest * rest * rest * F32(1 / 6),
        (3.0 * cube - 6.0 * square + 4.0) * F32(1 / 6),
        (-3.0 * cube + 3.0 * square + 3.0 * param + 1.0) * F32(1 / 6),
        cube * F32(1 / 6),
    ]


def slopes(param):
    rest = 1.0 - param
    square = param * param
    return [
        rest * rest * F32(-0.5),
        1.5 * square - 2.0 * param,
        -1.5 * square + param + 0.5,
        square * F32(0.5),
    ]


def split(value):
    high = value.astype(BF16)
    return high, (value - high.astype(F32)).astype(BF16)


def wide(row, rows):
    return jnp.broadcast_to(row, (rows, row.shape[1]))


def pick(offset, options):
    result = jnp.zeros(offset.shape, F32)
    for i in (3, 2, 1, 0):
        result = jnp.where(offset == F32(i), wide(options[i], offset.shape[0]), result)
    return result


def iota(rows):
    return lax.broadcasted_iota(jnp.int32, (rows, LANES), 0).astype(F32)


def rotation(tab, row_y):
    turn = tab[0] * wide(row_y, ROWS)
    turn = turn - jnp.round(turn)
    square = turn * turn
    sine = turn * poly(SIN_PI, square)
    cosine = poly(COS_PI, square)
    full_cos = 1.0 - 2.0 * sine * sine
    full_sin = 2.0 * sine * cosine
    return full_cos + full_sin, full_cos - full_sin


def along_y(tab, plus, minus, options):
    w = [wide(o, ROWS) for o in options]
    even = w[0] + tab[1] * w[1] + tab[2] * w[2] + tab[3] * w[3]
    odd = tab[4] * w[1] + tab[5] * w[2] + tab[6] * w[3]
    return even * plus + odd * minus


def z_tiles(row_z, options_list):
    tile = jnp.floor(row_z * F32(1 / 16))
    first = iota(16) - wide(row_z - 16.0 * tile, 16)
    here = wide(tile, 16)
    after = jnp.where(here == F32(N // 16 - 1), F32(0.0), here + 1.0)
    here = here.astype(BF16)
    after = after.astype(BF16)
    results = [[] for _ in range(2 * len(options_list))]
    pieces = []
    for options in options_list:
        pieces.append((*split(pick(first, options)), *split(pick(first + 16.0, options))))
    zero = jnp.zeros((16, LANES), BF16)
    for t in range(N // 16):
        at_here = here == BF16(t)
        at_after = after == BF16(t)
        for i, (h0, l0, h1, l1) in enumerate(pieces):
            results[2 * i].append(jnp.where(at_here, h0, jnp.where(at_after, h1, zero)))
            results[2 * i + 1].append(jnp.where(at_here, l0, jnp.where(at_after, l1, zero)))
    return [jnp.concatenate(r, axis=0) for r in results]


def lanes(parts):
    return parts[0] if len(parts) == 1 else jnp.concatenate(parts, axis=1)


def row(values, i):
    return [v[i : i + 1] for v in values]


NT = (((1,), (1,)), ((), ()))


def spread_kernel(group, unroll, steps, base_ref, pass_ref, tab_ref, in_ref, out_ref):
    a = pl.program_id(0)
    i = pl.program_id(1)

    @pl.when((a == 0) & (i == 0))
    def _():
        out_ref[...] = jnp.zeros_like(out_ref)

    tab = [tab_ref[m] for m in range(7)]
    for u in range(unroll):
        index = (a * steps + i) * unroll + u
        base = base_ref[index]
        sets = []
        z_high, z_low = [], []
        for j in range(group):
            rows = in_ref[0, j, :, u * LANES : (u + 1) * LANES]
            w = spline(rows)
            plus, minus = rotation(tab, rows[1:2])
            y = along_y(tab, plus, minus, row(w, 4)) * wide(rows[6:7], ROWS)
            high, low = z_tiles(rows[2:3], [row(w, 5)])
            z_high.append(high)
            z_low.append(low)
            sets.append((rows[0:1], row(w, 3), y))
        z_high, z_low = lanes(z_high), lanes(z_low)

        def one_pass(start):
            highs, lows = [], []
            for row_x, w, y in sets:
                x = pick(iota(PLANES) + (start.astype(F32) - wide(row_x, PLANES)), w)
                pieces = [split(wide(x[m : m + 1], ROWS) * y) for m in range(PLANES)]
                highs.append(jnp.concatenate([p[0] for p in pieces], axis=0))
                lows.append(jnp.concatenate([p[1] for p in pieces], axis=0))
            high, low = lanes(highs), lanes(lows)
            both = lax.dot_general(
                jnp.concatenate([high, low], axis=0), z_high, NT, preferred_element_type=F32
            )
            rows_in = PLANES * ROWS
            total = both[:rows_in] + both[rows_in:]
            total += lax.dot_general(high, z_low, NT, preferred_element_type=F32)
            total = total.reshape(PLANES, ROWS, N)
            for h in range(N // LANES):
                out_ref[h, pl.ds(start, PLANES)] += total[:, :, h * LANES : (h + 1) * LANES]

        one_pass(base)

        def more(p, carry):
            one_pass(base + p * PLANES)
            return carry

        lax.fori_loop(1, pass_ref[index], more, 0)

    @pl.when((a == pl.num_programs(0) - 1) & (i == pl.num_programs(1) - 1))
    def _():
        for h in range(N // LANES):
            out_ref[h, N] += out_ref[h, 0]
            out_ref[h, 1:3] += out_ref[h, N + 1 : N + 3]


def sample_kernel(group, unroll, steps, base_ref, pass_ref, tab_ref, in_ref, high_ref, low_ref, out_ref):
    a = pl.program_id(0)
    i = pl.program_id(1)
    tab = [tab_ref[m] for m in range(7)]
    for u in range(unroll):
        index = (a * steps + i) * unroll + u
        base = base_ref[index]
        sets = []
        tiles = [[] for _ in range(4)]
        for j in range(group):
            rows = in_ref[0, j, :, u * LANES : (u + 1) * LANES]
            w = spline(rows)
            s = slopes(rows)
            plus, minus = rotation(tab, rows[1:2])
            y = along_y(tab, plus, minus, row(w, 4))
            y_slope = along_y(tab, plus, minus, row(s, 4))
            for k, t in enumerate(z_tiles(rows[2:3], [row(w, 5), row(s, 5)])):
                tiles[k].append(t)
            sets.append((rows[0:1], row(w, 3), row(s, 3), y, y_slope))
        z_high, z_low, s_high, s_low = [lanes(t) for t in tiles]
        z_all = jnp.concatenate([z_high, z_high, z_low], axis=0)
        s_all = jnp.concatenate([s_high, s_high, s_low], axis=0)

        def one_pass(start):
            high = high_ref[pl.ds(start, PLANES)].reshape(PLANES * ROWS, N)
            low = low_ref[pl.ds(start, PLANES)].reshape(PLANES * ROWS, N)
            field = jnp.concatenate([high, low, high], axis=1)
            value = jnp.dot(field, z_all, preferred_element_type=F32)
            slope = jnp.dot(field, s_all, preferred_element_type=F32)
            results = []
            for j, (row_x, w, s, y, y_slope) in enumerate(sets):
                offset = iota(PLANES) + (start.astype(F32) - wide(row_x, PLANES))
                x = pick(offset, w)
                x_slope = pick(offset, s)
                sums = [jnp.zeros((ROWS, LANES), F32) for _ in range(4)]
                for m in range(PLANES):
                    v = value[m * ROWS : (m + 1) * ROWS, j * LANES : (j + 1) * LANES]
                    g = slope[m * ROWS : (m + 1) * ROWS, j * LANES : (j + 1) * LANES]
                    wx = wide(x[m : m + 1], ROWS)
                    sx = wide(x_slope[m : m + 1], ROWS)
                    sums[0] += v * wx
                    sums[1] += v * sx
                    sums[3] += g * wx
                results.append(
                    jnp.concatenate(
                        [
                            jnp.sum(sums[0] * y, axis=0, keepdims=True),
                            jnp.sum(sums[1] * y, axis=0, keepdims=True),
                            jnp.sum(sums[0] * y_slope, axis=0, keepdims=True),
                            jnp.sum(sums[3] * y, axis=0, keepdims=True),
                        ],
                        axis=0,
                    )
                )
            return results

        for j, r in enumerate(one_pass(base)):
            out_ref[0, j, :, u * LANES : (u + 1) * LANES] = r

        def more(p, carry):
            for j, r in enumerate(one_pass(base + p * PLANES)):
                out_ref[0, j, :, u * LANES : (u + 1) * LANES] += r
            return carry

        lax.fori_loop(1, pass_ref[index], more, 0)


def filter_kernel(table_ref, green_ref, in_ref, high_ref, low_ref, field):
    k = pl.program_id(0)
    t_high, t_low = split(table_ref[...])

    def right(value):
        high, low = split(value)
        both = jnp.dot(jnp.concatenate([high, low], axis=0), t_high, preferred_element_type=F32)
        return both[:N] + both[N:] + jnp.dot(high, t_low, preferred_element_type=F32)

    def left(value):
        high, low = split(value)
        both = jnp.dot(jnp.concatenate([t_high, t_low], axis=0), high, preferred_element_type=F32)
        return both[:N] + both[N:] + jnp.dot(t_high, low, preferred_element_type=F32)

    halves = range(N // LANES)
    value = lanes([in_ref.at[h][pl.ds(ROWS + k, N, ROWS), :] for h in halves])
    value = left(right(value)) * green_ref[0]
    value = right(left(value))
    for h in halves:
        field.at[h][pl.ds(ROWS + k, N, ROWS), :] = value[:, h * LANES : (h + 1) * LANES]

    @pl.when(k == pl.num_programs(0) - 1)
    def _():
        for h in halves:
            field[h, 0:ROWS, :] = field[h, N * ROWS : (N + 1) * ROWS, :]
            field[h, (N + 1) * ROWS : (N + PAD) * ROWS, :] = field[h, ROWS : PAD * ROWS, :]

        def part(x, carry):
            where = pl.ds(pl.multiple_of(x * (PLANES * ROWS), PLANES * ROWS), PLANES * ROWS)
            high, low = split(lanes([field[h, where, :] for h in halves]))
            high_ref[where, :] = high
            low_ref[where, :] = low
            return carry

        lax.fori_loop(0, (N + PAD) // PLANES, part, 0)


def table_part(rows, columns, size):
    product = rows[:, None] * columns[None, :] % size
    angle = product.astype(F32) * (2.0 * jnp.pi / size)
    return jnp.cos(angle) + jnp.sin(angle)


def symbol(index, size):
    sines = 2.0 * jnp.sin(jnp.pi * index.astype(F32) / size)
    return sines * sines


def green_of(freq_a, freq_b, freq_c, grid_size):
    total = (
        symbol(freq_a, grid_size)[:, None, None]
        + symbol(freq_b, grid_size)[None, :, None]
        + symbol(freq_c, grid_size)[None, None, :]
    )
    safe = jnp.where(total > 0, total, F32(1.0))
    return jnp.where(total > 0, jnp.exp(-0.5 * total) / safe, F32(0.0)) / float(
        grid_size * grid_size * grid_size
    )


def shards(cell_x, cell_y, cell_z, fraction, charge):
    count = charge.shape[0]
    n_x, n_y = lax.axis_size("gx"), lax.axis_size("gy")
    at_x, at_y = lax.axis_index("gx"), lax.axis_index("gy")
    planes_x, planes_y = N // n_x, N // n_y
    own = N // (n_x * n_y)
    chunks = count // LANES
    place = jnp.arange(count, dtype=jnp.int32)

    key, cy, cz, fx, fy, fz, q, order = lax.sort(
        (cell_x, cell_y, cell_z, fraction[0], fraction[1], fraction[2], charge, place),
        num_keys=1,
        is_stable=False,
    )
    plane = (key + at_x * planes_x).astype(F32)
    line = ((cy + (at_y * planes_y + N - 1)) % N).astype(F32)
    depth = ((cz + (N - 1)) % N).astype(F32)
    ends = plane.reshape(chunks, LANES)
    ends = jnp.concatenate([ends[:, 0], ends[:, -1], jnp.zeros((count - 2 * chunks,), F32)])
    packed = jnp.stack([plane, line, depth, fx, fy, fz, q, ends])
    everyone = lax.all_gather(packed, ("gx", "gy")).reshape(n_x, n_y, 8, count)

    ends = everyone[:, :, 7, : 2 * chunks]
    first = jnp.min(ends[:, :, :chunks], axis=1).astype(jnp.int32)
    last = jnp.max(ends[:, :, chunks:], axis=1).astype(jnp.int32)
    passes = ((last - first + (3 + PLANES)) // PLANES).reshape(-1)
    first = first.reshape(-1)

    freq = (at_x * n_y + at_y) * own + jnp.arange(ROWS, dtype=jnp.int32)
    angle = freq.astype(F32) * F32(2.0 * np.pi / N)
    offsets = jnp.arange(1, 4, dtype=F32)[:, None] * angle[None, :]
    tab = jnp.concatenate(
        [(freq.astype(F32) * F32(1.0 / N))[None], jnp.cos(offsets), jnp.sin(offsets)], axis=0
    )
    tab = jnp.broadcast_to(tab[:, :, None], (7, ROWS, LANES))
    full = jnp.arange(N, dtype=jnp.int32)
    table = table_part(full, full, N)
    green = green_of(freq[:own], full, full, N)

    unroll = 2 if chunks % 2 == 0 else 1
    steps = chunks // unroll
    size = N + PAD
    params = pltpu.CompilerParams(vmem_limit_bytes=50 * 1024 * 1024)
    in_spec = pl.BlockSpec((1, n_y, 8, unroll * LANES), lambda a, i, *_: (a, 0, 0, i))
    tab_spec = pl.BlockSpec((7, ROWS, LANES), lambda a, i, *_: (0, 0, 0))
    whole = pl.BlockSpec((size, ROWS, N), lambda a, i, *_: (0, 0, 0))
    mesh_part = pl.pallas_call(
        functools.partial(spread_kernel, n_y, unroll, steps),
        grid_spec=pltpu.PrefetchScalarGridSpec(
            num_scalar_prefetch=2,
            grid=(n_x, steps),
            in_specs=[tab_spec, in_spec],
            out_specs=pl.BlockSpec((N // LANES, size, ROWS, LANES), lambda a, i, *_: (0, 0, 0, 0)),
        ),
        out_shape=jax.ShapeDtypeStruct((N // LANES, size, ROWS, LANES), F32),
        compiler_params=params,
        name="spread",
    )(first, passes, tab, everyone)

    flat = jax.ShapeDtypeStruct((size * ROWS, N), BF16)
    flat_spec = pl.BlockSpec((size * ROWS, N), lambda k: (0, 0))
    high, low = pl.pallas_call(
        filter_kernel,
        grid=(own,),
        in_specs=[
            pl.BlockSpec((N, N), lambda k: (0, 0)),
            pl.BlockSpec((1, N, N), lambda k: (k, 0, 0)),
            pl.BlockSpec((N // LANES, size * ROWS, LANES), lambda k: (0, 0, 0)),
        ],
        out_specs=[flat_spec, flat_spec],
        out_shape=[flat, flat],
        scratch_shapes=[pltpu.VMEM((N // LANES, size * ROWS, LANES), F32)],
        compiler_params=params,
        name="filter",
    )(table, green, mesh_part.reshape(N // LANES, size * ROWS, LANES))

    partial = pl.pallas_call(
        functools.partial(sample_kernel, n_y, unroll, steps),
        grid_spec=pltpu.PrefetchScalarGridSpec(
            num_scalar_prefetch=2,
            grid=(n_x, steps),
            in_specs=[tab_spec, in_spec, whole, whole],
            out_specs=pl.BlockSpec((1, n_y, 4, unroll * LANES), lambda a, i, *_: (a, 0, 0, i)),
        ),
        out_shape=jax.ShapeDtypeStruct((n_x, n_y, 4, count), F32),
        compiler_params=params,
        name="sample",
    )(first, passes, tab, everyone, high.reshape(size, ROWS, N), low.reshape(size, ROWS, N))

    back = lax.all_to_all(
        partial.reshape(n_x * n_y, 4, count), ("gx", "gy"), split_axis=0, concat_axis=0, tiled=True
    )
    total = jnp.sum(back, axis=0)
    _, value, grad_x, grad_y, grad_z = lax.sort(
        (order, total[0], total[1], total[2], total[3]), num_keys=1, is_stable=False
    )
    forces = -charge[None, :] * jnp.stack([grad_x, grad_y, grad_z], axis=0)
    return (charge * value, forces)


def solution(mesh):
    placed = P(("parts", "gx", "gy"))
    return jax.shard_map(
        shards,
        mesh=mesh,
        in_specs=(placed, placed, placed, P(None, ("parts", "gx", "gy")), placed),
        out_specs=(placed, P(None, ("parts", "gx", "gy"))),
        check_vma=False,
    )
```

time: 1170 us -> 256 us (0.22)
  waiting for transfers between devices: 354 us -> 40 us
  matrix products: 278 us -> 0 us
  local copies, waits for them, and re-layouts: 247 us -> 6.23 us
  Pallas kernels: 0 us -> 149 us
  other arithmetic: 153 us -> 17.2 us
  blocking collectives: 98.4 us -> 28.1 us
  starting transfers between devices: 17.7 us -> 0.04 us
    dot_general x8 -> x0, matrix products: 278 us -> none  [the longest x1 139 us: shards(): lax.dot_general(nearby.reshape(-1, grid_size), both_z, (((1,), (1,)), (()...]
    reduce_scatter x2 -> x0, waiting for transfers between devices: 251 us -> none  [apply_y(): lax.psum_scatter(jnp.dot(table_part(wanted, own, grid_size), flat, precis...]
    pallas_call x0 -> x3, Pallas kernels: none -> 149 us  [the longest x1 68.3 us: shards(): pl.pallas_call(functools.partial(sample_kernel, n_y, unroll, steps), grid...]
    all_to_all x1 -> x0, waiting for transfers between devices: 93.2 us -> none  [shards(): lax.all_to_all(spectrum, 'gx', split_axis=2, concat_axis=1, tiled=True)]
    all_to_all x1, blocking collectives: 98.4 us -> 28.1 us  [shards(): lax.all_to_all(partial.reshape(n_x * n_y, 4, count), ('gx', 'gy'), split_...]
    dot_general x4 -> x0, local copies, waits for them, and re-layouts: 69.3 us -> none  [the longest x1 61.8 us: shards(): lax.dot_general(plane, along_z, (((0,), (0,)), ((), ())), precision=high)]
    mul x1 -> x0, local copies, waits for them, and re-layouts: 61.5 us -> none  [shards(): plane = (charge[:, None] * along_y)[:, :, None] * along_x[:, None, :]]
    unnamed x2 -> x0, other arithmetic: 51.9 us -> none
  transfers between devices with their start and end apart: 11 -> 1, of which waited for: 7 -> 1; matrix products, arithmetic and copies ran while one was open for 1% -> 2% of each run, Pallas kernels for 0% -> 0%
where the time goes in v1:
time: 256 us; the launch traced here: 255 us
  Pallas kernels  149 us (58%)
  waiting for transfers between devices  40 us (16%)
  blocking collectives  28.1 us (11%)
  other arithmetic  17.2 us (7%)
  between operations  14.2 us (6%)
  local copies, waits for them, and re-layouts  6.23 us (2%)
    pallas_call x1, Pallas kernels, shards(): pl.pallas_call(functools.partial(sample_kernel, n_y, unroll, steps), grid...  68.3 us
    pallas_call x1, Pallas kernels, shards(): pl.pallas_call(functools.partial(spread_kernel, n_y, unroll, steps), grid...  54.1 us
    all_gather x1, waiting for transfers between devices, shards(): everyone = lax.all_gather(packed, ('gx', 'gy')).reshape(n_x, n_y, 8, count)  40 us
    all_to_all x1, blocking collectives, shards(): lax.all_to_all(partial.reshape(n_x * n_y, 4, count), ('gx', 'gy'), split_...  28.1 us
    pallas_call x1, Pallas kernels, shards(): pl.pallas_call(filter_kernel, grid=(own,), in_specs=[pl.BlockSpec((N, N),...  26.9 us
    sort x1, other arithmetic, shards(): lax.sort((cell_x, cell_y, cell_z, fraction[0], fraction[1], fraction[2],...  5.83 us
    sort x1, other arithmetic, shards(): lax.sort((order, total[0], total[1], total[2], total[3]), num_keys=1, is_...  5.61 us
  transfers between devices with their start and end apart: 1, of which 1 were waited for; matrix products, arithmetic and copies ran while one was open for 2% of the time, Pallas kernels for 0%

profile of v1, /device:TPU:0, one launch (start us, length us, event | category | flops | bytes accessed | tf_op | source)
XLA Modules:
  0.0 255.1 jit_solution(15768281609720550268)
XLA Ops:
  7.2 1.0 fusion.15
  8.2 5.8 %sort.84 = (s32[4096]{0:T(1024)S(1)}, s32[4096]{0:T(1024)S(1)}, s32[4096]{0:T(1024)S(1)}, f32[4096]{0:T(1024)S(1)}, f32[4096]{0:T(1024)S(1)}, /*index=5*/f32[4096]{0:T(1024)S(1)}, f32[4096]{0:T(1024)S(1)}, s32[4096]{0:T(1024)S(1)}) sort(s32[4096]{0:T(1024)} %param.5, s32[4096]{0:T(1024)} %param.6, s32[4096]{0:T(1024)} %param.7, f32[4096]{0:T(1024)S(1)} %bitcast.43, ...), dimensions={0}, to_apply=%region_0.0 | sort | flops 49152 | bytes 262144 | tf_op jit(solution)/shard_map/sort | solution.py:324
  14.1 0.2 slice_reduce_fusion
  14.3 0.1 concatenate.6
  14.4 0.8 stack.47
  15.4 0.1 multiply_cosine_fusion
  15.5 1.0 sine_add_fusion.table_ref
  16.6 2.8 %fusion.1.green_ref = f32[16,256,256]{2,1,0:T(8,128)} fusion(f32[256]{0:T(256)S(1)} %multiply_multiply_fusion, f32[16,256]{1,0:T(8,128)S(1)} %broadcast_add_fusion), kind=kLoop, calls=%fused_computation.4 | loop fusion | flops 7340032 | bytes 4211712 | tf_op jit(solution)/shard_map/div | solution.py:310
  19.5 40.0 %all-gather.3.cloned.1.call-done = f32[128,4096]{1,0:T(8,128)} async-done(((f32[8,4096]{1,0:T(8,128)}), f32[128,4096]{1,0:T(8,128)}) %all-gather.3.cloned.1.call-update) | async-done | bytes 2097168 | tf_op jit(solution)/shard_map/all_gather | solution.py:335
  59.5 0.8 slice.50
  60.4 0.1 slice_reduce_fusion.2
  60.5 0.1 convert_element_type.68
  60.5 0.1 convert_element_type.66.base_ref
  60.6 0.1 broadcast_in_dim.9.tab_ref
  60.7 1.6 copy-done
  62.3 54.1 %spread.1 = f32[2,272,16,128]{3,2,1,0:T(8,128)} custom-call(s32[128]{0:T(128)S(1)} %convert_element_type.66.base_ref, s32[128]{0:T(128)S(1)} %and_select_fusion.pass_ref, f32[7,16,128]{2,1,0:T(8,128)S(1)} %broadcast_in_dim.9.tab_ref, f32[4,4,8,4096]{3,2,1,0:T(8,128)S(1)} %bitcast.27), custom_call_target="tpu_custom_call" | custom-call | tf_op jit(solution)/shard_map/spread/pallas_call | solution.py:361
  116.4 26.9 %filter.1 = (bf16[4352,256]{1,0:T(8,128)(2,1)S(1)}, bf16[4352,256]{1,0:T(8,128)(2,1)}) custom-call(f32[256,256]{1,0:T(8,128)S(1)} %sine_add_fusion.table_ref, f32[16,256,256]{2,1,0:T(8,128)} %fusion.1.green_ref, f32[2,4352,128]{2,1,0:T(8,128)} %bitcast.31), custom_call_target="tpu_custom_call" | custom-call | tf_op jit(solution)/shard_map/filter/pallas_call | solution.py:376
  143.3 1.4 copy-done.2
  144.7 68.3 %sample.1 = f32[4,4,4,4096]{3,2,1,0:T(4,128)S(1)} custom-call(s32[128]{0:T(128)S(1)} %convert_element_type.66.base_ref, s32[128]{0:T(128)S(1)} %and_select_fusion.pass_ref, f32[7,16,128]{2,1,0:T(8,128)S(1)} %broadcast_in_dim.9.tab_ref, f32[4,4,8,4096]{3,2,1,0:T(8,128)S(1)} %bitcast.28, bf16[272,16,256]{2,1,0:T(8,128)(2,1)} %bitcast.30, ...), custom_call_target="tpu_custom_call" | custom-call | tf_op jit(solution)/shard_map/sample/pallas_call | solution.py:391
  213.0 28.1 %all_to_all.5 = f32[16,4,4096]{2,1,0:T(4,128)S(1)} all-to-all(f32[16,4,4096]{2,1,0:T(4,128)S(1)} %bitcast.29), channel_id=1, replica_groups=mesh['parts'=2,'gx'=4,'gy'=4] {'gx','gy'}, dimensions={0} | all-to-all | bytes 2097152 | tf_op jit(solution)/shard_map/all_to_all | solution.py:404
  241.1 0.2 reduce_sum.9
  241.4 5.6 %sort.85 = (s32[4096]{0:T(1024)}, f32[4096]{0:T(1024)S(1)}, f32[4096]{0:T(1024)S(1)}, f32[4096]{0:T(1024)S(1)}, f32[4096]{0:T(1024)S(1)}) sort(s32[4096]{0:T(1024)S(1)} %get-tuple-element.16, f32[4096]{0:T(1024)S(1)} %bitcast.41, f32[4096]{0:T(1024)S(1)} %bitcast.40, f32[4096]{0:T(1024)S(1)} %bitcast.39, f32[4096]{0:T(1024)S(1)} %bitcast.38), dimensions={0}, to_apply=%region_4.5 | sort | flops 49152 | bytes 163840 | tf_op jit(solution)/shard_map/sort | solution.py:408
  247.0 0.6 fusion.16
  247.6 0.7 maximum_multiply_fusion
  (23 shorter events, 0.4 us)
Async XLA Ops:
  7.2 52.3 %all-gather.3.cloned.1.call-start = ((), (), s32[]{:S(2)}) async-start(), calls=%async_computation.1 | async-start | bytes 2228224 | tf_op jit(solution)/shard_map/all_gather | solution.py:335
  60.7 1.6 copy-start
  116.4 28.3 %copy-start.1 = (f32[128,4096]{1,0:T(8,128)S(1)}, f32[128,4096]{1,0:T(8,128)}, u32[]{:S(2)}) copy-start(f32[128,4096]{1,0:T(8,128)} %all-gather.3.cloned.1.call-done) | copy-start | bytes 6291460
  143.3 1.4 copy-start.2
  144.7 102.2 %copy-start.3 = (f32[4096]{0:T(1024)S(1)}, f32[4096]{0:T(1024)}, u32[]{:S(2)}) copy-start(f32[4096]{0:T(1024)} %param.9) | copy-start | bytes 49156
Sparse Core Ops, SparseCore 0:
  15.4 44.0 all-gather.2

commit v2 on v0

v2 whole, which is shorter than its diff:
```python
import functools

import jax
import jax.numpy as jnp
import numpy as np
from jax import lax
from jax.experimental import pallas as pl
from jax.experimental.pallas import tpu as pltpu
from jax.sharding import PartitionSpec as P

N = 256
LANES = 128
ROWS = 16
PLANES = 7
PAD = 16
LINES = 80
F32 = jnp.float32
BF16 = jnp.bfloat16
NT = (((1,), (1,)), ((), ()))

SIN_PI = (3.141592640130707, -5.167710083507877, 2.550077523214437, -0.5982912856197345, 0.07765766030450941)
COS_PI = (
    0.9999999997799038,
    -4.934802137078749,
    4.058709159554242,
    -1.335212003029471,
    0.23493731372678894,
    -0.024396324214549327,
)


def poly(coefficients, x):
    result = coefficients[-1]
    for value in coefficients[-2::-1]:
        result = result * x + F32(value)
    return result


def spline(param):
    rest = 1.0 - param
    square = param * param
    cube = square * param
    return [
        rest * rest * rest * F32(1 / 6),
        (3.0 * cube - 6.0 * square + 4.0) * F32(1 / 6),
        (-3.0 * cube + 3.0 * square + 3.0 * param + 1.0) * F32(1 / 6),
        cube * F32(1 / 6),
    ]


def slopes(param):
    rest = 1.0 - param
    square = param * param
    return [
        rest * rest * F32(-0.5),
        1.5 * square - 2.0 * param,
        -1.5 * square + param + 0.5,
        square * F32(0.5),
    ]


def split(value):
    high = value.astype(BF16)
    return high, (value - high.astype(F32)).astype(BF16)


def wide(row, rows):
    return jnp.broadcast_to(row, (rows, row.shape[1]))


def at(values, i):
    return [v[i : i + 1] for v in values]


def pick(offset, options):
    result = jnp.zeros(offset.shape, F32)
    for i in (3, 2, 1, 0):
        result = jnp.where(offset == F32(i), wide(options[i], offset.shape[0]), result)
    return result


def iota(rows):
    return lax.broadcasted_iota(jnp.int32, (rows, LANES), 0).astype(F32)


def along_x(start, row_x, options):
    return pick(iota(8) + (start.astype(F32) - wide(row_x, 8)), options)


def rotation(tab, row_z):
    turn = tab[0] * wide(row_z + 0.5, ROWS)
    turn = turn - jnp.round(turn)
    square = turn * turn
    sine = turn * poly(SIN_PI, square)
    cosine = poly(COS_PI, square)
    twice = sine + sine
    full_cos = 1.0 - twice * sine
    full_sin = twice * cosine
    return full_cos + full_sin, full_cos - full_sin


def along_z(tab, plus, minus, options):
    w = at(options, 5)
    even = tab[1] * wide(w[0] + w[3], ROWS) + tab[2] * wide(w[1] + w[2], ROWS)
    odd = tab[3] * wide(w[3] - w[0], ROWS) + tab[4] * wide(w[2] - w[1], ROWS)
    return even * plus + odd * minus


def along_y(row_y, options_list):
    tile = wide(jnp.floor(row_y * F32(1 / 16)), 16)
    offset = iota(16) - (wide(row_y, 16) - 16.0 * tile)
    before = offset < 0.0
    offset = jnp.where(before, offset + 16.0, offset)
    tile = jnp.where(before, tile + 1.0, tile).astype(BF16)
    pieces = []
    for options in options_list:
        pieces += split(pick(offset, options))
    zero = jnp.zeros((16, LANES), BF16)
    results = [[] for _ in pieces]
    for t in range(LINES // 16):
        here = tile == BF16(t)
        for result, piece in zip(results, pieces):
            result.append(jnp.where(here, piece, zero))
    return [jnp.concatenate(r, axis=0) for r in results]


def lanes(parts):
    return parts[0] if len(parts) == 1 else jnp.concatenate(parts, axis=1)


def place_of(u):
    return pl.ds(pl.multiple_of(u * LANES, LANES), LANES)


def loader(refs, step, n_x):
    def load(place):
        rows = refs[0][0, :, place]
        for g in range(1, len(refs)):
            rows = jnp.where(step >= g * n_x, refs[g][0, :, place], rows)
        return rows

    return load


def rounds(unroll, chunks, begin, base_ref, pass_ref, one_pass):
    def some(i, most):
        for u in range(unroll):
            index = begin + i * unroll + u
            most = jnp.maximum(most, pass_ref[index])
            one_pass(place_of(i * unroll + u), base_ref[index], False)
        return most

    most = lax.fori_loop(0, chunks // unroll, some, jnp.int32(1))

    @pl.when(most > 1)
    def _():
        def one(u, carry):
            def more(p, carry):
                one_pass(place_of(u), base_ref[begin + u] + p * PLANES, True)
                return carry

            return lax.fori_loop(1, pass_ref[begin + u], more, carry)

        lax.fori_loop(0, chunks, one, 0)


def spread(unroll, chunks, step, base_ref, pass_ref, tab_ref, load, out_ref):
    tab = [tab_ref[m] for m in range(5)]
    empty = jnp.zeros((LANES - LINES, 2 * LANES), BF16)

    def one_pass(place, start, again):
        rows = load(place)
        w = spline(rows)
        plus, minus = rotation(tab, rows[2:3])
        z = along_z(tab, plus, minus, w) * wide(rows[6:7], ROWS)
        high, low = along_y(rows[1:2], [at(w, 4)])
        lines = jnp.concatenate(
            [lanes([high, high]), empty, lanes([low, jnp.zeros_like(low)]), empty], axis=0
        )
        x = along_x(start, rows[0:1], at(w, 3))
        pieces = [split(wide(x[m : m + 1], ROWS) * z) for m in range(PLANES)]
        left = lanes([jnp.concatenate([p[k] for p in pieces], axis=0) for k in range(2)])
        both = lax.dot_general(left, lines, NT, preferred_element_type=F32)
        total = both[:, :LANES] + both[:, LANES:]
        out_ref[pl.ds(start, PLANES)] += total.reshape(PLANES, ROWS, LANES)

    rounds(unroll, chunks, step * chunks, base_ref, pass_ref, one_pass)


def add_rows(terms):
    a, c, b, d = terms
    place = lax.broadcasted_iota(jnp.int32, (8, LANES), 0)
    low, even = place < 4, place & 2 == 0
    p = jnp.where(low, a, b) + pltpu.roll(jnp.where(low, b, a), 4, 0)
    q = jnp.where(low, c, d) + pltpu.roll(jnp.where(low, d, c), 4, 0)
    r = jnp.where(even, p, q) + jnp.where(even, pltpu.roll(p, 6, 0), pltpu.roll(q, 2, 0))
    r = r + pltpu.roll(r, 7, 0)
    return jnp.concatenate([r[i : i + 1] for i in (0, 2, 4, 6)], axis=0)


def sample(unroll, chunks, step, base_ref, pass_ref, tab_ref, load, field_ref, out_ref):
    tab = [tab_ref[m] for m in range(5)]

    def one_pass(place, start, again):
        rows = load(place)
        w, s = spline(rows), slopes(rows)
        plus, minus = rotation(tab, rows[2:3])
        charge = wide(rows[6:7], ROWS)
        z = along_z(tab, plus, minus, w) * charge
        z_slope = along_z(tab, plus, minus, s) * charge
        high, low, s_high, s_low = along_y(rows[1:2], [at(w, 4), at(s, 4)])
        lines = lanes([stack_lines(high, low), stack_lines(s_high, s_low)])
        field = field_ref[pl.ds(start, PLANES)].reshape(PLANES * ROWS, N)
        sampled = jnp.dot(field, lines, preferred_element_type=F32)
        x = along_x(start, rows[0:1], at(w, 3))
        x_slope = along_x(start, rows[0:1], at(s, 3))
        both, by_x, by_y = [jnp.zeros((ROWS, LANES), F32) for _ in range(3)]
        for m in range(PLANES):
            v = sampled[m * ROWS : (m + 1) * ROWS, :LANES]
            g = sampled[m * ROWS : (m + 1) * ROWS, LANES:]
            wx = wide(x[m : m + 1], ROWS)
            both += v * wx
            by_x += v * wide(x_slope[m : m + 1], ROWS)
            by_y += g * wx
        terms = [both * z, by_x * z, by_y * z, both * z_slope]
        total = add_rows([t[:8] + t[8:] for t in terms])
        if again:
            total += out_ref[:, place]
        out_ref[:, place] = total

    rounds(unroll, chunks, step * chunks, base_ref, pass_ref, one_pass)


MORE = LANES - LINES


def stack_lines(high, low):
    zero = jnp.zeros((2 * LANES - 3 * LINES, LANES), BF16)
    return jnp.concatenate([high, low[MORE:], zero, high, low[:MORE]], axis=0)


def pack(field, out_ref):
    field[0:ROWS, :] = field[N * ROWS : (N + 1) * ROWS, :]
    field[(N + 1) * ROWS : (N + PAD) * ROWS, :] = field[ROWS : PAD * ROWS, :]
    size = (N + PAD) * ROWS // 4
    lane = lax.broadcasted_iota(jnp.int32, (size, LANES), 1)

    def part(i, carry):
        where = pl.ds(pl.multiple_of(i * size, size), size)
        value = field[where, :]
        high = value.astype(BF16).astype(F32)
        first = jnp.where(lane < LINES, high, pltpu.roll(high, LANES - MORE + LINES - LANES, 1))
        second = jnp.where(lane < LINES, value - high, pltpu.roll(high, LINES, 1))
        out_ref[where, :LANES] = first.astype(BF16)
        out_ref[where, LANES:] = second.astype(BF16)
        return carry

    lax.fori_loop(0, (N + PAD) * ROWS // size, part, 0)


def wrap(mesh_ref):
    mesh_ref[N] += mesh_ref[0]
    mesh_ref[1:3] += mesh_ref[N + 1 : N + 3]


def near_kernel(unroll, chunks, n_x, base_ref, pass_ref, tab_ref, *refs):
    in_refs, out_ref = refs[:-1], refs[-1]
    step = pl.program_id(0)

    @pl.when(step == 0)
    def _():
        out_ref[...] = jnp.zeros_like(out_ref)

    load = loader(in_refs, step, n_x)
    spread(unroll, chunks, step, base_ref, pass_ref, tab_ref, load, out_ref.at[step // n_x])

    @pl.when(step == pl.num_programs(0) - 1)
    def _():
        for g in range(len(in_refs)):
            wrap(out_ref.at[g])


def far_kernel(longer, unroll, chunks, n_x, turns, base_ref, pass_ref, tab_ref, *refs):
    groups = len(refs) - 10
    in_refs = refs[:groups]
    near_ref, table_ref, lines_ref, back_ref, green_ref = refs[groups : groups + 5]
    field_ref, out_ref, mesh, far_field, arrived = refs[groups + 5 :]
    step = pl.program_id(0)
    spreads = groups * n_x
    packs = spreads + turns
    samples = packs + 2 * groups
    copy = pltpu.make_async_copy(near_ref, mesh.at[pl.ds(0, groups)], arrived)

    @pl.when(step == 0)
    def _():
        copy.start()
        mesh[groups:] = jnp.zeros_like(mesh[groups:])

    @pl.when(step < spreads)
    def _():
        load = loader(in_refs, step, n_x)
        to = mesh.at[groups + step // n_x]
        spread(longer, chunks, step, base_ref, pass_ref, tab_ref, load, to)

    @pl.when(step == spreads)
    def _():
        copy.wait()
        for g in range(groups):
            wrap(mesh.at[groups + g])

    flat = mesh.reshape(2 * groups, (N + PAD) * ROWS, LANES)

    @pl.when((step >= spreads) & (step < packs))
    def _():
        def right(value, matrix_ref):
            high, low = split(value)
            return jnp.dot(lanes([high, low, high]), matrix_ref[...], preferred_element_type=F32)

        def left(value):
            high, low = split(value)
            both = jnp.concatenate([high, high, low], axis=0)
            return jnp.dot(table_ref[...], both, preferred_element_type=F32)

        at_once = green_ref.shape[0]
        begin = ROWS + (step - spreads) * at_once
        owns = [pl.ds(begin + u, N, ROWS) for u in range(at_once)]
        values = [lanes([flat.at[s][own, :] for s in range(2 * groups)]) for own in owns]
        values = [right(v, lines_ref) for v in values]
        values = [left(v) * green_ref[u] for u, v in enumerate(values)]
        values = [left(v) for v in values]
        values = [right(v, back_ref) for v in values]
        for own, value in zip(owns, values):
            for s in range(2 * groups):
                flat.at[s][own, :] = value[:, s * LANES : (s + 1) * LANES]

    far_flat = far_field.reshape(groups, (N + PAD) * ROWS, N)

    @pl.when((step >= packs) & (step < packs + groups))
    def _():
        pack(flat.at[groups + step - packs], far_flat.at[step - packs])

    @pl.when((step >= packs + groups) & (step < samples))
    def _():
        pack(flat.at[step - packs - groups], field_ref.at[0])

    @pl.when(step >= samples)
    def _():
        now = step - samples
        load = loader(in_refs, now, n_x)
        at_field = far_field.at[now // n_x]
        sample(unroll, chunks, now, base_ref, pass_ref, tab_ref, load, at_field, out_ref.at[0, 0])


def last_kernel(unroll, chunks, n_x, base_ref, pass_ref, tab_ref, *refs):
    in_refs, (field_ref, out_ref) = refs[:-2], refs[-2:]
    step = pl.program_id(0)
    load = loader(in_refs, step, n_x)
    sample(unroll, chunks, step, base_ref, pass_ref, tab_ref, load, field_ref.at[0], out_ref.at[0, 0])


def table_part(rows, columns, size):
    product = rows[:, None] * columns[None, :] % size
    angle = product.astype(F32) * (2.0 * jnp.pi / size)
    return jnp.cos(angle) + jnp.sin(angle)


def symbol(index, size):
    sines = 2.0 * jnp.sin(jnp.pi * index.astype(F32) / size)
    return sines * sines


def green_of(freq_a, freq_b, freq_c, grid_size):
    total = (
        symbol(freq_a, grid_size)[:, None, None]
        + symbol(freq_b, grid_size)[None, :, None]
        + symbol(freq_c, grid_size)[None, None, :]
    )
    safe = jnp.where(total > 0, total, F32(1.0))
    return jnp.where(total > 0, jnp.exp(-0.5 * total) / safe, F32(0.0)) / float(
        grid_size * grid_size * grid_size
    )


def halves(value):
    high = lax.reduce_precision(value, exponent_bits=8, mantissa_bits=7)
    return high.astype(BF16), (value - high).astype(BF16)


def exchange(value, axis, distance, flip):
    size = lax.axis_size(axis)
    pairs = [(i, i ^ distance if flip else (i + distance) % size) for i in range(size)]
    return lax.ppermute(value, axis, pairs)


def gather_x(value):
    size = lax.axis_size("gx")
    if size > 8:
        return lax.all_gather(value, "gx")
    me = lax.axis_index("gx")
    parts = jnp.stack([value] + [exchange(value, "gx", s, False) for s in range(1, size)])
    return parts[(me - jnp.arange(size)) % size] if size > 1 else parts


def scatter_x(value):
    size = lax.axis_size("gx")
    if size > 8:
        return jnp.sum(lax.all_to_all(value, "gx", split_axis=0, concat_axis=0, tiled=True), axis=0)
    me = lax.axis_index("gx")
    total = lax.dynamic_index_in_dim(value, me, 0, keepdims=False)
    for s in range(1, size):
        part = lax.dynamic_index_in_dim(value, (me + s) % size, 0, keepdims=False)
        total = total + exchange(part, "gx", s, False)
    return total


def shards(cell_x, cell_y, cell_z, fraction, charge):
    count = charge.shape[0]
    n_x, n_y = lax.axis_size("gx"), lax.axis_size("gy")
    at_x, at_y = lax.axis_index("gx"), lax.axis_index("gy")
    planes_x, planes_y = N // n_x, N // n_y
    own = N // (n_x * n_y)
    chunks = count // LANES
    place = jnp.arange(count, dtype=jnp.int32)

    key, cy, cz, fx, fy, fz, q, order = lax.sort(
        (cell_x, cell_y, cell_z, fraction[0], fraction[1], fraction[2], charge, place),
        num_keys=1,
        is_stable=False,
    )
    plane = (key + at_x * planes_x).astype(F32)
    ends = plane.reshape(chunks, LANES)
    ends = jnp.concatenate([ends[:, 0], ends[:, -1], jnp.zeros((count - 2 * chunks,), F32)])
    packed = jnp.stack([plane, cy.astype(F32), cz.astype(F32), fx, fy, fz, q, ends])

    half = n_y // 2
    groups = [gather_x(packed)]
    for s in range(1, half + 1):
        step = s & -s
        groups.append(exchange(groups[s ^ step], "gy", step, True))
    partners = [at_y ^ s for s in range(n_y)]

    freq = (at_x * n_y + at_y) * own + jnp.arange(ROWS, dtype=jnp.int32)
    angle = freq.astype(F32) * F32(np.pi / N)
    tab = jnp.stack(
        [freq.astype(F32) * F32(1 / N), jnp.cos(3 * angle), jnp.cos(angle), jnp.sin(3 * angle), jnp.sin(angle)]
    )
    tab = jnp.where((jnp.arange(ROWS) < own)[None], tab, F32(0.0))
    tab = jnp.broadcast_to(tab[:, :, None], (5, ROWS, LANES))
    full = jnp.arange(N, dtype=jnp.int32)
    table = table_part(full, full, N)
    green = green_of(freq[:own], full, full, N)
    reach = jnp.arange(LANES, dtype=jnp.int32)
    line = jnp.concatenate([p * planes_y + reach - 1 for p in partners]) % N
    used = jnp.tile(reach < planes_y + 3, n_y)
    lines = jnp.where(used[:, None], table_part(line, full, N), F32(0.0))
    back = jnp.where(used[None, :], table_part(full, line, N), F32(0.0))

    unroll = 8 if chunks % 8 == 0 else 1
    longer = 32 if chunks % 32 == 0 else unroll
    size = N + PAD
    steps = half * n_x
    at_once = 4 if own % 4 == 0 else 1
    turns = own // at_once
    params = pltpu.CompilerParams(vmem_limit_bytes=56 * 1024 * 1024)

    def bounds(some):
        ends = jnp.concatenate([g[:, 7, : 2 * chunks] for g in some]).astype(jnp.int32)
        first, last = ends[:, :chunks].reshape(-1), ends[:, chunks:].reshape(-1)
        return first, (last - first + (3 + PLANES)) // PLANES

    def clamp(step, top):
        return jnp.minimum(jnp.maximum(step, 0), top)

    def charges(begins):
        def spec(g):
            def place(t, *_):
                at = 0
                for begin in begins:
                    at = jnp.where(t >= begin, clamp(t - begin - g * n_x, n_x - 1), at)
                return (at, 0, 0)

            return pl.BlockSpec((1, 8, count), place)

        return [spec(g) for g in range(half)]

    def whole(*shape):
        return pl.BlockSpec(shape, lambda *_: (0,) * len(shape))

    def results(begin):
        def place(t, *_):
            at = clamp(t - begin, steps - 1)
            return (at // n_x, at % n_x, 0, 0)

        return pl.BlockSpec((1, 1, 4, count), place)

    def estimate(passes):
        return pl.CostEstimate(
            flops=passes * steps * count * 600000,
            bytes_accessed=passes * steps * count * 160,
            transcendentals=0,
        )

    tab_spec = whole(5, ROWS, LANES)
    mesh_shape = (half, size, ROWS, LANES)
    sums_shape = jax.ShapeDtypeStruct((half, n_x, 4, count), F32)
    near = groups[:half]
    near_bounds = bounds(near)

    near_mesh = pl.pallas_call(
        functools.partial(near_kernel, longer, chunks, n_x),
        grid_spec=pltpu.PrefetchScalarGridSpec(
            num_scalar_prefetch=2,
            grid=(steps,),
            in_specs=[tab_spec] + charges([0]),
            out_specs=whole(*mesh_shape),
        ),
        out_shape=jax.ShapeDtypeStruct(mesh_shape, F32),
        compiler_params=params,
        cost_estimate=estimate(1),
        name="near_spread",
    )(*near_bounds, tab, *near)

    near_mesh, arrived = lax.optimization_barrier((near_mesh, groups[half]))
    far = [arrived]
    for s in range(1, half):
        step = s & -s
        far.append(exchange(far[s ^ step], "gy", step, True))
    far_bounds = bounds(far)

    packs = steps + turns
    samples = packs + 2 * half
    t_high, t_low = halves(table)
    l_high, l_low = halves(lines)
    b_high, b_low = halves(back)
    near_field, far_sums = pl.pallas_call(
        functools.partial(far_kernel, longer, unroll, chunks, n_x, turns),
        grid_spec=pltpu.PrefetchScalarGridSpec(
            num_scalar_prefetch=2,
            grid=(samples + steps,),
            in_specs=[tab_spec]
            + charges([0, samples])
            + [
                pl.BlockSpec(memory_space=pl.ANY),
                whole(N, 3 * N),
                whole(3 * n_y * LANES, N),
                whole(3 * N, n_y * LANES),
                pl.BlockSpec((at_once, N, N), lambda t, *_: (clamp(t - steps, turns - 1), 0, 0)),
            ],
            out_specs=[
                pl.BlockSpec(
                    (1, size * ROWS, N), lambda t, *_: (clamp(t - packs - half, half - 1), 0, 0)
                ),
                results(samples),
            ],
            scratch_shapes=[
                pltpu.VMEM((n_y, size, ROWS, LANES), F32),
                pltpu.VMEM((half, size, ROWS, N), BF16),
                pltpu.SemaphoreType.DMA,
            ],
        ),
        out_shape=[jax.ShapeDtypeStruct((half, size * ROWS, N), BF16), sums_shape],
        compiler_params=params,
        cost_estimate=estimate(3),
        name="far_spread_filter_sample",
    )(
        *far_bounds,
        tab,
        *far,
        near_mesh,
        jnp.concatenate([t_high, t_low, t_high], axis=1),
        jnp.concatenate([l_high, l_high, l_low], axis=0),
        jnp.concatenate([b_high, b_high, b_low], axis=0),
        green,
    )

    def fold(sums):
        for s in range(len(sums) - 1, 0, -1):
            step = s & -s
            sums[s ^ step] = sums[s ^ step] + exchange(sums[s], "gy", step, True)
        return sums[0]

    far_total = fold([far_sums[s] for s in range(half)])
    far_total, near_field = lax.optimization_barrier((far_total, near_field))
    far_total = exchange(far_total, "gy", half, True)
    near_sums = pl.pallas_call(
        functools.partial(last_kernel, unroll, chunks, n_x),
        grid_spec=pltpu.PrefetchScalarGridSpec(
            num_scalar_prefetch=2,
            grid=(steps,),
            in_specs=[tab_spec]
            + charges([0])
            + [pl.BlockSpec((1, size, ROWS, N), lambda t, *_: (t // n_x, 0, 0, 0))],
            out_specs=results(0),
        ),
        out_shape=sums_shape,
        compiler_params=params,
        cost_estimate=estimate(1),
        name="near_sample",
    )(*near_bounds, tab, *near, near_field.reshape(half, size, ROWS, N))

    near_total = fold([near_sums[s] for s in range(half)])
    total = scatter_x(near_total + far_total)
    _, value, grad_x, grad_y, grad_z = lax.sort(
        (order, total[0], total[1], total[2], total[3]), num_keys=1, is_stable=False
    )
    return (value, -jnp.stack([grad_x, grad_y, grad_z], axis=0))


def solution(mesh):
    placed = P(("parts", "gx", "gy"))
    return jax.shard_map(
        shards,
        mesh=mesh,
        in_specs=(placed, placed, placed, P(None, ("parts", "gx", "gy")), placed),
        out_specs=(placed, P(None, ("parts", "gx", "gy"))),
        check_vma=False,
    )
```

time: 1170 us -> 151 us (0.13)
  waiting for transfers between devices: 354 us -> 10.7 us
  matrix products: 278 us -> 0 us
  local copies, waits for them, and re-layouts: 247 us -> 5.91 us
  other arithmetic: 153 us -> 27.6 us
  blocking collectives: 98.4 us -> 0 us
  Pallas kernels: 0 us -> 91.2 us
  between operations: 14.6 us -> 0.98 us
    dot_general x8 -> x0, matrix products: 278 us -> none  [the longest x1 139 us: shards(): lax.dot_general(nearby.reshape(-1, grid_size), both_z, (((1,), (1,)), (()...]
    reduce_scatter x2 -> x0, waiting for transfers between devices: 251 us -> none  [apply_y(): lax.psum_scatter(jnp.dot(table_part(wanted, own, grid_size), flat, precis...]
    all_to_all x1 -> x0, blocking collectives: 98.4 us -> none  [shards(): lax.all_to_all(pencil, 'gx', split_axis=1, concat_axis=2, tiled=True)]
    all_to_all x1 -> x0, waiting for transfers between devices: 93.2 us -> none  [shards(): lax.all_to_all(spectrum, 'gx', split_axis=2, concat_axis=1, tiled=True)]
    pallas_call x0 -> x3, Pallas kernels: none -> 91.2 us  [the longest x1 55.4 us: shards(): pl.pallas_call(functools.partial(far_kernel, longer, unroll, chunks, n_x,...]
    dot_general x4 -> x0, local copies, waits for them, and re-layouts: 69.3 us -> none  [the longest x1 61.8 us: shards(): lax.dot_general(plane, along_z, (((0,), (0,)), ((), ())), precision=high)]
    mul x1 -> x0, local copies, waits for them, and re-layouts: 61.5 us -> none  [shards(): plane = (charge[:, None] * along_y)[:, :, None] * along_x[:, None, :]]
    unnamed x2 -> x0, other arithmetic: 51.9 us -> none
  transfers between devices with their start and end apart: 11 -> 12, of which waited for: 7 -> 4; matrix products, arithmetic and copies ran while one was open for 1% -> 10% of each run, Pallas kernels for 0% -> 24%
where the time goes in v2:
time: 151 us; the launch traced here: 150 us
  Pallas kernels  91.2 us (60%)
  other arithmetic  27.6 us (18%)
  starting transfers between devices  13.7 us (9%)
  waiting for transfers between devices  10.7 us (7%)
  local copies, waits for them, and re-layouts  5.91 us (4%)
    pallas_call x1, Pallas kernels, shards(): pl.pallas_call(functools.partial(far_kernel, longer, unroll, chunks, n_x,...  55.4 us
    pallas_call x1, Pallas kernels, shards(): pl.pallas_call(functools.partial(last_kernel, unroll, chunks, n_x), grid_...  19.3 us
    pallas_call x1, Pallas kernels, shards(): pl.pallas_call(functools.partial(near_kernel, longer, chunks, n_x), grid_...  16.5 us
    ppermute x12, starting transfers between devices, exchange(): return lax.ppermute(value, axis, pairs)  13.7 us
    ppermute x12, waiting for transfers between devices, exchange(): return lax.ppermute(value, axis, pairs)  10.7 us
    convert_element_type x3, other arithmetic, halves(): return (high.astype(BF16), (value - high).astype(BF16))  6.06 us
    sort x1, other arithmetic, shards(): lax.sort((cell_x, cell_y, cell_z, fraction[0], fraction[1], fraction[2],...  5.83 us
    sort x1, other arithmetic, shards(): lax.sort((order, total[0], total[1], total[2], total[3]), num_keys=1, is_...  5.62 us
  transfers between devices with their start and end apart: 12, of which 4 were waited for; matrix products, arithmetic and copies ran while one was open for 10% of the time, Pallas kernels for 24%

profile of v2, /device:TPU:0, one launch (start us, length us, event | category | flops | bytes accessed | tf_op | source)
XLA Modules:
  0.0 150.2 jit_solution(6705615514129235884)
XLA Ops:
  0.6 1.0 fusion.37
  1.7 5.8 %sort.84 = (s32[4096]{0:T(1024)S(1)}, s32[4096]{0:T(1024)S(1)}, s32[4096]{0:T(1024)S(1)}, f32[4096]{0:T(1024)S(1)}, f32[4096]{0:T(1024)S(1)}, /*index=5*/f32[4096]{0:T(1024)S(1)}, f32[4096]{0:T(1024)S(1)}, s32[4096]{0:T(1024)S(1)}) sort(s32[4096]{0:T(1024)} %param.5, s32[4096]{0:T(1024)} %param.6, s32[4096]{0:T(1024)} %param.7, f32[4096]{0:T(1024)S(1)} %bitcast.72, ...), dimensions={0}, to_apply=%region_0.0 | sort | flops 49152 | bytes 262144 | tf_op jit(solution)/shard_map/sort | solution.py:425
  8.0 5.1 %collective-permute-start.2 = (f32[8,4096]{1,0:T(8,128)S(1)}, f32[8,4096]{1,0:T(8,128)S(1)}, u32[]{:S(2)}, u32[]{:S(2)}) collective-permute-start(f32[8,4096]{1,0:T(8,128)S(1)} %stack.70), channel_id=1, source_target_pairs={{0,12},{4,0},{8,4},{12,8},{1,13},{5,1},{9,5},{13,9},{2,14},{6,2},{... | collective-permute-start | bytes 393224 | tf_op jit(solution)/shard_map/ppermute | solution.py:392
  13.1 1.0 collective-permute-start
  14.5 3.0 %fusion.1.refs_6_ = f32[16,256,256]{2,1,0:T(8,128)} fusion(f32[256]{0:T(256)S(1)} %multiply_multiply_fusion, f32[16,256]{1,0:T(8,128)S(1)} %broadcast_add_fusion), kind=kLoop, calls=%fused_computation.5 | loop fusion | flops 7340032 | bytes 4211712 | tf_op jit(solution)/shard_map/div | solution.py:379
  17.6 2.3 %reduce-precision_convert_fusion = (bf16[256,512]{1,0:T(8,128)(2,1)S(1)}, bf16[256,512]{1,0:T(8,128)(2,1)S(1)}) fusion(s32[512]{0:T(512)S(1)} %add_select_fusion.6, pred[512]{0:T(512)(128)(4,1)S(1)} %broadcast_bitcast_fusion), kind=kLoop, calls=%fused_computation.17 | loop fusion | flops 2621440 | bytes 526848 | tf_op jit(solution)/shard_map/convert_element_type | solution.py:386
  19.9 1.0 pad_maximum_fusion.1.refs_5_
  20.9 3.4 %collective-permute-done.1 = f32[8,4096]{1,0:T(8,128)S(1)} collective-permute-done((f32[8,4096]{1,0:T(8,128)S(1)}, f32[8,4096]{1,0:T(8,128)S(1)}, u32[]{:S(2)}, u32[]{:S(2)}) %collective-permute-start.1) | collective-permute-done | bytes 131104 | tf_op jit(solution)/shard_map/ppermute | solution.py:392
  25.0 1.1 reduce-precision_convert_fusion.2
  26.2 2.6 %reduce-precision_convert_fusion.1 = (bf16[512,256]{1,0:T(8,128)(2,1)S(1)}, bf16[512,256]{1,0:T(8,128)(2,1)S(1)}) fusion(s32[512]{0:T(512)S(1)} %add_select_fusion.6, pred[512]{0:T(512)(128)(4,1)S(1)} %broadcast_bitcast_fusion), kind=kLoop, calls=%fused_computation.19 | loop fusion | flops 2621440 | bytes 526848 | tf_op jit(solution)/shard_map/convert_element_type | solution.py:386
  29.2 1.6 %collective-permute-start.4 = (f32[4,8,4096]{2,0,1:T(4,128)S(1)}, f32[4,8,4096]{2,0,1:T(4,128)S(1)}, u32[]{:S(2)}, u32[]{:S(2)}) collective-permute-start(f32[4,8,4096]{2,0,1:T(4,128)S(1)} %copy.16), channel_id=1, source_target_pairs={{0,2},{1,3},{2,0},{3,1},{4,6},{5,7},{6,4},{7,5},{8,10},{9,11},{10,... | collective-permute-start | bytes 1572872 | tf_op jit(solution)/shard_map/ppermute | solution.py:392
  32.2 16.5 %near_spread.1.refs_2_ = f32[2,272,16,128]{3,2,1,0:T(8,128)} custom-call(s32[256]{0:T(256)} %copy-done.2, s32[256]{0:T(256)} %and_select_fusion.1.pass_ref, f32[5,16,128]{2,1,0:T(8,128)} %broadcast_in_dim.68.tab_ref, f32[4,8,4096]{2,1,0:T(8,128)} %copy-done, f32[4,8,4096]{2,1,0:T(8,128)} %copy-done.4), custom_call_target="tpu_custom_call" | custom-call | flops 19660800000 | bytes 5242880 | tf_op jit(solution)/shard_map/near_spread/pallas_call | solution.py:509
  52.0 55.4 %far_spread_filter_sample.1 = (bf16[2,4352,256]{2,1,0:T(8,128)(2,1)}, f32[2,4,4,4096]{3,2,1,0:T(4,128)}) custom-call(s32[256]{0:T(256)} %copy-done.3, s32[256]{0:T(256)} %and_select_fusion.pass_ref, f32[5,16,128]{2,1,0:T(8,128)} %broadcast_in_dim.68.tab_ref, f32[4,8,4096]{2,1,0:T(8,128)} %copy-done.1, f32[4,8,4096]{2,1,0:T(8,128)} %copy-done.5, ...), custom_call_target="tpu_custom_call" | custom-call | flops 58982400000 | bytes 15728640 | tf_op jit(solution)/shard_map/far_spread_filter_sample/pallas_call | solution.py:535
  107.4 1.0 slice_bitcast_fusion.2
  108.7 1.2 collective-permute-done.6
  109.9 1.0 bitcast_add_fusion
  111.5 19.3 %near_sample.1 = f32[2,4,4,4096]{3,2,1,0:T(4,128)} custom-call(s32[256]{0:T(256)} %copy-done.2, s32[256]{0:T(256)} %and_select_fusion.1.pass_ref, f32[5,16,128]{2,1,0:T(8,128)} %broadcast_in_dim.68.tab_ref, f32[4,8,4096]{2,1,0:T(8,128)} %copy-done, f32[4,8,4096]{2,1,0:T(8,128)} %copy-done.4, bf16[2,272,16,256]{3,2,1,0:T(8,128)(2,1)} %bitcast.83), custom_call_target="tpu_custom_call" | custom-call | flops 19660800000 | bytes 5242880 | tf_op jit(solution)/shard_map/near_sample/pallas_call | solution.py:585
  132.0 1.5 collective-permute-done.7
  133.4 1.0 fusion.23
  134.5 1.7 %collective-permute-start.11 = (f32[4,4096]{1,0:T(4,128)S(1)}, f32[4,4096]{1,0:T(4,128)S(1)}, u32[]{:S(2)}, u32[]{:S(2)}) collective-permute-start(f32[4,4096]{1,0:T(4,128)S(1)} %get-tuple-element.41), channel_id=1, source_target_pairs={{0,12},{4,0},{8,4},{12,8},{1,13},{5,1},{9,5},{13,9},{2,14},{6,2},{... | collective-permute-start | bytes 196616 | tf_op jit(solution)/shard_map/ppermute | solution.py:392
  136.2 1.1 collective-permute-start.10
  137.3 1.9 %collective-permute-start.9 = (f32[4,4096]{1,0:T(4,128)S(1)}, f32[4,4096]{1,0:T(4,128)S(1)}, u32[]{:S(2)}, u32[]{:S(2)}) collective-permute-start(f32[4,4096]{1,0:T(4,128)S(1)} %get-tuple-element.40), channel_id=1, source_target_pairs={{0,4},{4,8},{8,12},{12,0},{1,5},{5,9},{9,13},{13,1},{2,6},{6,10},{... | collective-permute-start | bytes 196616 | tf_op jit(solution)/shard_map/ppermute | solution.py:392
  139.2 4.6 %collective-permute-done.10 = f32[4,4096]{1,0:T(4,128)S(1)} collective-permute-done((f32[4,4096]{1,0:T(4,128)S(1)}, f32[4,4096]{1,0:T(4,128)S(1)}, u32[]{:S(2)}, u32[]{:S(2)}) %collective-permute-start.10) | collective-permute-done | bytes 65568 | tf_op jit(solution)/shard_map/ppermute | solution.py:392
  143.9 5.6 %sort.85 = (s32[4096]{0:T(1024)}, f32[4096]{0:T(1024)}, f32[4096]{0:T(1024)S(1)}, f32[4096]{0:T(1024)S(1)}, f32[4096]{0:T(1024)S(1)}) sort(s32[4096]{0:T(1024)S(1)} %get-tuple-element.20, f32[4096]{0:T(1024)S(1)} %bitcast.70, f32[4096]{0:T(1024)S(1)} %bitcast.69, f32[4096]{0:T(1024)S(1)} %bitcast.68, f32[4096]{0:T(1024)S(1)} %bitcast.67), dimensions={0}, to_apply=%region_1.2 | sort | flops 49152 | bytes 163840 | tf_op jit(solution)/shard_map/sort | solution.py:603
  (77 shorter events, 9.4 us)
Async XLA Ops:
  8.0 12.9 %collective-permute-start.2 = (f32[8,4096]{1,0:T(8,128)S(1)}, f32[8,4096]{1,0:T(8,128)S(1)}, u32[]{:S(2)}, u32[]{:S(2)}) collective-permute-start(f32[8,4096]{1,0:T(8,128)S(1)} %stack.70), channel_id=1, source_target_pairs={{0,12},{4,0},{8,4},{12,8},{1,13},{5,1},{9,5},{13,9},{2,14},{6,2},{... | collective-permute-start | bytes 393224 | tf_op jit(solution)/shard_map/ppermute | solution.py:392
  13.1 11.2 %collective-permute-start.1 = (f32[8,4096]{1,0:T(8,128)S(1)}, f32[8,4096]{1,0:T(8,128)S(1)}, u32[]{:S(2)}, u32[]{:S(2)}) collective-permute-start(f32[8,4096]{1,0:T(8,128)S(1)} %stack.70), channel_id=1, source_target_pairs={{0,8},{4,12},{8,0},{12,4},{1,9},{5,13},{9,1},{13,5},{2,10},{6,14},... | collective-permute-start | bytes 393224 | tf_op jit(solution)/shard_map/ppermute | solution.py:392
  13.1 11.2 %collective-permute-start = (f32[8,4096]{1,0:T(8,128)S(1)}, f32[8,4096]{1,0:T(8,128)S(1)}, u32[]{:S(2)}, u32[]{:S(2)}) collective-permute-start(f32[8,4096]{1,0:T(8,128)S(1)} %stack.70), channel_id=1, source_target_pairs={{0,4},{4,8},{8,12},{12,0},{1,5},{5,9},{9,13},{13,1},{2,6},{6,10},{... | collective-permute-start | bytes 393224 | tf_op jit(solution)/shard_map/ppermute | solution.py:392
  25.0 7.3 %copy-start = (f32[4,8,4096]{2,1,0:T(8,128)}, f32[4,8,4096]{2,1,0:T(8,128)S(1)}, u32[]{:S(2)}) copy-start(f32[4,8,4096]{2,1,0:T(8,128)S(1)} %gather_fusion) | copy-start | bytes 1572868
  25.0 5.8 %collective-permute-start.3 = (f32[4,8,4096]{2,1,0:T(8,128)S(1)}, f32[4,8,4096]{2,1,0:T(8,128)S(1)}, u32[]{:S(2)}, u32[]{:S(2)}) collective-permute-start(f32[4,8,4096]{2,1,0:T(8,128)S(1)} %gather_fusion), channel_id=1, source_target_pairs={{0,1},{1,0},{2,3},{3,2},{4,5},{5,4},{6,7},{7,6},{8,9},{9,8},{10,11... | collective-permute-start | bytes 1572872 | tf_op jit(solution)/shard_map/ppermute | solution.py:392
  29.2 19.6 %collective-permute-start.4 = (f32[4,8,4096]{2,0,1:T(4,128)S(1)}, f32[4,8,4096]{2,0,1:T(4,128)S(1)}, u32[]{:S(2)}, u32[]{:S(2)}) collective-permute-start(f32[4,8,4096]{2,0,1:T(4,128)S(1)} %copy.16), channel_id=1, source_target_pairs={{0,2},{1,3},{2,0},{3,1},{4,6},{5,7},{6,4},{7,5},{8,10},{9,11},{10,... | collective-permute-start | bytes 1572872 | tf_op jit(solution)/shard_map/ppermute | solution.py:392
  30.7 1.5 %copy-start.4 = (f32[4,8,4096]{2,1,0:T(8,128)}, f32[4,8,4096]{2,1,0:T(8,128)S(1)}, u32[]{:S(2)}) copy-start(f32[4,8,4096]{2,1,0:T(8,128)S(1)} %collective-permute-done.3.refs_1_) | copy-start | bytes 1572868
  30.9 1.3 copy-start.2
  49.1 2.9 %copy-start.1 = (f32[4,8,4096]{2,1,0:T(8,128)}, f32[4,8,4096]{2,1,0:T(8,128)S(1)}, u32[]{:S(2)}) copy-start(f32[4,8,4096]{2,1,0:T(8,128)S(1)} %copy.18.refs_0_) | copy-start | bytes 1572868
  49.1 2.0 %collective-permute-start.5 = (f32[4,8,4096]{2,1,0:T(8,128)S(1)}, f32[4,8,4096]{2,1,0:T(8,128)S(1)}, u32[]{:S(2)}, u32[]{:S(2)}) collective-permute-start(f32[4,8,4096]{2,1,0:T(8,128)S(1)} %copy.18.refs_0_), channel_id=1, source_target_pairs={{0,1},{1,0},{2,3},{3,2},{4,5},{5,4},{6,7},{7,6},{8,9},{9,8},{10,11... | collective-permute-start | bytes 1572872 | tf_op jit(solution)/shard_map/ppermute | solution.py:392
  51.1 0.9 copy-start.5
  51.3 0.7 copy-start.3
  108.3 1.6 %collective-permute-start.6 = (f32[4,4,4096]{2,1,0:T(4,128)S(1)}, f32[4,4,4096]{2,1,0:T(4,128)S(1)}, u32[]{:S(2)}, u32[]{:S(2)}) collective-permute-start(f32[4,4,4096]{2,1,0:T(4,128)S(1)} %slice_bitcast_fusion.2), channel_id=1, source_target_pairs={{0,1},{1,0},{2,3},{3,2},{4,5},{5,4},{6,7},{7,6},{8,9},{9,8},{10,11... | collective-permute-start | bytes 786440 | tf_op jit(solution)/shard_map/ppermute | solution.py:392
  111.0 21.0 %collective-permute-start.8 = (f32[4,4,4096]{2,1,0:T(4,128)S(1)}, f32[4,4,4096]{2,1,0:T(4,128)S(1)}, u32[]{:S(2)}, u32[]{:S(2)}) collective-permute-start(f32[4,4,4096]{2,1,0:T(4,128)S(1)} %bitcast_add_fusion), channel_id=1, source_target_pairs={{0,2},{1,3},{2,0},{3,1},{4,6},{5,7},{6,4},{7,5},{8,10},{9,11},{10,... | collective-permute-start | bytes 786440 | tf_op jit(solution)/shard_map/ppermute | solution.py:392
  131.8 1.6 %collective-permute-start.7 = (f32[4,4,4096]{2,1,0:T(4,128)S(1)}, f32[4,4,4096]{2,1,0:T(4,128)S(1)}, u32[]{:S(2)}, u32[]{:S(2)}) collective-permute-start(f32[4,4,4096]{2,1,0:T(4,128)S(1)} %slice_bitcast_fusion), channel_id=1, source_target_pairs={{0,1},{1,0},{2,3},{3,2},{4,5},{5,4},{6,7},{7,6},{8,9},{9,8},{10,11... | collective-permute-start | bytes 786440 | tf_op jit(solution)/shard_map/ppermute | solution.py:392
  134.5 4.7 %collective-permute-start.11 = (f32[4,4096]{1,0:T(4,128)S(1)}, f32[4,4096]{1,0:T(4,128)S(1)}, u32[]{:S(2)}, u32[]{:S(2)}) collective-permute-start(f32[4,4096]{1,0:T(4,128)S(1)} %get-tuple-element.41), channel_id=1, source_target_pairs={{0,12},{4,0},{8,4},{12,8},{1,13},{5,1},{9,5},{13,9},{2,14},{6,2},{... | collective-permute-start | bytes 196616 | tf_op jit(solution)/shard_map/ppermute | solution.py:392
  136.2 7.6 %collective-permute-start.10 = (f32[4,4096]{1,0:T(4,128)S(1)}, f32[4,4096]{1,0:T(4,128)S(1)}, u32[]{:S(2)}, u32[]{:S(2)}) collective-permute-start(f32[4,4096]{1,0:T(4,128)S(1)} %get-tuple-element.42), channel_id=1, source_target_pairs={{0,8},{4,12},{8,0},{12,4},{1,9},{5,13},{9,1},{13,5},{2,10},{6,14},... | collective-permute-start | bytes 196616 | tf_op jit(solution)/shard_map/ppermute | solution.py:392
  137.3 6.5 %collective-permute-start.9 = (f32[4,4096]{1,0:T(4,128)S(1)}, f32[4,4096]{1,0:T(4,128)S(1)}, u32[]{:S(2)}, u32[]{:S(2)}) collective-permute-start(f32[4,4096]{1,0:T(4,128)S(1)} %get-tuple-element.40), channel_id=1, source_target_pairs={{0,4},{4,8},{8,12},{12,0},{1,5},{5,9},{9,13},{13,1},{2,6},{6,10},{... | collective-permute-start | bytes 196616 | tf_op jit(solution)/shard_map/ppermute | solution.py:392

commit v3 on v2

--- a/solution.py
+++ b/solution.py
@@ -12,6 +12,7 @@
 LANES = 128
 ROWS = 16
 PLANES = 7
+TABLES = 7
 PAD = 16
 LINES = 80
 F32 = jnp.float32
@@ -32,31 +33,28 @@
 def poly(coefficients, x):
     result = coefficients[-1]
     for value in coefficients[-2::-1]:
-        result = result * x + F32(value)
+        result = result * x + value
     return result
 
 
-def spline(param):
-    rest = 1.0 - param
-    square = param * param
-    cube = square * param
-    return [
-        rest * rest * rest * F32(1 / 6),
-        (3.0 * cube - 6.0 * square + 4.0) * F32(1 / 6),
-        (-3.0 * cube + 3.0 * square + 3.0 * param + 1.0) * F32(1 / 6),
-        cube * F32(1 / 6),
-    ]
-
-
-def slopes(param):
-    rest = 1.0 - param
-    square = param * param
-    return [
-        rest * rest * F32(-0.5),
-        1.5 * square - 2.0 * param,
-        -1.5 * square + param + 0.5,
-        square * F32(0.5),
-    ]
+SPLINE = (
+    (1 / 6, 4 / 6, 1 / 6, 0.0),
+    (-1 / 2, 0.0, 1 / 2, 0.0),
+    (1 / 2, -1.0, 1 / 2, 0.0),
+    (-1 / 6, 1 / 2, -1 / 2, 1 / 6),
+)
+SLOPES = ((-1 / 2, 0.0, 1 / 2, 0.0), (1.0, -2.0, 1.0, 0.0), (-1 / 2, 3 / 2, -3 / 2, 1 / 2))
+
+
+def coefficients(table):
+    place = iota(8)
+    results = []
+    for values in table:
+        result = jnp.zeros((8, LANES), F32)
+        for i, value in enumerate(values):
+            result = jnp.where(place == i, F32(value), result)
+        results.append(result)
+    return results
 
 
 def split(value):
@@ -68,23 +66,17 @@
     return jnp.broadcast_to(row, (rows, row.shape[1]))
 
 
-def at(values, i):
-    return [v[i : i + 1] for v in values]
-
-
-def pick(offset, options):
-    result = jnp.zeros(offset.shape, F32)
-    for i in (3, 2, 1, 0):
-        result = jnp.where(offset == F32(i), wide(options[i], offset.shape[0]), result)
-    return result
-
-
 def iota(rows):
-    return lax.broadcasted_iota(jnp.int32, (rows, LANES), 0).astype(F32)
-
-
-def along_x(start, row_x, options):
-    return pick(iota(8) + (start.astype(F32) - wide(row_x, 8)), options)
+    return lax.broadcasted_iota(jnp.int32, (rows, LANES), 0)
+
+
+def pick(options, index):
+    return jnp.take_along_axis(options, index, axis=0)
+
+
+def x_index(start, row_x):
+    offset = iota(8) + (start - wide(row_x, 8).astype(jnp.int32))
+    return jnp.minimum(offset & 0x7FFFFFFF, 7)
 
 
 def rotation(tab, row_z):
@@ -99,22 +91,23 @@
     return full_cos + full_sin, full_cos - full_sin
 
 
-def along_z(tab, plus, minus, options):
-    w = at(options, 5)
-    even = tab[1] * wide(w[0] + w[3], ROWS) + tab[2] * wide(w[1] + w[2], ROWS)
-    odd = tab[3] * wide(w[3] - w[0], ROWS) + tab[4] * wide(w[2] - w[1], ROWS)
-    return even * plus + odd * minus
+def along_z(tab, plus, minus, middle, square):
+    return (tab[1] + tab[2] * square) * plus + middle * (tab[3] + tab[4] * square) * minus
+
+
+def slope_along_z(tab, plus, minus, middle, square):
+    return (tab[5] * middle) * plus + (tab[3] + tab[6] * square) * minus
 
 
 def along_y(row_y, options_list):
-    tile = wide(jnp.floor(row_y * F32(1 / 16)), 16)
-    offset = iota(16) - (wide(row_y, 16) - 16.0 * tile)
-    before = offset < 0.0
-    offset = jnp.where(before, offset + 16.0, offset)
-    tile = jnp.where(before, tile + 1.0, tile).astype(BF16)
+    cell = wide(row_y, 8).astype(jnp.int32)
+    places = [iota(8), iota(8) + 8]
+    index = [jnp.minimum((p - cell) & 15, 7) for p in places]
+    tile = jnp.concatenate([(cell + (15 - p)) >> 4 for p in places], axis=0)
+    tile = tile.astype(F32).astype(BF16)
     pieces = []
     for options in options_list:
-        pieces += split(pick(offset, options))
+        pieces += split(jnp.concatenate([pick(options, i) for i in index], axis=0))
     zero = jnp.zeros((16, LANES), BF16)
     results = [[] for _ in pieces]
     for t in range(LINES // 16):
@@ -164,20 +157,31 @@
         lax.fori_loop(0, chunks, one, 0)
 
 
-def spread(unroll, chunks, step, base_ref, pass_ref, tab_ref, load, out_ref):
-    tab = [tab_ref[m] for m in range(5)]
+def factors(rows, tab):
+    plus, minus = rotation(tab, rows[2:3])
+    middle = wide(rows[5:6] - 0.5, ROWS)
+    square = middle * middle
+    charge = wide(rows[6:7], ROWS)
+    z = along_z(tab, plus, minus, middle, square) * charge
+    return z, slope_along_z(tab, plus, minus, middle, square) * charge
+
+
+def spread(unroll, chunks, step, base_ref, pass_ref, tab_ref, load, out_ref, kept):
+    tab = [tab_ref[m] for m in range(TABLES)]
+    cubic = coefficients(SPLINE)
     empty = jnp.zeros((LANES - LINES, 2 * LANES), BF16)
 
     def one_pass(place, start, again):
         rows = load(place)
-        w = spline(rows)
-        plus, minus = rotation(tab, rows[2:3])
-        z = along_z(tab, plus, minus, w) * wide(rows[6:7], ROWS)
-        high, low = along_y(rows[1:2], [at(w, 4)])
+        z, z_slope = factors(rows, tab)
+        if kept is not None and not again:
+            kept[:ROWS, place] = z
+            kept[ROWS:, place] = z_slope
+        high, low = along_y(rows[1:2], [poly(cubic, wide(rows[4:5], 8))])
         lines = jnp.concatenate(
             [lanes([high, high]), empty, lanes([low, jnp.zeros_like(low)]), empty], axis=0
         )
-        x = along_x(start, rows[0:1], at(w, 3))
+        x = pick(poly(cubic, wide(rows[3:4], 8)), x_index(start, rows[0:1]))
         pieces = [split(wide(x[m : m + 1], ROWS) * z) for m in range(PLANES)]
         left = lanes([jnp.concatenate([p[k] for p in pieces], axis=0) for k in range(2)])
         both = lax.dot_general(left, lines, NT, preferred_element_type=F32)
@@ -198,22 +202,25 @@
     return jnp.concatenate([r[i : i + 1] for i in (0, 2, 4, 6)], axis=0)
 
 
-def sample(unroll, chunks, step, base_ref, pass_ref, tab_ref, load, field_ref, out_ref):
-    tab = [tab_ref[m] for m in range(5)]
+def sample(unroll, chunks, step, base_ref, pass_ref, tab_ref, load, field_ref, out_ref, kept):
+    tab = [tab_ref[m] for m in range(TABLES)]
+    cubic, quadratic = coefficients(SPLINE), coefficients(SLOPES)
 
     def one_pass(place, start, again):
         rows = load(place)
-        w, s = spline(rows), slopes(rows)
-        plus, minus = rotation(tab, rows[2:3])
-        charge = wide(rows[6:7], ROWS)
-        z = along_z(tab, plus, minus, w) * charge
-        z_slope = along_z(tab, plus, minus, s) * charge
-        high, low, s_high, s_low = along_y(rows[1:2], [at(w, 4), at(s, 4)])
+        if kept is None:
+            z, z_slope = factors(rows, tab)
+        else:
+            z, z_slope = kept[:ROWS, place], kept[ROWS:, place]
+        part = wide(rows[4:5], 8)
+        high, low, s_high, s_low = along_y(rows[1:2], [poly(cubic, part), poly(quadratic, part)])
         lines = lanes([stack_lines(high, low), stack_lines(s_high, s_low)])
         field = field_ref[pl.ds(start, PLANES)].reshape(PLANES * ROWS, N)
         sampled = jnp.dot(field, lines, preferred_element_type=F32)
-        x = along_x(start, rows[0:1], at(w, 3))
-        x_slope = along_x(start, rows[0:1], at(s, 3))
+        part = wide(rows[3:4], 8)
+        index = x_index(start, rows[0:1])
+        x = pick(poly(cubic, part), index)
+        x_slope = pick(poly(quadratic, part), index)
         both, by_x, by_y = [jnp.zeros((ROWS, LANES), F32) for _ in range(3)]
         for m in range(PLANES):
             v = sampled[m * ROWS : (m + 1) * ROWS, :LANES]
@@ -263,50 +270,66 @@
     mesh_ref[1:3] += mesh_ref[N + 1 : N + 3]
 
 
+def deliver(step, n_x, sums, out_refs):
+    for g, out_ref in enumerate(out_refs):
+
+        @pl.when(step // n_x == g)
+        def _():
+            out_ref[0] = sums[...]
+
+
 def near_kernel(unroll, chunks, n_x, base_ref, pass_ref, tab_ref, *refs):
-    in_refs, out_ref = refs[:-1], refs[-1]
+    in_refs, out_ref, kept = refs[:-2], refs[-2], refs[-1]
     step = pl.program_id(0)
 
-    @pl.when(step == 0)
+    @pl.when(step % n_x == 0)
     def _():
         out_ref[...] = jnp.zeros_like(out_ref)
 
     load = loader(in_refs, step, n_x)
-    spread(unroll, chunks, step, base_ref, pass_ref, tab_ref, load, out_ref.at[step // n_x])
-
-    @pl.when(step == pl.num_programs(0) - 1)
-    def _():
-        for g in range(len(in_refs)):
-            wrap(out_ref.at[g])
-
-
-def far_kernel(longer, unroll, chunks, n_x, turns, base_ref, pass_ref, tab_ref, *refs):
-    groups = len(refs) - 10
+    spread(unroll, chunks, step, base_ref, pass_ref, tab_ref, load, out_ref.at[0], kept.at[0])
+
+    @pl.when(step % n_x == n_x - 1)
+    def _():
+        wrap(out_ref.at[0])
+
+
+def far_kernel(longer, unroll, chunks, n_x, turns, base_ref, pass_ref, at_ref, tab_ref, *refs):
+    groups = (len(refs) - 11) // 2
     in_refs = refs[:groups]
     near_ref, table_ref, lines_ref, back_ref, green_ref = refs[groups : groups + 5]
-    field_ref, out_ref, mesh, far_field, arrived = refs[groups + 5 :]
+    field_ref, out_refs = refs[groups + 5], refs[groups + 6 : -5]
+    mesh, far_field, sums, kept, arrived = refs[-5:]
+    keep = kept.shape[0] == groups * n_x
     step = pl.program_id(0)
     spreads = groups * n_x
     packs = spreads + turns
     samples = packs + 2 * groups
-    copy = pltpu.make_async_copy(near_ref, mesh.at[pl.ds(0, groups)], arrived)
+    slots = [at_ref[0] ^ s for s in range(2 * groups)]
+    copies = [
+        pltpu.make_async_copy(near_ref.at[g], mesh.at[slots[g]], arrived.at[g]) for g in range(groups)
+    ]
 
     @pl.when(step == 0)
     def _():
-        copy.start()
-        mesh[groups:] = jnp.zeros_like(mesh[groups:])
+        for copy in copies:
+            copy.start()
+        for slot in slots[groups:]:
+            mesh[slot] = jnp.zeros(mesh.shape[1:], F32)
 
     @pl.when(step < spreads)
     def _():
         load = loader(in_refs, step, n_x)
-        to = mesh.at[groups + step // n_x]
-        spread(longer, chunks, step, base_ref, pass_ref, tab_ref, load, to)
+        to = mesh.at[at_ref[0] ^ (groups + step // n_x)]
+        at_kept = kept.at[step] if keep else None
+        spread(longer, chunks, step, base_ref, pass_ref, tab_ref, load, to, at_kept)
 
     @pl.when(step == spreads)
     def _():
-        copy.wait()
-        for g in range(groups):
-            wrap(mesh.at[groups + g])
+        for copy in copies:
+            copy.wait()
+        for slot in slots[groups:]:
+            wrap(mesh.at[slot])
 
     flat = mesh.reshape(2 * groups, (N + PAD) * ROWS, LANES)
 
@@ -337,31 +360,55 @@
 
     @pl.when((step >= packs) & (step < packs + groups))
     def _():
-        pack(flat.at[groups + step - packs], far_flat.at[step - packs])
+        pack(flat.at[at_ref[0] ^ (groups + step - packs)], far_flat.at[step - packs])
 
     @pl.when((step >= packs + groups) & (step < samples))
     def _():
-        pack(flat.at[step - packs - groups], field_ref.at[0])
+        pack(flat.at[at_ref[0] ^ (step - packs - groups)], field_ref.at[0])
 
     @pl.when(step >= samples)
     def _():
         now = step - samples
         load = loader(in_refs, now, n_x)
         at_field = far_field.at[now // n_x]
-        sample(unroll, chunks, now, base_ref, pass_ref, tab_ref, load, at_field, out_ref.at[0, 0])
+        at_kept = kept.at[now] if keep else None
+        sample(unroll, chunks, now, base_ref, pass_ref, tab_ref, load, at_field, sums, at_kept)
+        deliver(now, n_x, sums, out_refs)
 
 
 def last_kernel(unroll, chunks, n_x, base_ref, pass_ref, tab_ref, *refs):
-    in_refs, (field_ref, out_ref) = refs[:-2], refs[-2:]
+    groups = (len(refs) - 3) // 2
+    in_refs, (kept, field_ref) = refs[:groups], refs[groups : groups + 2]
+    out_refs, sums = refs[groups + 2 : -1], refs[-1]
     step = pl.program_id(0)
     load = loader(in_refs, step, n_x)
-    sample(unroll, chunks, step, base_ref, pass_ref, tab_ref, load, field_ref.at[0], out_ref.at[0, 0])
-
-
-def table_part(rows, columns, size):
-    product = rows[:, None] * columns[None, :] % size
-    angle = product.astype(F32) * (2.0 * jnp.pi / size)
-    return jnp.cos(angle) + jnp.sin(angle)
+    sample(
+        unroll, chunks, step, base_ref, pass_ref, tab_ref, load, field_ref.at[0], sums, kept.at[0]
+    )
+    deliver(step, n_x, sums, out_refs)
+
+
+def tables(n_y, planes_y):
+    def halves(value):
+        value = value.astype(np.float32)
+        high = value.astype(BF16)
+        return high, (value - high.astype(np.float32)).astype(BF16)
+
+    full = np.arange(N)
+    reach = np.arange(LANES)
+    line = np.concatenate([b * planes_y + reach - 1 for b in range(n_y)]) % N
+    used = np.tile(reach < planes_y + 3, n_y)
+
+    def table(rows, columns):
+        angle = (rows[:, None] * columns[None, :] % N) * (2.0 * np.pi / N)
+        return np.cos(angle) + np.sin(angle)
+
+    high, low = halves(table(full, full))
+    left = np.concatenate([high, low, high], axis=1)
+    high, low = halves(table(line, full) * used[:, None])
+    lines = np.concatenate([high, high, low], axis=0)
+    high, low = halves(table(full, line) * used[None, :])
+    return left, lines, np.concatenate([high, high, low], axis=0)
 
 
 def symbol(index, size):
@@ -381,11 +428,6 @@
     )
 
 
-def halves(value):
-    high = lax.reduce_precision(value, exponent_bits=8, mantissa_bits=7)
-    return high.astype(BF16), (value - high).astype(BF16)
-
-
 def exchange(value, axis, distance, flip):
     size = lax.axis_size(axis)
     pairs = [(i, i ^ distance if flip else (i + distance) % size) for i in range(size)]
@@ -432,28 +474,31 @@
     ends = jnp.concatenate([ends[:, 0], ends[:, -1], jnp.zeros((count - 2 * chunks,), F32)])
     packed = jnp.stack([plane, cy.astype(F32), cz.astype(F32), fx, fy, fz, q, ends])
 
+    freq = (at_x * n_y + at_y) * own + jnp.arange(ROWS, dtype=jnp.int32)
+    angle = freq.astype(F32) * F32(np.pi / N)
+    far_cos, near_cos = jnp.cos(3 * angle), jnp.cos(angle)
+    far_sin, near_sin = jnp.sin(3 * angle), jnp.sin(angle)
+    tab = [
+        freq.astype(F32) * F32(1 / N),
+        (far_cos + 23 * near_cos) * F32(1 / 24),
+        (far_cos - near_cos) * F32(1 / 2),
+        (far_sin + 5 * near_sin) * F32(1 / 4),
+        far_sin * F32(1 / 3) - near_sin,
+        far_cos - near_cos,
+        far_sin - 3 * near_sin,
+    ]
+    tab = jnp.stack(tab)
+    tab = jnp.where((jnp.arange(ROWS) < own)[None], tab, F32(0.0))
+    tab = jnp.broadcast_to(tab[:, :, None], (TABLES, ROWS, LANES))
+    full = jnp.arange(N, dtype=jnp.int32)
+    green = green_of(freq[:own], full, full, N)
+
     half = n_y // 2
-    groups = [gather_x(packed)]
+    arrived, green, tab = lax.optimization_barrier((gather_x(packed), green, tab))
+    groups = [arrived]
     for s in range(1, half + 1):
         step = s & -s
         groups.append(exchange(groups[s ^ step], "gy", step, True))
-    partners = [at_y ^ s for s in range(n_y)]
-
-    freq = (at_x * n_y + at_y) * own + jnp.arange(ROWS, dtype=jnp.int32)
-    angle = freq.astype(F32) * F32(np.pi / N)
-    tab = jnp.stack(
-        [freq.astype(F32) * F32(1 / N), jnp.cos(3 * angle), jnp.cos(angle), jnp.sin(3 * angle), jnp.sin(angle)]
-    )
-    tab = jnp.where((jnp.arange(ROWS) < own)[None], tab, F32(0.0))
-    tab = jnp.broadcast_to(tab[:, :, None], (5, ROWS, LANES))
-    full = jnp.arange(N, dtype=jnp.int32)
-    table = table_part(full, full, N)
-    green = green_of(freq[:own], full, full, N)
-    reach = jnp.arange(LANES, dtype=jnp.int32)
-    line = jnp.concatenate([p * planes_y + reach - 1 for p in partners]) % N
-    used = jnp.tile(reach < planes_y + 3, n_y)
-    lines = jnp.where(used[:, None], table_part(line, full, N), F32(0.0))
-    back = jnp.where(used[None, :], table_part(full, line, N), F32(0.0))
 
     unroll = 8 if chunks % 8 == 0 else 1
     longer = 32 if chunks % 32 == 0 else unroll
@@ -487,11 +532,12 @@
         return pl.BlockSpec(shape, lambda *_: (0,) * len(shape))
 
     def results(begin):
-        def place(t, *_):
-            at = clamp(t - begin, steps - 1)
-            return (at // n_x, at % n_x, 0, 0)
-
-        return pl.BlockSpec((1, 1, 4, count), place)
+        def spec(g):
+            return pl.BlockSpec(
+                (1, 4, count), lambda t, *_: (clamp(t - begin - g * n_x, n_x - 1), 0, 0)
+            )
+
+        return [spec(g) for g in range(half)]
 
     def estimate(passes):
         return pl.CostEstimate(
@@ -500,21 +546,27 @@
             transcendentals=0,
         )
 
-    tab_spec = whole(5, ROWS, LANES)
+    tab_spec = whole(TABLES, ROWS, LANES)
     mesh_shape = (half, size, ROWS, LANES)
-    sums_shape = jax.ShapeDtypeStruct((half, n_x, 4, count), F32)
+    sums_shape = [jax.ShapeDtypeStruct((n_x, 4, count), F32)] * half
+    sums_scratch = pltpu.VMEM((4, count), F32)
     near = groups[:half]
     near_bounds = bounds(near)
 
-    near_mesh = pl.pallas_call(
+    kept_spec = pl.BlockSpec((1, 2 * ROWS, count), lambda t, *_: (t, 0, 0))
+    kept_shape = jax.ShapeDtypeStruct((steps, 2 * ROWS, count), F32)
+    near_mesh, near_kept = pl.pallas_call(
         functools.partial(near_kernel, longer, chunks, n_x),
         grid_spec=pltpu.PrefetchScalarGridSpec(
             num_scalar_prefetch=2,
             grid=(steps,),
             in_specs=[tab_spec] + charges([0]),
-            out_specs=whole(*mesh_shape),
+            out_specs=[
+                pl.BlockSpec((1, size, ROWS, LANES), lambda t, *_: (t // n_x, 0, 0, 0)),
+                kept_spec,
+            ],
         ),
-        out_shape=jax.ShapeDtypeStruct(mesh_shape, F32),
+        out_shape=[jax.ShapeDtypeStruct(mesh_shape, F32), kept_shape],
         compiler_params=params,
         cost_estimate=estimate(1),
         name="near_spread",
@@ -529,13 +581,10 @@
 
     packs = steps + turns
     samples = packs + 2 * half
-    t_high, t_low = halves(table)
-    l_high, l_low = halves(lines)
-    b_high, b_low = halves(back)
-    near_field, far_sums = pl.pallas_call(
+    near_field, *far_sums = pl.pallas_call(
         functools.partial(far_kernel, longer, unroll, chunks, n_x, turns),
         grid_spec=pltpu.PrefetchScalarGridSpec(
-            num_scalar_prefetch=2,
+            num_scalar_prefetch=3,
             grid=(samples + steps,),
             in_specs=[tab_spec]
             + charges([0, samples])
@@ -550,38 +599,32 @@
                 pl.BlockSpec(
                     (1, size * ROWS, N), lambda t, *_: (clamp(t - packs - half, half - 1), 0, 0)
                 ),
-                results(samples),
-            ],
+            ]
+            + results(samples),
             scratch_shapes=[
                 pltpu.VMEM((n_y, size, ROWS, LANES), F32),
                 pltpu.VMEM((half, size, ROWS, N), BF16),
-                pltpu.SemaphoreType.DMA,
+                sums_scratch,
+                pltpu.VMEM((steps if steps <= 8 else 1, 2 * ROWS, count), F32),
+                pltpu.SemaphoreType.DMA((half,)),
             ],
         ),
-        out_shape=[jax.ShapeDtypeStruct((half, size * ROWS, N), BF16), sums_shape],
+        out_shape=[jax.ShapeDtypeStruct((half, size * ROWS, N), BF16)] + sums_shape,
         compiler_params=params,
         cost_estimate=estimate(3),
         name="far_spread_filter_sample",
     )(
         *far_bounds,
+        at_y[None],
         tab,
         *far,
         near_mesh,
-        jnp.concatenate([t_high, t_low, t_high], axis=1),
-        jnp.concatenate([l_high, l_high, l_low], axis=0),
-        jnp.concatenate([b_high, b_high, b_low], axis=0),
+        *tables(n_y, planes_y),
         green,
     )
 
-    def fold(sums):
-        for s in range(len(sums) - 1, 0, -1):
-            step = s & -s
-            sums[s ^ step] = sums[s ^ step] + exchange(sums[s], "gy", step, True)
-        return sums[0]
-
-    far_total = fold([far_sums[s] for s in range(half)])
-    far_total, near_field = lax.optimization_barrier((far_total, near_field))
-    far_total = exchange(far_total, "gy", half, True)
+    *far_sums, near_field = lax.optimization_barrier((*far_sums, near_field))
+    far_sums = [exchange(v, "gy", half, True) for v in far_sums]
     near_sums = pl.pallas_call(
         functools.partial(last_kernel, unroll, chunks, n_x),
         grid_spec=pltpu.PrefetchScalarGridSpec(
@@ -589,17 +632,21 @@
             grid=(steps,),
             in_specs=[tab_spec]
             + charges([0])
-            + [pl.BlockSpec((1, size, ROWS, N), lambda t, *_: (t // n_x, 0, 0, 0))],
+            + [kept_spec, pl.BlockSpec((1, size, ROWS, N), lambda t, *_: (t // n_x, 0, 0, 0))],
             out_specs=results(0),
+            scratch_shapes=[sums_scratch],
         ),
         out_shape=sums_shape,
         compiler_params=params,
         cost_estimate=estimate(1),
         name="near_sample",
-    )(*near_bounds, tab, *near, near_field.reshape(half, size, ROWS, N))
-
-    near_total = fold([near_sums[s] for s in range(half)])
-    total = scatter_x(near_total + far_total)
+    )(*near_bounds, tab, *near, near_kept, near_field.reshape(half, size, ROWS, N))
+
+    sums = [near_sums[s] + far_sums[s] for s in range(half)]
+    for s in range(half - 1, 0, -1):
+        step = s & -s
+        sums[s ^ step] = sums[s ^ step] + exchange(sums[s], "gy", step, True)
+    total = scatter_x(sums[0])
     _, value, grad_x, grad_y, grad_z = lax.sort(
         (order, total[0], total[1], total[2], total[3]), num_keys=1, is_stable=False
     )

time: 151 us -> 136 us (0.901)
  other arithmetic: 27.6 us -> 18.6 us
  Pallas kernels: 91.2 us -> 82.4 us
  waiting for transfers between devices: 10.7 us -> 14.6 us
  local copies, waits for them, and re-layouts: 5.91 us -> 4.06 us
    convert_element_type x3 -> x0, other arithmetic: 6.06 us -> none  [halves(): return (high.astype(BF16), (value - high).astype(BF16))]
    pallas_call x1, Pallas kernels: 55.4 us -> 50.8 us  [shards(): pl.pallas_call(functools.partial(far_kernel, longer, unroll, chunks, n_x,...]
    ppermute x12, waiting for transfers between devices: 10.7 us -> 14.6 us  [exchange(): return lax.ppermute(value, axis, pairs)]
    pallas_call x1, Pallas kernels: 19.3 us -> 15.8 us  [shards(): pl.pallas_call(functools.partial(last_kernel, unroll, chunks, n_x), grid_...]
    concatenate x3 -> x0, other arithmetic: 2.7 us -> none  [the longest x1 0.98 us: shards(): jnp.concatenate([b_high, b_high, b_low], axis=0)]
    squeeze x2 -> x0, local copies, waits for them, and re-layouts: 1.94 us -> none  [the longest x1 0.97 us: shards(): far_total = fold([far_sums[s] for s in range(half)])]
  transfers between devices with their start and end apart: 12 -> 12, of which waited for: 4 -> 4; matrix products, arithmetic and copies ran while one was open for 10% -> 4% of each run, Pallas kernels for 24% -> 23%
where the time goes in v3:
time: 136 us; the launch traced here: 135 us
  Pallas kernels  82.4 us (61%)
  other arithmetic  18.6 us (14%)
  starting transfers between devices  14.8 us (11%)
  waiting for transfers between devices  14.6 us (11%)
  local copies, waits for them, and re-layouts  4.06 us (3%)
    pallas_call x1, Pallas kernels, shards(): pl.pallas_call(functools.partial(far_kernel, longer, unroll, chunks, n_x,...  50.8 us
    pallas_call x1, Pallas kernels, shards(): pl.pallas_call(functools.partial(last_kernel, unroll, chunks, n_x), grid_...  15.8 us
    pallas_call x1, Pallas kernels, shards(): pl.pallas_call(functools.partial(near_kernel, longer, chunks, n_x), grid_...  15.8 us
    ppermute x12, starting transfers between devices, exchange(): return lax.ppermute(value, axis, pairs)  14.8 us
    ppermute x12, waiting for transfers between devices, exchange(): return lax.ppermute(value, axis, pairs)  14.6 us
    sort x1, other arithmetic, shards(): lax.sort((cell_x, cell_y, cell_z, fraction[0], fraction[1], fraction[2],...  5.83 us
    sort x1, other arithmetic, shards(): lax.sort((order, total[0], total[1], total[2], total[3]), num_keys=1, is_...  5.62 us
    div x1, other arithmetic, green_of(): jnp.where(total > 0, jnp.exp(-0.5 * total) / safe, F32(0.0))  2.83 us
  transfers between devices with their start and end apart: 12, of which 4 were waited for; matrix products, arithmetic and copies ran while one was open for 4% of the time, Pallas kernels for 23%

profile of v3, /device:TPU:0, one launch (start us, length us, event | category | flops | bytes accessed | tf_op | source)
XLA Modules:
  0.0 135.4 jit_solution(5695981566204180106)
XLA Ops:
  0.6 1.0 fusion.14
  1.7 5.8 %sort.84 = (s32[4096]{0:T(1024)S(1)}, s32[4096]{0:T(1024)S(1)}, s32[4096]{0:T(1024)S(1)}, f32[4096]{0:T(1024)S(1)}, f32[4096]{0:T(1024)S(1)}, /*index=5*/f32[4096]{0:T(1024)S(1)}, f32[4096]{0:T(1024)S(1)}, s32[4096]{0:T(1024)S(1)}) sort(s32[4096]{0:T(1024)} %param.8, s32[4096]{0:T(1024)} %param.9, s32[4096]{0:T(1024)} %param.10, f32[4096]{0:T(1024)S(1)} %bitcast.68, ...), dimensions={0}, to_apply=%region_0.0 | sort | flops 49152 | bytes 262144 | tf_op jit(solution)/shard_map/sort | solution.py:467
  8.0 5.1 %collective-permute-start.2 = (f32[8,4096]{1,0:T(8,128)S(1)}, f32[8,4096]{1,0:T(8,128)S(1)}, u32[]{:S(2)}, u32[]{:S(2)}) collective-permute-start(f32[8,4096]{1,0:T(8,128)S(1)} %stack.72), channel_id=1, source_target_pairs={{0,12},{4,0},{8,4},{12,8},{1,13},{5,1},{9,5},{13,9},{2,14},{6,2},{... | collective-permute-start | bytes 393224 | tf_op jit(solution)/shard_map/ppermute | solution.py:434
  13.1 1.0 collective-permute-start
  14.6 2.8 %fusion.1.refs_6_ = f32[16,256,256]{2,1,0:T(8,128)} fusion(f32[256]{0:T(256)S(1)} %multiply_multiply_fusion, f32[16,256]{1,0:T(8,128)S(1)} %broadcast_add_fusion), kind=kLoop, calls=%fused_computation.5 | loop fusion | flops 7340032 | bytes 4211712 | tf_op jit(solution)/shard_map/div | solution.py:426
  17.5 6.9 %collective-permute-done.1 = f32[8,4096]{1,0:T(8,128)S(1)} collective-permute-done((f32[8,4096]{1,0:T(8,128)S(1)}, f32[8,4096]{1,0:T(8,128)S(1)}, u32[]{:S(2)}, u32[]{:S(2)}) %collective-permute-start.1) | collective-permute-done | bytes 131104 | tf_op jit(solution)/shard_map/ppermute | solution.py:434
  24.4 0.6 gather_fusion
  25.0 0.8 broadcast_in_dim.38.tab_ref
  26.1 1.6 %collective-permute-start.4 = (f32[4,8,4096]{2,0,1:T(4,128)S(1)}, f32[4,8,4096]{2,0,1:T(4,128)S(1)}, u32[]{:S(2)}, u32[]{:S(2)}) collective-permute-start(f32[4,8,4096]{2,0,1:T(4,128)S(1)} %copy.19), channel_id=1, source_target_pairs={{0,2},{1,3},{2,0},{3,1},{4,6},{5,7},{6,4},{7,5},{8,10},{9,11},{10,... | collective-permute-start | bytes 1572872 | tf_op jit(solution)/shard_map/ppermute | solution.py:434
  27.9 0.6 and_select_fusion.1.pass_ref
  28.5 15.8 %near_spread.1 = (f32[2,272,16,128]{3,2,1,0:T(8,128)}, f32[8,32,4096]{2,1,0:T(8,128)}) custom-call(s32[256]{0:T(256)} %copy-done.2, s32[256]{0:T(256)} %and_select_fusion.1.pass_ref, f32[7,16,128]{2,1,0:T(8,128)} %broadcast_in_dim.38.tab_ref, f32[4,8,4096]{2,1,0:T(8,128)} %copy-done, f32[4,8,4096]{2,1,0:T(8,128)} %copy-done.4), custom_call_target="tpu_custom_call" | custom-call | flops 19660800000 | bytes 5242880 | tf_op jit(solution)/shard_map/near_spread/pallas_call | solution.py:558
  44.9 1.7 %collective-permute-done.5.refs_1_ = f32[4,8,4096]{2,1,0:T(8,128)S(1)} collective-permute-done((f32[4,8,4096]{2,1,0:T(8,128)S(1)}, f32[4,8,4096]{2,1,0:T(8,128)S(1)}, u32[]{:S(2)}, u32[]{:S(2)}) %collective-permute-start.5) | collective-permute-done | bytes 524320 | tf_op jit(solution)/shard_map/ppermute | solution.py:434
  47.3 50.8 %far_spread_filter_sample.1 = (bf16[2,4352,256]{2,1,0:T(8,128)(2,1)}, f32[4,4,4096]{2,1,0:T(4,128)}, f32[4,4,4096]{2,1,0:T(4,128)}) custom-call(s32[256]{0:T(256)} %copy-done.3, s32[256]{0:T(256)} %and_select_fusion.pass_ref, s32[1]{0:T(128)} %bitcast.21.at_ref, f32[7,16,128]{2,1,0:T(8,128)} %broadcast_in_dim.38.tab_ref, f32[4,8,4096]{2,1,0:T(8,128)} %copy-done.1, ...), custom_call_target="tpu_custom_call" | custom-call | flops 58982400000 | bytes 15728640 | tf_op jit(solution)/shard_map/far_spread_filter_sample/pallas_call | solution.py:584
  98.1 1.5 %collective-permute-start.7 = (f32[4,4,4096]{2,1,0:T(4,128)}, f32[4,4,4096]{2,1,0:T(4,128)S(1)}, u32[]{:S(2)}, u32[]{:S(2)}) collective-permute-start(f32[4,4,4096]{2,1,0:T(4,128)} %get-tuple-element.51), channel_id=1, source_target_pairs={{0,2},{1,3},{2,0},{3,1},{4,6},{5,7},{6,4},{7,5},{8,10},{9,11},{10,... | collective-permute-start | bytes 786440 | tf_op jit(solution)/shard_map/ppermute | solution.py:434
  100.2 15.8 %near_sample.1 = (f32[4,4,4096]{2,1,0:T(4,128)}, f32[4,4,4096]{2,1,0:T(4,128)}) custom-call(s32[256]{0:T(256)} %copy-done.2, s32[256]{0:T(256)} %and_select_fusion.1.pass_ref, f32[7,16,128]{2,1,0:T(8,128)} %broadcast_in_dim.38.tab_ref, f32[4,8,4096]{2,1,0:T(8,128)} %copy-done, f32[4,8,4096]{2,1,0:T(8,128)} %copy-done.4, ...), custom_call_target="tpu_custom_call" | custom-call | flops 19660800000 | bytes 5242880 | tf_op jit(solution)/shard_map/near_sample/pallas_call | solution.py:628
  116.0 1.0 add.224
  117.2 1.5 %collective-permute-done.8 = f32[4,4,4096]{2,1,0:T(4,128)S(1)} collective-permute-done((f32[4,4,4096]{2,1,0:T(4,128)S(1)}, f32[4,4,4096]{2,1,0:T(4,128)S(1)}, u32[]{:S(2)}, u32[]{:S(2)}) %collective-permute-start.8) | collective-permute-done | bytes 262176 | tf_op jit(solution)/shard_map/ppermute | solution.py:434
  118.7 1.0 add_add_fusion
  119.7 1.7 %collective-permute-start.11 = (f32[4,4096]{1,0:T(4,128)S(1)}, f32[4,4096]{1,0:T(4,128)S(1)}, u32[]{:S(2)}, u32[]{:S(2)}) collective-permute-start(f32[4,4096]{1,0:T(4,128)S(1)} %get-tuple-element.59), channel_id=1, source_target_pairs={{0,12},{4,0},{8,4},{12,8},{1,13},{5,1},{9,5},{13,9},{2,14},{6,2},{... | collective-permute-start | bytes 196616 | tf_op jit(solution)/shard_map/ppermute | solution.py:434
  121.4 1.1 collective-permute-start.10
  122.5 1.9 %collective-permute-start.9 = (f32[4,4096]{1,0:T(4,128)S(1)}, f32[4,4096]{1,0:T(4,128)S(1)}, u32[]{:S(2)}, u32[]{:S(2)}) collective-permute-start(f32[4,4096]{1,0:T(4,128)S(1)} %get-tuple-element.58), channel_id=1, source_target_pairs={{0,4},{4,8},{8,12},{12,0},{1,5},{5,9},{9,13},{13,1},{2,6},{6,10},{... | collective-permute-start | bytes 196616 | tf_op jit(solution)/shard_map/ppermute | solution.py:434
  124.4 4.6 %collective-permute-done.10 = f32[4,4096]{1,0:T(4,128)S(1)} collective-permute-done((f32[4,4096]{1,0:T(4,128)S(1)}, f32[4,4096]{1,0:T(4,128)S(1)}, u32[]{:S(2)}, u32[]{:S(2)}) %collective-permute-start.10) | collective-permute-done | bytes 65568 | tf_op jit(solution)/shard_map/ppermute | solution.py:434
  129.1 5.6 %sort.85 = (s32[4096]{0:T(1024)}, f32[4096]{0:T(1024)}, f32[4096]{0:T(1024)S(1)}, f32[4096]{0:T(1024)S(1)}, f32[4096]{0:T(1024)S(1)}) sort(s32[4096]{0:T(1024)S(1)} %get-tuple-element.29, f32[4096]{0:T(1024)S(1)} %bitcast.66, f32[4096]{0:T(1024)S(1)} %bitcast.65, f32[4096]{0:T(1024)S(1)} %bitcast.64, f32[4096]{0:T(1024)S(1)} %bitcast.63), dimensions={0}, to_apply=%region_1.2 | sort | flops 49152 | bytes 163840 | tf_op jit(solution)/shard_map/sort | solution.py:650
  134.7 0.7 maximum_negate_fusion
  (65 shorter events, 3.7 us)
Async XLA Ops:
  8.0 9.4 %collective-permute-start.2 = (f32[8,4096]{1,0:T(8,128)S(1)}, f32[8,4096]{1,0:T(8,128)S(1)}, u32[]{:S(2)}, u32[]{:S(2)}) collective-permute-start(f32[8,4096]{1,0:T(8,128)S(1)} %stack.72), channel_id=1, source_target_pairs={{0,12},{4,0},{8,4},{12,8},{1,13},{5,1},{9,5},{13,9},{2,14},{6,2},{... | collective-permute-start | bytes 393224 | tf_op jit(solution)/shard_map/ppermute | solution.py:434
  13.1 11.2 %collective-permute-start.1 = (f32[8,4096]{1,0:T(8,128)S(1)}, f32[8,4096]{1,0:T(8,128)S(1)}, u32[]{:S(2)}, u32[]{:S(2)}) collective-permute-start(f32[8,4096]{1,0:T(8,128)S(1)} %stack.72), channel_id=1, source_target_pairs={{0,8},{4,12},{8,0},{12,4},{1,9},{5,13},{9,1},{13,5},{2,10},{6,14},... | collective-permute-start | bytes 393224 | tf_op jit(solution)/shard_map/ppermute | solution.py:434
  13.1 11.2 %collective-permute-start = (f32[8,4096]{1,0:T(8,128)S(1)}, f32[8,4096]{1,0:T(8,128)S(1)}, u32[]{:S(2)}, u32[]{:S(2)}) collective-permute-start(f32[8,4096]{1,0:T(8,128)S(1)} %stack.72), channel_id=1, source_target_pairs={{0,4},{4,8},{8,12},{12,0},{1,5},{5,9},{9,13},{13,1},{2,6},{6,10},{... | collective-permute-start | bytes 393224 | tf_op jit(solution)/shard_map/ppermute | solution.py:434
  25.0 3.5 %copy-start = (f32[4,8,4096]{2,1,0:T(8,128)}, f32[4,8,4096]{2,1,0:T(8,128)S(1)}, u32[]{:S(2)}) copy-start(f32[4,8,4096]{2,1,0:T(8,128)S(1)} %gather_fusion) | copy-start | bytes 1572868
  25.8 1.9 %collective-permute-start.3 = (f32[4,8,4096]{2,1,0:T(8,128)S(1)}, f32[4,8,4096]{2,1,0:T(8,128)S(1)}, u32[]{:S(2)}, u32[]{:S(2)}) collective-permute-start(f32[4,8,4096]{2,1,0:T(8,128)S(1)} %gather_fusion), channel_id=1, source_target_pairs={{0,1},{1,0},{2,3},{3,2},{4,5},{5,4},{6,7},{7,6},{8,9},{9,8},{10,11... | collective-permute-start | bytes 1572872 | tf_op jit(solution)/shard_map/ppermute | solution.py:434
  26.1 18.1 %collective-permute-start.4 = (f32[4,8,4096]{2,0,1:T(4,128)S(1)}, f32[4,8,4096]{2,0,1:T(4,128)S(1)}, u32[]{:S(2)}, u32[]{:S(2)}) collective-permute-start(f32[4,8,4096]{2,0,1:T(4,128)S(1)} %copy.19), channel_id=1, source_target_pairs={{0,2},{1,3},{2,0},{3,1},{4,6},{5,7},{6,4},{7,5},{8,10},{9,11},{10,... | collective-permute-start | bytes 1572872 | tf_op jit(solution)/shard_map/ppermute | solution.py:434
  27.7 0.8 copy-start.4
  27.8 0.6 copy-start.2
  44.6 2.8 %copy-start.1 = (f32[4,8,4096]{2,1,0:T(8,128)}, f32[4,8,4096]{2,1,0:T(8,128)S(1)}, u32[]{:S(2)}) copy-start(f32[4,8,4096]{2,1,0:T(8,128)S(1)} %copy.21.refs_0_) | copy-start | bytes 1572868
  44.6 2.0 %collective-permute-start.5 = (f32[4,8,4096]{2,1,0:T(8,128)S(1)}, f32[4,8,4096]{2,1,0:T(8,128)S(1)}, u32[]{:S(2)}, u32[]{:S(2)}) collective-permute-start(f32[4,8,4096]{2,1,0:T(8,128)S(1)} %copy.21.refs_0_), channel_id=1, source_target_pairs={{0,1},{1,0},{2,3},{3,2},{4,5},{5,4},{6,7},{7,6},{8,9},{9,8},{10,11... | collective-permute-start | bytes 1572872 | tf_op jit(solution)/shard_map/ppermute | solution.py:434
  46.5 0.8 copy-start.5
  46.7 0.6 copy-start.3
  98.1 17.9 %collective-permute-start.7 = (f32[4,4,4096]{2,1,0:T(4,128)}, f32[4,4,4096]{2,1,0:T(4,128)S(1)}, u32[]{:S(2)}, u32[]{:S(2)}) collective-permute-start(f32[4,4,4096]{2,1,0:T(4,128)} %get-tuple-element.51), channel_id=1, source_target_pairs={{0,2},{1,3},{2,0},{3,1},{4,6},{5,7},{6,4},{7,5},{8,10},{9,11},{10,... | collective-permute-start | bytes 786440 | tf_op jit(solution)/shard_map/ppermute | solution.py:434
  99.7 17.5 %collective-permute-start.6 = (f32[4,4,4096]{2,1,0:T(4,128)}, f32[4,4,4096]{2,1,0:T(4,128)S(1)}, u32[]{:S(2)}, u32[]{:S(2)}) collective-permute-start(f32[4,4,4096]{2,1,0:T(4,128)} %get-tuple-element.49), channel_id=1, source_target_pairs={{0,2},{1,3},{2,0},{3,1},{4,6},{5,7},{6,4},{7,5},{8,10},{9,11},{10,... | collective-permute-start | bytes 786440 | tf_op jit(solution)/shard_map/ppermute | solution.py:434
  117.1 1.6 %collective-permute-start.8 = (f32[4,4,4096]{2,1,0:T(4,128)S(1)}, f32[4,4,4096]{2,1,0:T(4,128)S(1)}, u32[]{:S(2)}, u32[]{:S(2)}) collective-permute-start(f32[4,4,4096]{2,1,0:T(4,128)S(1)} %add.224), channel_id=1, source_target_pairs={{0,1},{1,0},{2,3},{3,2},{4,5},{5,4},{6,7},{7,6},{8,9},{9,8},{10,11... | collective-permute-start | bytes 786440 | tf_op jit(solution)/shard_map/ppermute | solution.py:434
  119.7 4.7 %collective-permute-start.11 = (f32[4,4096]{1,0:T(4,128)S(1)}, f32[4,4096]{1,0:T(4,128)S(1)}, u32[]{:S(2)}, u32[]{:S(2)}) collective-permute-start(f32[4,4096]{1,0:T(4,128)S(1)} %get-tuple-element.59), channel_id=1, source_target_pairs={{0,12},{4,0},{8,4},{12,8},{1,13},{5,1},{9,5},{13,9},{2,14},{6,2},{... | collective-permute-start | bytes 196616 | tf_op jit(solution)/shard_map/ppermute | solution.py:434
  121.4 7.6 %collective-permute-start.10 = (f32[4,4096]{1,0:T(4,128)S(1)}, f32[4,4096]{1,0:T(4,128)S(1)}, u32[]{:S(2)}, u32[]{:S(2)}) collective-permute-start(f32[4,4096]{1,0:T(4,128)S(1)} %get-tuple-element.60), channel_id=1, source_target_pairs={{0,8},{4,12},{8,0},{12,4},{1,9},{5,13},{9,1},{13,5},{2,10},{6,14},... | collective-permute-start | bytes 196616 | tf_op jit(solution)/shard_map/ppermute | solution.py:434
  122.5 6.5 %collective-permute-start.9 = (f32[4,4096]{1,0:T(4,128)S(1)}, f32[4,4096]{1,0:T(4,128)S(1)}, u32[]{:S(2)}, u32[]{:S(2)}) collective-permute-start(f32[4,4096]{1,0:T(4,128)S(1)} %get-tuple-element.58), channel_id=1, source_target_pairs={{0,4},{4,8},{8,12},{12,0},{1,5},{5,9},{9,13},{13,1},{2,6},{6,10},{... | collective-permute-start | bytes 196616 | tf_op jit(solution)/shard_map/ppermute | solution.py:434

commit v4 on v3

--- a/solution.py
+++ b/solution.py
@@ -12,23 +12,13 @@
 LANES = 128
 ROWS = 16
 PLANES = 7
-TABLES = 7
+AHEAD = 1
+TABLES = 9
 PAD = 16
 LINES = 80
 F32 = jnp.float32
 BF16 = jnp.bfloat16
 NT = (((1,), (1,)), ((), ()))
-
-SIN_PI = (3.141592640130707, -5.167710083507877, 2.550077523214437, -0.5982912856197345, 0.07765766030450941)
-COS_PI = (
-    0.9999999997799038,
-    -4.934802137078749,
-    4.058709159554242,
-    -1.335212003029471,
-    0.23493731372678894,
-    -0.024396324214549327,
-)
-
 
 def poly(coefficients, x):
     result = coefficients[-1]
@@ -80,15 +70,13 @@
 
 
 def rotation(tab, row_z):
-    turn = tab[0] * wide(row_z + 0.5, ROWS)
-    turn = turn - jnp.round(turn)
-    square = turn * turn
-    sine = turn * poly(SIN_PI, square)
-    cosine = poly(COS_PI, square)
-    twice = sine + sine
-    full_cos = 1.0 - twice * sine
-    full_sin = twice * cosine
-    return full_cos + full_sin, full_cos - full_sin
+    cell = wide(row_z, 8).astype(jnp.int32) & (LANES - 1)
+
+    def look(table):
+        tiles = [table[i : i + 8] for i in range(0, ROWS, 8)]
+        return jnp.concatenate([jnp.take_along_axis(t, cell, axis=1) for t in tiles], axis=0)
+
+    return look(tab[0]), look(tab[7])
 
 
 def along_z(tab, plus, minus, middle, square):
@@ -135,12 +123,18 @@
     return load
 
 
-def rounds(unroll, chunks, begin, base_ref, pass_ref, one_pass):
+def rounds(unroll, chunks, begin, base_ref, pass_ref, prepare, finish):
     def some(i, most):
+        waiting = []
         for u in range(unroll):
             index = begin + i * unroll + u
             most = jnp.maximum(most, pass_ref[index])
-            one_pass(place_of(i * unroll + u), base_ref[index], False)
+            place, start = place_of(i * unroll + u), base_ref[index]
+            waiting.append((place, start, prepare(place, start, False)))
+            if len(waiting) > AHEAD:
+                finish(*waiting.pop(0), False)
+        for item in waiting:
+            finish(*item, False)
         return most
 
     most = lax.fori_loop(0, chunks // unroll, some, jnp.int32(1))
@@ -149,7 +143,8 @@
     def _():
         def one(u, carry):
             def more(p, carry):
-                one_pass(place_of(u), base_ref[begin + u] + p * PLANES, True)
+                place, start = place_of(u), base_ref[begin + u] + p * PLANES
+                finish(place, start, prepare(place, start, True), True)
                 return carry
 
             return lax.fori_loop(1, pass_ref[begin + u], more, carry)
@@ -161,7 +156,8 @@
     plus, minus = rotation(tab, rows[2:3])
     middle = wide(rows[5:6] - 0.5, ROWS)
     square = middle * middle
-    charge = wide(rows[6:7], ROWS)
+    turned = tab[8] * (wide(rows[2:3], ROWS) >= F32(N // 2)).astype(F32)
+    charge = wide(rows[6:7], ROWS) * (1.0 - 2.0 * turned)
     z = along_z(tab, plus, minus, middle, square) * charge
     return z, slope_along_z(tab, plus, minus, middle, square) * charge
 
@@ -169,26 +165,26 @@
 def spread(unroll, chunks, step, base_ref, pass_ref, tab_ref, load, out_ref, kept):
     tab = [tab_ref[m] for m in range(TABLES)]
     cubic = coefficients(SPLINE)
-    empty = jnp.zeros((LANES - LINES, 2 * LANES), BF16)
-
-    def one_pass(place, start, again):
+    empty = jnp.zeros((LANES - LINES, LANES), BF16)
+
+    def prepare(place, start, again):
         rows = load(place)
         z, z_slope = factors(rows, tab)
         if kept is not None and not again:
             kept[:ROWS, place] = z
             kept[ROWS:, place] = z_slope
         high, low = along_y(rows[1:2], [poly(cubic, wide(rows[4:5], 8))])
-        lines = jnp.concatenate(
-            [lanes([high, high]), empty, lanes([low, jnp.zeros_like(low)]), empty], axis=0
-        )
+        high, low = [jnp.concatenate([v, empty], axis=0) for v in (high, low)]
+        lines = lanes([high, high, low])
         x = pick(poly(cubic, wide(rows[3:4], 8)), x_index(start, rows[0:1]))
         pieces = [split(wide(x[m : m + 1], ROWS) * z) for m in range(PLANES)]
-        left = lanes([jnp.concatenate([p[k] for p in pieces], axis=0) for k in range(2)])
-        both = lax.dot_general(left, lines, NT, preferred_element_type=F32)
-        total = both[:, :LANES] + both[:, LANES:]
+        left = lanes([jnp.concatenate([p[k] for p in pieces], axis=0) for k in (0, 1, 0)])
+        return lax.dot_general(left, lines, NT, preferred_element_type=F32)
+
+    def finish(place, start, total, again):
         out_ref[pl.ds(start, PLANES)] += total.reshape(PLANES, ROWS, LANES)
 
-    rounds(unroll, chunks, step * chunks, base_ref, pass_ref, one_pass)
+    rounds(unroll, chunks, step * chunks, base_ref, pass_ref, prepare, finish)
 
 
 def add_rows(terms):
@@ -206,17 +202,20 @@
     tab = [tab_ref[m] for m in range(TABLES)]
     cubic, quadratic = coefficients(SPLINE), coefficients(SLOPES)
 
-    def one_pass(place, start, again):
+    def prepare(place, start, again):
         rows = load(place)
+        part = wide(rows[4:5], 8)
+        high, low, s_high, s_low = along_y(rows[1:2], [poly(cubic, part), poly(quadratic, part)])
+        lines = lanes([stack_lines(high, low), stack_lines(s_high, s_low)])
+        field = field_ref[pl.ds(start, PLANES)].reshape(PLANES * ROWS, N)
+        return rows, jnp.dot(field, lines, preferred_element_type=F32)
+
+    def finish(place, start, prepared, again):
+        rows, sampled = prepared
         if kept is None:
             z, z_slope = factors(rows, tab)
         else:
             z, z_slope = kept[:ROWS, place], kept[ROWS:, place]
-        part = wide(rows[4:5], 8)
-        high, low, s_high, s_low = along_y(rows[1:2], [poly(cubic, part), poly(quadratic, part)])
-        lines = lanes([stack_lines(high, low), stack_lines(s_high, s_low)])
-        field = field_ref[pl.ds(start, PLANES)].reshape(PLANES * ROWS, N)
-        sampled = jnp.dot(field, lines, preferred_element_type=F32)
         part = wide(rows[3:4], 8)
         index = x_index(start, rows[0:1])
         x = pick(poly(cubic, part), index)
@@ -235,7 +234,7 @@
             total += out_ref[:, place]
         out_ref[:, place] = total
 
-    rounds(unroll, chunks, step * chunks, base_ref, pass_ref, one_pass)
+    rounds(unroll, chunks, step * chunks, base_ref, pass_ref, prepare, finish)
 
 
 MORE = LANES - LINES
@@ -479,17 +478,20 @@
     far_cos, near_cos = jnp.cos(3 * angle), jnp.cos(angle)
     far_sin, near_sin = jnp.sin(3 * angle), jnp.sin(angle)
     tab = [
-        freq.astype(F32) * F32(1 / N),
         (far_cos + 23 * near_cos) * F32(1 / 24),
         (far_cos - near_cos) * F32(1 / 2),
         (far_sin + 5 * near_sin) * F32(1 / 4),
         far_sin * F32(1 / 3) - near_sin,
         far_cos - near_cos,
         far_sin - 3 * near_sin,
+        (freq % 2).astype(F32),
     ]
-    tab = jnp.stack(tab)
-    tab = jnp.where((jnp.arange(ROWS) < own)[None], tab, F32(0.0))
-    tab = jnp.broadcast_to(tab[:, :, None], (TABLES, ROWS, LANES))
+    tab = [jnp.broadcast_to(t[:, None], (ROWS, LANES)) for t in tab]
+    cells = 2 * jnp.arange(LANES, dtype=jnp.int32) + 1
+    turns = (freq[:, None] * cells[None, :] % (2 * N)).astype(F32) * F32(np.pi / N)
+    turn_cos, turn_sin = jnp.cos(turns), jnp.sin(turns)
+    tab = jnp.stack([turn_cos + turn_sin] + tab[:6] + [turn_cos - turn_sin] + tab[6:])
+    tab = jnp.where((jnp.arange(ROWS) < own)[None, :, None], tab, F32(0.0))
     full = jnp.arange(N, dtype=jnp.int32)
     green = green_of(freq[:own], full, full, N)
 
@@ -500,7 +502,7 @@
         step = s & -s
         groups.append(exchange(groups[s ^ step], "gy", step, True))
 
-    unroll = 8 if chunks % 8 == 0 else 1
+    unroll = 16 if chunks % 16 == 0 else 1
     longer = 32 if chunks % 32 == 0 else unroll
     size = N + PAD
     steps = half * n_x

time: 136 us -> 128 us (0.941)
  Pallas kernels: 82.4 us -> 75.5 us
  waiting for transfers between devices: 14.6 us -> 13.2 us
    pallas_call x1, Pallas kernels: 50.8 us -> 47.2 us  [shards(): pl.pallas_call(functools.partial(far_kernel, longer, unroll, chunks, n_x,...]
    pallas_call x1, Pallas kernels: 15.8 us -> 14 us  [shards(): pl.pallas_call(functools.partial(near_kernel, longer, chunks, n_x), grid_...]
    pallas_call x1, Pallas kernels: 15.8 us -> 14.3 us  [shards(): pl.pallas_call(functools.partial(last_kernel, unroll, chunks, n_x), grid_...]
    ppermute x12, waiting for transfers between devices: 14.6 us -> 13.2 us  [exchange(): return lax.ppermute(value, axis, pairs)]
  transfers between devices with their start and end apart: 12 -> 12, of which waited for: 4 -> 4; matrix products, arithmetic and copies ran while one was open for 4% -> 5% of each run, Pallas kernels for 23% -> 22%
where the time goes in v4:
time: 128 us
  Pallas kernels  75.5 us (59%)
  other arithmetic  19.6 us (15%)
  starting transfers between devices  14.9 us (12%)
  waiting for transfers between devices  13.2 us (10%)
  local copies, waits for them, and re-layouts  3.74 us (3%)
    pallas_call x1, Pallas kernels, shards(): pl.pallas_call(functools.partial(far_kernel, longer, unroll, chunks, n_x,...  47.2 us
    ppermute x12, starting transfers between devices, exchange(): return lax.ppermute(value, axis, pairs)  14.9 us
    pallas_call x1, Pallas kernels, shards(): pl.pallas_call(functools.partial(last_kernel, unroll, chunks, n_x), grid_...  14.3 us
    pallas_call x1, Pallas kernels, shards(): pl.pallas_call(functools.partial(near_kernel, longer, chunks, n_x), grid_...  14 us
    ppermute x12, waiting for transfers between devices, exchange(): return lax.ppermute(value, axis, pairs)  13.2 us
    sort x1, other arithmetic, shards(): lax.sort((cell_x, cell_y, cell_z, fraction[0], fraction[1], fraction[2],...  5.83 us
    sort x1, other arithmetic, shards(): lax.sort((order, total[0], total[1], total[2], total[3]), num_keys=1, is_...  5.62 us
    div x1, other arithmetic, green_of(): jnp.where(total > 0, jnp.exp(-0.5 * total) / safe, F32(0.0))  2.83 us
  transfers between devices with their start and end apart: 12, of which 4 were waited for; matrix products, arithmetic and copies ran while one was open for 5% of the time, Pallas kernels for 22%

profile of v4, /device:TPU:0, one launch (start us, length us, event | category | flops | bytes accessed | tf_op | source)
XLA Modules:
  0.0 127.9 jit_solution(2551472244352865177)
XLA Ops:
  0.6 1.0 fusion.21
  1.7 5.8 %sort.84 = (s32[4096]{0:T(1024)S(1)}, s32[4096]{0:T(1024)S(1)}, s32[4096]{0:T(1024)S(1)}, f32[4096]{0:T(1024)S(1)}, f32[4096]{0:T(1024)S(1)}, /*index=5*/f32[4096]{0:T(1024)S(1)}, f32[4096]{0:T(1024)S(1)}, s32[4096]{0:T(1024)S(1)}) sort(s32[4096]{0:T(1024)} %param.8, s32[4096]{0:T(1024)} %param.9, s32[4096]{0:T(1024)} %param.10, f32[4096]{0:T(1024)S(1)} %bitcast.68, ...), dimensions={0}, to_apply=%region_0.0 | sort | flops 49152 | bytes 262144 | tf_op jit(solution)/shard_map/sort | solution.py:466
  8.0 5.1 %collective-permute-start.2 = (f32[8,4096]{1,0:T(8,128)S(1)}, f32[8,4096]{1,0:T(8,128)S(1)}, u32[]{:S(2)}, u32[]{:S(2)}) collective-permute-start(f32[8,4096]{1,0:T(8,128)S(1)} %stack.67), channel_id=1, source_target_pairs={{0,12},{4,0},{8,4},{12,8},{1,13},{5,1},{9,5},{13,9},{2,14},{6,2},{... | collective-permute-start | bytes 393224 | tf_op jit(solution)/shard_map/ppermute | solution.py:433
  13.1 1.0 collective-permute-start
  14.5 2.8 %fusion.1.refs_6_ = f32[16,256,256]{2,1,0:T(8,128)} fusion(f32[256]{0:T(256)S(1)} %multiply_multiply_fusion, f32[16,256]{1,0:T(8,128)S(1)} %broadcast_add_fusion), kind=kLoop, calls=%fused_computation.5 | loop fusion | flops 7340032 | bytes 4211712 | tf_op jit(solution)/shard_map/div | solution.py:425
  18.1 0.7 broadcast_select_fusion.tab_ref
  18.9 5.5 %collective-permute-done.1 = f32[8,4096]{1,0:T(8,128)S(1)} collective-permute-done((f32[8,4096]{1,0:T(8,128)S(1)}, f32[8,4096]{1,0:T(8,128)S(1)}, u32[]{:S(2)}, u32[]{:S(2)}) %collective-permute-start.1) | collective-permute-done | bytes 131104 | tf_op jit(solution)/shard_map/ppermute | solution.py:433
  24.4 0.6 gather_fusion
  25.4 1.6 %collective-permute-start.4 = (f32[4,8,4096]{2,0,1:T(4,128)S(1)}, f32[4,8,4096]{2,0,1:T(4,128)S(1)}, u32[]{:S(2)}, u32[]{:S(2)}) collective-permute-start(f32[4,8,4096]{2,0,1:T(4,128)S(1)} %copy.19), channel_id=1, source_target_pairs={{0,2},{1,3},{2,0},{3,1},{4,6},{5,7},{6,4},{7,5},{8,10},{9,11},{10,... | collective-permute-start | bytes 1572872 | tf_op jit(solution)/shard_map/ppermute | solution.py:433
  27.8 14.0 %near_spread.1 = (f32[2,272,16,128]{3,2,1,0:T(8,128)}, f32[8,32,4096]{2,1,0:T(8,128)}) custom-call(s32[256]{0:T(256)} %copy-done.2, s32[256]{0:T(256)} %and_select_fusion.1.pass_ref, f32[9,16,128]{2,1,0:T(8,128)} %broadcast_select_fusion.tab_ref, f32[4,8,4096]{2,1,0:T(8,128)} %copy-done, f32[4,8,4096]{2,1,0:T(8,128)} %copy-done.4), custom_call_target="tpu_custom_call" | custom-call | flops 19660800000 | bytes 5242880 | tf_op jit(solution)/shard_map/near_spread/pallas_call | solution.py:560
  42.4 1.7 %collective-permute-done.5.refs_1_ = f32[4,8,4096]{2,1,0:T(8,128)S(1)} collective-permute-done((f32[4,8,4096]{2,1,0:T(8,128)S(1)}, f32[4,8,4096]{2,1,0:T(8,128)S(1)}, u32[]{:S(2)}, u32[]{:S(2)}) %collective-permute-start.5) | collective-permute-done | bytes 524320 | tf_op jit(solution)/shard_map/ppermute | solution.py:433
  44.4 0.6 and_select_fusion.pass_ref
  45.0 47.2 %far_spread_filter_sample.1 = (bf16[2,4352,256]{2,1,0:T(8,128)(2,1)}, f32[4,4,4096]{2,1,0:T(4,128)}, f32[4,4,4096]{2,1,0:T(4,128)}) custom-call(s32[256]{0:T(256)} %copy-done.3, s32[256]{0:T(256)} %and_select_fusion.pass_ref, s32[1]{0:T(128)} %bitcast.21.at_ref, f32[9,16,128]{2,1,0:T(8,128)} %broadcast_select_fusion.tab_ref, f32[4,8,4096]{2,1,0:T(8,128)} %copy-done.1, ...), custom_call_target="tpu_custom_call" | custom-call | flops 58982400000 | bytes 15728640 | tf_op jit(solution)/shard_map/far_spread_filter_sample/pallas_call | solution.py:586
  92.2 1.6 %collective-permute-start.7 = (f32[4,4,4096]{2,1,0:T(4,128)}, f32[4,4,4096]{2,1,0:T(4,128)S(1)}, u32[]{:S(2)}, u32[]{:S(2)}) collective-permute-start(f32[4,4,4096]{2,1,0:T(4,128)} %get-tuple-element.51), channel_id=1, source_target_pairs={{0,2},{1,3},{2,0},{3,1},{4,6},{5,7},{6,4},{7,5},{8,10},{9,11},{10,... | collective-permute-start | bytes 786440 | tf_op jit(solution)/shard_map/ppermute | solution.py:433
  94.3 14.3 %near_sample.1 = (f32[4,4,4096]{2,1,0:T(4,128)}, f32[4,4,4096]{2,1,0:T(4,128)}) custom-call(s32[256]{0:T(256)} %copy-done.2, s32[256]{0:T(256)} %and_select_fusion.1.pass_ref, f32[9,16,128]{2,1,0:T(8,128)} %broadcast_select_fusion.tab_ref, f32[4,8,4096]{2,1,0:T(8,128)} %copy-done, f32[4,8,4096]{2,1,0:T(8,128)} %copy-done.4, ...), custom_call_target="tpu_custom_call" | custom-call | flops 19660800000 | bytes 5242880 | tf_op jit(solution)/shard_map/near_sample/pallas_call | solution.py:630
  108.6 1.0 add.207
  109.7 1.5 %collective-permute-done.8 = f32[4,4,4096]{2,1,0:T(4,128)S(1)} collective-permute-done((f32[4,4,4096]{2,1,0:T(4,128)S(1)}, f32[4,4,4096]{2,1,0:T(4,128)S(1)}, u32[]{:S(2)}, u32[]{:S(2)}) %collective-permute-start.8) | collective-permute-done | bytes 262176 | tf_op jit(solution)/shard_map/ppermute | solution.py:433
  111.2 1.0 add_add_fusion
  112.2 1.7 %collective-permute-start.11 = (f32[4,4096]{1,0:T(4,128)S(1)}, f32[4,4096]{1,0:T(4,128)S(1)}, u32[]{:S(2)}, u32[]{:S(2)}) collective-permute-start(f32[4,4096]{1,0:T(4,128)S(1)} %get-tuple-element.59), channel_id=1, source_target_pairs={{0,12},{4,0},{8,4},{12,8},{1,13},{5,1},{9,5},{13,9},{2,14},{6,2},{... | collective-permute-start | bytes 196616 | tf_op jit(solution)/shard_map/ppermute | solution.py:433
  113.9 1.1 collective-permute-start.10
  115.0 1.9 %collective-permute-start.9 = (f32[4,4096]{1,0:T(4,128)S(1)}, f32[4,4096]{1,0:T(4,128)S(1)}, u32[]{:S(2)}, u32[]{:S(2)}) collective-permute-start(f32[4,4096]{1,0:T(4,128)S(1)} %get-tuple-element.58), channel_id=1, source_target_pairs={{0,4},{4,8},{8,12},{12,0},{1,5},{5,9},{9,13},{13,1},{2,6},{6,10},{... | collective-permute-start | bytes 196616 | tf_op jit(solution)/shard_map/ppermute | solution.py:433
  116.9 4.6 %collective-permute-done.10 = f32[4,4096]{1,0:T(4,128)S(1)} collective-permute-done((f32[4,4096]{1,0:T(4,128)S(1)}, f32[4,4096]{1,0:T(4,128)S(1)}, u32[]{:S(2)}, u32[]{:S(2)}) %collective-permute-start.10) | collective-permute-done | bytes 65568 | tf_op jit(solution)/shard_map/ppermute | solution.py:433
  121.6 5.6 %sort.85 = (s32[4096]{0:T(1024)}, f32[4096]{0:T(1024)}, f32[4096]{0:T(1024)S(1)}, f32[4096]{0:T(1024)S(1)}, f32[4096]{0:T(1024)S(1)}) sort(s32[4096]{0:T(1024)S(1)} %get-tuple-element.29, f32[4096]{0:T(1024)S(1)} %bitcast.66, f32[4096]{0:T(1024)S(1)} %bitcast.65, f32[4096]{0:T(1024)S(1)} %bitcast.64, f32[4096]{0:T(1024)S(1)} %bitcast.63), dimensions={0}, to_apply=%region_1.2 | sort | flops 49152 | bytes 163840 | tf_op jit(solution)/shard_map/sort | solution.py:652
  127.2 0.7 maximum_negate_fusion
  (73 shorter events, 4.4 us)
Async XLA Ops:
  8.0 10.8 %collective-permute-start.2 = (f32[8,4096]{1,0:T(8,128)S(1)}, f32[8,4096]{1,0:T(8,128)S(1)}, u32[]{:S(2)}, u32[]{:S(2)}) collective-permute-start(f32[8,4096]{1,0:T(8,128)S(1)} %stack.67), channel_id=1, source_target_pairs={{0,12},{4,0},{8,4},{12,8},{1,13},{5,1},{9,5},{13,9},{2,14},{6,2},{... | collective-permute-start | bytes 393224 | tf_op jit(solution)/shard_map/ppermute | solution.py:433
  13.1 11.2 %collective-permute-start.1 = (f32[8,4096]{1,0:T(8,128)S(1)}, f32[8,4096]{1,0:T(8,128)S(1)}, u32[]{:S(2)}, u32[]{:S(2)}) collective-permute-start(f32[8,4096]{1,0:T(8,128)S(1)} %stack.67), channel_id=1, source_target_pairs={{0,8},{4,12},{8,0},{12,4},{1,9},{5,13},{9,1},{13,5},{2,10},{6,14},... | collective-permute-start | bytes 393224 | tf_op jit(solution)/shard_map/ppermute | solution.py:433
  13.1 11.2 %collective-permute-start = (f32[8,4096]{1,0:T(8,128)S(1)}, f32[8,4096]{1,0:T(8,128)S(1)}, u32[]{:S(2)}, u32[]{:S(2)}) collective-permute-start(f32[8,4096]{1,0:T(8,128)S(1)} %stack.67), channel_id=1, source_target_pairs={{0,4},{4,8},{8,12},{12,0},{1,5},{5,9},{9,13},{13,1},{2,6},{6,10},{... | collective-permute-start | bytes 393224 | tf_op jit(solution)/shard_map/ppermute | solution.py:433
  25.0 2.8 %copy-start = (f32[4,8,4096]{2,1,0:T(8,128)}, f32[4,8,4096]{2,1,0:T(8,128)S(1)}, u32[]{:S(2)}) copy-start(f32[4,8,4096]{2,1,0:T(8,128)S(1)} %gather_fusion) | copy-start | bytes 1572868
  25.0 2.0 %collective-permute-start.3 = (f32[4,8,4096]{2,1,0:T(8,128)S(1)}, f32[4,8,4096]{2,1,0:T(8,128)S(1)}, u32[]{:S(2)}, u32[]{:S(2)}) collective-permute-start(f32[4,8,4096]{2,1,0:T(8,128)S(1)} %gather_fusion), channel_id=1, source_target_pairs={{0,1},{1,0},{2,3},{3,2},{4,5},{5,4},{6,7},{7,6},{8,9},{9,8},{10,11... | collective-permute-start | bytes 1572872 | tf_op jit(solution)/shard_map/ppermute | solution.py:433
  25.4 16.4 %collective-permute-start.4 = (f32[4,8,4096]{2,0,1:T(4,128)S(1)}, f32[4,8,4096]{2,0,1:T(4,128)S(1)}, u32[]{:S(2)}, u32[]{:S(2)}) collective-permute-start(f32[4,8,4096]{2,0,1:T(4,128)S(1)} %copy.19), channel_id=1, source_target_pairs={{0,2},{1,3},{2,0},{3,1},{4,6},{5,7},{6,4},{7,5},{8,10},{9,11},{10,... | collective-permute-start | bytes 1572872 | tf_op jit(solution)/shard_map/ppermute | solution.py:433
  27.0 0.8 copy-start.4
  27.1 0.7 copy-start.2
  42.1 2.8 %copy-start.1 = (f32[4,8,4096]{2,1,0:T(8,128)}, f32[4,8,4096]{2,1,0:T(8,128)S(1)}, u32[]{:S(2)}) copy-start(f32[4,8,4096]{2,1,0:T(8,128)S(1)} %copy.21.refs_0_) | copy-start | bytes 1572868
  42.2 2.0 %collective-permute-start.5 = (f32[4,8,4096]{2,1,0:T(8,128)S(1)}, f32[4,8,4096]{2,1,0:T(8,128)S(1)}, u32[]{:S(2)}, u32[]{:S(2)}) collective-permute-start(f32[4,8,4096]{2,1,0:T(8,128)S(1)} %copy.21.refs_0_), channel_id=1, source_target_pairs={{0,1},{1,0},{2,3},{3,2},{4,5},{5,4},{6,7},{7,6},{8,9},{9,8},{10,11... | collective-permute-start | bytes 1572872 | tf_op jit(solution)/shard_map/ppermute | solution.py:433
  44.1 0.9 copy-start.5
  44.3 0.7 copy-start.3
  92.2 16.4 %collective-permute-start.7 = (f32[4,4,4096]{2,1,0:T(4,128)}, f32[4,4,4096]{2,1,0:T(4,128)S(1)}, u32[]{:S(2)}, u32[]{:S(2)}) collective-permute-start(f32[4,4,4096]{2,1,0:T(4,128)} %get-tuple-element.51), channel_id=1, source_target_pairs={{0,2},{1,3},{2,0},{3,1},{4,6},{5,7},{6,4},{7,5},{8,10},{9,11},{10,... | collective-permute-start | bytes 786440 | tf_op jit(solution)/shard_map/ppermute | solution.py:433
  93.8 15.9 %collective-permute-start.6 = (f32[4,4,4096]{2,1,0:T(4,128)}, f32[4,4,4096]{2,1,0:T(4,128)S(1)}, u32[]{:S(2)}, u32[]{:S(2)}) collective-permute-start(f32[4,4,4096]{2,1,0:T(4,128)} %get-tuple-element.49), channel_id=1, source_target_pairs={{0,2},{1,3},{2,0},{3,1},{4,6},{5,7},{6,4},{7,5},{8,10},{9,11},{10,... | collective-permute-start | bytes 786440 | tf_op jit(solution)/shard_map/ppermute | solution.py:433
  109.6 1.6 %collective-permute-start.8 = (f32[4,4,4096]{2,1,0:T(4,128)S(1)}, f32[4,4,4096]{2,1,0:T(4,128)S(1)}, u32[]{:S(2)}, u32[]{:S(2)}) collective-permute-start(f32[4,4,4096]{2,1,0:T(4,128)S(1)} %add.207), channel_id=1, source_target_pairs={{0,1},{1,0},{2,3},{3,2},{4,5},{5,4},{6,7},{7,6},{8,9},{9,8},{10,11... | collective-permute-start | bytes 786440 | tf_op jit(solution)/shard_map/ppermute | solution.py:433
  112.2 4.7 %collective-permute-start.11 = (f32[4,4096]{1,0:T(4,128)S(1)}, f32[4,4096]{1,0:T(4,128)S(1)}, u32[]{:S(2)}, u32[]{:S(2)}) collective-permute-start(f32[4,4096]{1,0:T(4,128)S(1)} %get-tuple-element.59), channel_id=1, source_target_pairs={{0,12},{4,0},{8,4},{12,8},{1,13},{5,1},{9,5},{13,9},{2,14},{6,2},{... | collective-permute-start | bytes 196616 | tf_op jit(solution)/shard_map/ppermute | solution.py:433
  113.9 7.6 %collective-permute-start.10 = (f32[4,4096]{1,0:T(4,128)S(1)}, f32[4,4096]{1,0:T(4,128)S(1)}, u32[]{:S(2)}, u32[]{:S(2)}) collective-permute-start(f32[4,4096]{1,0:T(4,128)S(1)} %get-tuple-element.60), channel_id=1, source_target_pairs={{0,8},{4,12},{8,0},{12,4},{1,9},{5,13},{9,1},{13,5},{2,10},{6,14},... | collective-permute-start | bytes 196616 | tf_op jit(solution)/shard_map/ppermute | solution.py:433
  115.0 6.5 %collective-permute-start.9 = (f32[4,4096]{1,0:T(4,128)S(1)}, f32[4,4096]{1,0:T(4,128)S(1)}, u32[]{:S(2)}, u32[]{:S(2)}) collective-permute-start(f32[4,4096]{1,0:T(4,128)S(1)} %get-tuple-element.58), channel_id=1, source_target_pairs={{0,4},{4,8},{8,12},{12,0},{1,5},{5,9},{9,13},{13,1},{2,6},{6,10},{... | collective-permute-start | bytes 196616 | tf_op jit(solution)/shard_map/ppermute | solution.py:433

commit v5 on v4

--- a/solution.py
+++ b/solution.py
@@ -13,6 +13,8 @@
 ROWS = 16
 PLANES = 7
 AHEAD = 1
+FIELDS = 7
+KEPT = 2 * ROWS + 8
 TABLES = 9
 PAD = 16
 LINES = 80
@@ -114,10 +116,12 @@
 
 
 def loader(refs, step, n_x):
-    def load(place):
-        rows = refs[0][0, :, place]
+    def load(u):
+        chunks = refs[0].shape[1] // FIELDS
+        where = pl.ds(u, FIELDS, chunks)
+        rows = refs[0].at[0][where, :]
         for g in range(1, len(refs)):
-            rows = jnp.where(step >= g * n_x, refs[g][0, :, place], rows)
+            rows = jnp.where(step >= g * n_x, refs[g].at[0][where, :], rows)
         return rows
 
     return load
@@ -129,8 +133,8 @@
         for u in range(unroll):
             index = begin + i * unroll + u
             most = jnp.maximum(most, pass_ref[index])
-            place, start = place_of(i * unroll + u), base_ref[index]
-            waiting.append((place, start, prepare(place, start, False)))
+            chunk, start = i * unroll + u, base_ref[index]
+            waiting.append((chunk, start, prepare(chunk, start, False)))
             if len(waiting) > AHEAD:
                 finish(*waiting.pop(0), False)
         for item in waiting:
@@ -143,8 +147,8 @@
     def _():
         def one(u, carry):
             def more(p, carry):
-                place, start = place_of(u), base_ref[begin + u] + p * PLANES
-                finish(place, start, prepare(place, start, True), True)
+                start = base_ref[begin + u] + p * PLANES
+                finish(u, start, prepare(u, start, True), True)
                 return carry
 
             return lax.fori_loop(1, pass_ref[begin + u], more, carry)
@@ -167,12 +171,13 @@
     cubic = coefficients(SPLINE)
     empty = jnp.zeros((LANES - LINES, LANES), BF16)
 
-    def prepare(place, start, again):
-        rows = load(place)
+    def prepare(chunk, start, again):
+        rows, place = load(chunk), place_of(chunk)
         z, z_slope = factors(rows, tab)
         if kept is not None and not again:
             kept[:ROWS, place] = z
-            kept[ROWS:, place] = z_slope
+            kept[ROWS : 2 * ROWS, place] = z_slope
+            kept[2 * ROWS : 2 * ROWS + FIELDS, place] = rows
         high, low = along_y(rows[1:2], [poly(cubic, wide(rows[4:5], 8))])
         high, low = [jnp.concatenate([v, empty], axis=0) for v in (high, low)]
         lines = lanes([high, high, low])
@@ -181,7 +186,7 @@
         left = lanes([jnp.concatenate([p[k] for p in pieces], axis=0) for k in (0, 1, 0)])
         return lax.dot_general(left, lines, NT, preferred_element_type=F32)
 
-    def finish(place, start, total, again):
+    def finish(chunk, start, total, again):
         out_ref[pl.ds(start, PLANES)] += total.reshape(PLANES, ROWS, LANES)
 
     rounds(unroll, chunks, step * chunks, base_ref, pass_ref, prepare, finish)
@@ -199,23 +204,24 @@
 
 
 def sample(unroll, chunks, step, base_ref, pass_ref, tab_ref, load, field_ref, out_ref, kept):
-    tab = [tab_ref[m] for m in range(TABLES)]
+    tab = None if tab_ref is None else [tab_ref[m] for m in range(TABLES)]
     cubic, quadratic = coefficients(SPLINE), coefficients(SLOPES)
 
-    def prepare(place, start, again):
-        rows = load(place)
+    def prepare(chunk, start, again):
+        rows = load(chunk) if kept is None else kept[2 * ROWS :, place_of(chunk)]
         part = wide(rows[4:5], 8)
         high, low, s_high, s_low = along_y(rows[1:2], [poly(cubic, part), poly(quadratic, part)])
         lines = lanes([stack_lines(high, low), stack_lines(s_high, s_low)])
         field = field_ref[pl.ds(start, PLANES)].reshape(PLANES * ROWS, N)
         return rows, jnp.dot(field, lines, preferred_element_type=F32)
 
-    def finish(place, start, prepared, again):
+    def finish(chunk, start, prepared, again):
         rows, sampled = prepared
+        place = place_of(chunk)
         if kept is None:
             z, z_slope = factors(rows, tab)
         else:
-            z, z_slope = kept[:ROWS, place], kept[ROWS:, place]
+            z, z_slope = kept[:ROWS, place], kept[ROWS : 2 * ROWS, place]
         part = wide(rows[3:4], 8)
         index = x_index(start, rows[0:1])
         x = pick(poly(cubic, part), index)
@@ -343,17 +349,28 @@
             both = jnp.concatenate([high, high, low], axis=0)
             return jnp.dot(table_ref[...], both, preferred_element_type=F32)
 
+        first_half = lax.broadcasted_iota(jnp.int32, (N, LANES), 1) < LANES // 2
+
+        def lines_of(own, t):
+            before, here, after = [
+                flat.at[(2 * t + s) % (2 * groups)][own, :] for s in (-1, 0, 1)
+            ]
+            return here + pltpu.roll(jnp.where(first_half, after, before), LANES // 2, 1)
+
         at_once = green_ref.shape[0]
         begin = ROWS + (step - spreads) * at_once
         owns = [pl.ds(begin + u, N, ROWS) for u in range(at_once)]
-        values = [lanes([flat.at[s][own, :] for s in range(2 * groups)]) for own in owns]
+        values = [lanes([lines_of(own, t) for t in range(groups)]) for own in owns]
         values = [right(v, lines_ref) for v in values]
         values = [left(v) * green_ref[u] for u, v in enumerate(values)]
         values = [left(v) for v in values]
         values = [right(v, back_ref) for v in values]
         for own, value in zip(owns, values):
-            for s in range(2 * groups):
-                flat.at[s][own, :] = value[:, s * LANES : (s + 1) * LANES]
+            tiles = [value[:, t * LANES : (t + 1) * LANES] for t in range(groups)]
+            for t in range(groups):
+                flat.at[2 * t][own, :] = tiles[t]
+                odd = jnp.where(first_half, tiles[(t + 1) % groups], tiles[t])
+                flat.at[2 * t + 1][own, :] = pltpu.roll(odd, LANES // 2, 1)
 
     far_flat = far_field.reshape(groups, (N + PAD) * ROWS, N)
 
@@ -375,28 +392,21 @@
         deliver(now, n_x, sums, out_refs)
 
 
-def last_kernel(unroll, chunks, n_x, base_ref, pass_ref, tab_ref, *refs):
-    groups = (len(refs) - 3) // 2
-    in_refs, (kept, field_ref) = refs[:groups], refs[groups : groups + 2]
-    out_refs, sums = refs[groups + 2 : -1], refs[-1]
+def last_kernel(unroll, chunks, n_x, base_ref, pass_ref, kept, field_ref, *refs):
+    out_refs, sums = refs[:-1], refs[-1]
     step = pl.program_id(0)
-    load = loader(in_refs, step, n_x)
-    sample(
-        unroll, chunks, step, base_ref, pass_ref, tab_ref, load, field_ref.at[0], sums, kept.at[0]
-    )
+    sample(unroll, chunks, step, base_ref, pass_ref, None, None, field_ref.at[0], sums, kept.at[0])
     deliver(step, n_x, sums, out_refs)
 
 
-def tables(n_y, planes_y):
+def tables():
     def halves(value):
         value = value.astype(np.float32)
         high = value.astype(BF16)
         return high, (value - high.astype(np.float32)).astype(BF16)
 
     full = np.arange(N)
-    reach = np.arange(LANES)
-    line = np.concatenate([b * planes_y + reach - 1 for b in range(n_y)]) % N
-    used = np.tile(reach < planes_y + 3, n_y)
+    line = (full - 1) % N
 
     def table(rows, columns):
         angle = (rows[:, None] * columns[None, :] % N) * (2.0 * np.pi / N)
@@ -404,9 +414,9 @@
 
     high, low = halves(table(full, full))
     left = np.concatenate([high, low, high], axis=1)
-    high, low = halves(table(line, full) * used[:, None])
+    high, low = halves(table(line, full))
     lines = np.concatenate([high, high, low], axis=0)
-    high, low = halves(table(full, line) * used[None, :])
+    high, low = halves(table(full, line))
     return left, lines, np.concatenate([high, high, low], axis=0)
 
 
@@ -458,7 +468,8 @@
     count = charge.shape[0]
     n_x, n_y = lax.axis_size("gx"), lax.axis_size("gy")
     at_x, at_y = lax.axis_index("gx"), lax.axis_index("gy")
-    planes_x, planes_y = N // n_x, N // n_y
+    planes_x = N // n_x
+    assert 2 * (N // n_y) == LANES
     own = N // (n_x * n_y)
     chunks = count // LANES
     place = jnp.arange(count, dtype=jnp.int32)
@@ -469,9 +480,8 @@
         is_stable=False,
     )
     plane = (key + at_x * planes_x).astype(F32)
-    ends = plane.reshape(chunks, LANES)
-    ends = jnp.concatenate([ends[:, 0], ends[:, -1], jnp.zeros((count - 2 * chunks,), F32)])
-    packed = jnp.stack([plane, cy.astype(F32), cz.astype(F32), fx, fy, fz, q, ends])
+    sent = [plane, cy.astype(F32), cz.astype(F32), fx, fy, fz, q]
+    packed = jnp.concatenate([v.reshape(chunks, LANES) for v in sent])
 
     freq = (at_x * n_y + at_y) * own + jnp.arange(ROWS, dtype=jnp.int32)
     angle = freq.astype(F32) * F32(np.pi / N)
@@ -511,8 +521,8 @@
     params = pltpu.CompilerParams(vmem_limit_bytes=56 * 1024 * 1024)
 
     def bounds(some):
-        ends = jnp.concatenate([g[:, 7, : 2 * chunks] for g in some]).astype(jnp.int32)
-        first, last = ends[:, :chunks].reshape(-1), ends[:, chunks:].reshape(-1)
+        planes = jnp.concatenate([g[:, :chunks] for g in some]).astype(jnp.int32)
+        first, last = planes[:, :, 0].reshape(-1), planes[:, :, -1].reshape(-1)
         return first, (last - first + (3 + PLANES)) // PLANES
 
     def clamp(step, top):
@@ -526,7 +536,7 @@
                     at = jnp.where(t >= begin, clamp(t - begin - g * n_x, n_x - 1), at)
                 return (at, 0, 0)
 
-            return pl.BlockSpec((1, 8, count), place)
+            return pl.BlockSpec((1, FIELDS * chunks, LANES), place)
 
         return [spec(g) for g in range(half)]
 
@@ -555,8 +565,8 @@
     near = groups[:half]
     near_bounds = bounds(near)
 
-    kept_spec = pl.BlockSpec((1, 2 * ROWS, count), lambda t, *_: (t, 0, 0))
-    kept_shape = jax.ShapeDtypeStruct((steps, 2 * ROWS, count), F32)
+    kept_spec = pl.BlockSpec((1, KEPT, count), lambda t, *_: (t, 0, 0))
+    kept_shape = jax.ShapeDtypeStruct((steps, KEPT, count), F32)
     near_mesh, near_kept = pl.pallas_call(
         functools.partial(near_kernel, longer, chunks, n_x),
         grid_spec=pltpu.PrefetchScalarGridSpec(
@@ -583,18 +593,19 @@
 
     packs = steps + turns
     samples = packs + 2 * half
+    keep = steps <= 8
     near_field, *far_sums = pl.pallas_call(
         functools.partial(far_kernel, longer, unroll, chunks, n_x, turns),
         grid_spec=pltpu.PrefetchScalarGridSpec(
             num_scalar_prefetch=3,
             grid=(samples + steps,),
             in_specs=[tab_spec]
-            + charges([0, samples])
+            + charges([0] if keep else [0, samples])
             + [
                 pl.BlockSpec(memory_space=pl.ANY),
                 whole(N, 3 * N),
-                whole(3 * n_y * LANES, N),
-                whole(3 * N, n_y * LANES),
+                whole(3 * N, N),
+                whole(3 * N, N),
                 pl.BlockSpec((at_once, N, N), lambda t, *_: (clamp(t - steps, turns - 1), 0, 0)),
             ],
             out_specs=[
@@ -607,7 +618,7 @@
                 pltpu.VMEM((n_y, size, ROWS, LANES), F32),
                 pltpu.VMEM((half, size, ROWS, N), BF16),
                 sums_scratch,
-                pltpu.VMEM((steps if steps <= 8 else 1, 2 * ROWS, count), F32),
+                pltpu.VMEM((steps if keep else 1, KEPT, count), F32),
                 pltpu.SemaphoreType.DMA((half,)),
             ],
         ),
@@ -621,7 +632,7 @@
         tab,
         *far,
         near_mesh,
-        *tables(n_y, planes_y),
+        *tables(),
         green,
     )
 
@@ -632,9 +643,10 @@
         grid_spec=pltpu.PrefetchScalarGridSpec(
             num_scalar_prefetch=2,
             grid=(steps,),
-            in_specs=[tab_spec]
-            + charges([0])
-            + [kept_spec, pl.BlockSpec((1, size, ROWS, N), lambda t, *_: (t // n_x, 0, 0, 0))],
+            in_specs=[
+                kept_spec,
+                pl.BlockSpec((1, size, ROWS, N), lambda t, *_: (t // n_x, 0, 0, 0)),
+            ],
             out_specs=results(0),
             scratch_shapes=[sums_scratch],
         ),
@@ -642,7 +654,7 @@
         compiler_params=params,
         cost_estimate=estimate(1),
         name="near_sample",
-    )(*near_bounds, tab, *near, near_kept, near_field.reshape(half, size, ROWS, N))
+    )(*near_bounds, near_kept, near_field.reshape(half, size, ROWS, N))
 
     sums = [near_sums[s] + far_sums[s] for s in range(half)]
     for s in range(half - 1, 0, -1):

time: 128 us -> 122 us (0.953)
  Pallas kernels: 75.5 us -> 70.4 us
    pallas_call x1, Pallas kernels: 47.2 us -> 42.3 us  [shards(): pl.pallas_call(functools.partial(far_kernel, longer, unroll, chunks, n_x,...]
  transfers between devices with their start and end apart: 12 -> 12, of which waited for: 4 -> 5; matrix products, arithmetic and copies ran while one was open for 5% -> 6% of each run, Pallas kernels for 22% -> 23%
where the time goes in v5:
time: 122 us; the launch traced here: 121 us
  Pallas kernels  70.4 us (58%)
  other arithmetic  19.6 us (16%)
  starting transfers between devices  14.6 us (12%)
  waiting for transfers between devices  12.5 us (10%)
  local copies, waits for them, and re-layouts  3.38 us (3%)
    pallas_call x1, Pallas kernels, shards(): pl.pallas_call(functools.partial(far_kernel, longer, unroll, chunks, n_x,...  42.3 us
    ppermute x12, starting transfers between devices, exchange(): return lax.ppermute(value, axis, pairs)  14.6 us
    pallas_call x1, Pallas kernels, shards(): pl.pallas_call(functools.partial(near_kernel, longer, chunks, n_x), grid_...  14.3 us
    pallas_call x1, Pallas kernels, shards(): pl.pallas_call(functools.partial(last_kernel, unroll, chunks, n_x), grid_...  13.8 us
    ppermute x12, waiting for transfers between devices, exchange(): return lax.ppermute(value, axis, pairs)  12.5 us
    sort x1, other arithmetic, shards(): lax.sort((cell_x, cell_y, cell_z, fraction[0], fraction[1], fraction[2],...  5.83 us
    sort x1, other arithmetic, shards(): lax.sort((order, total[0], total[1], total[2], total[3]), num_keys=1, is_...  5.62 us
    div x1, other arithmetic, green_of(): jnp.where(total > 0, jnp.exp(-0.5 * total) / safe, F32(0.0))  2.83 us
  transfers between devices with their start and end apart: 12, of which 5 were waited for; matrix products, arithmetic and copies ran while one was open for 6% of the time, Pallas kernels for 23%

profile of v5, /device:TPU:0, one launch (start us, length us, event | category | flops | bytes accessed | tf_op | source)
XLA Modules:
  0.0 121.4 jit_solution(16774685239809105386)
XLA Ops:
  0.6 1.0 fusion.21
  1.7 5.8 %sort.84 = (s32[4096]{0:T(1024)S(1)}, s32[4096]{0:T(1024)S(1)}, s32[4096]{0:T(1024)S(1)}, f32[4096]{0:T(1024)S(1)}, f32[4096]{0:T(1024)S(1)}, /*index=5*/f32[4096]{0:T(1024)S(1)}, f32[4096]{0:T(1024)S(1)}, s32[4096]{0:T(1024)S(1)}) sort(s32[4096]{0:T(1024)} %param.8, s32[4096]{0:T(1024)} %param.9, s32[4096]{0:T(1024)} %param.10, f32[4096]{0:T(1024)S(1)} %bitcast.62, ...), dimensions={0}, to_apply=%region_0.0 | sort | flops 49152 | bytes 262144 | tf_op jit(solution)/shard_map/sort | solution.py:477
  7.6 5.1 %collective-permute-start.2 = (f32[224,128]{1,0:T(8,128)S(1)}, f32[224,128]{1,0:T(8,128)S(1)}, u32[]{:S(2)}, u32[]{:S(2)}) collective-permute-start(f32[224,128]{1,0:T(8,128)S(1)} %constant_dynamic-update-slice_fusion), channel_id=1, source_target_pairs={{0,12},{4,0},{8,4},{12,8},{1,13},{5,1},{9,5},{13,9},{2,14},{6,2},{... | collective-permute-start | bytes 344072 | tf_op jit(solution)/shard_map/ppermute | solution.py:443
  12.7 1.0 collective-permute-start
  14.1 2.8 %fusion.1.refs_6_ = f32[16,256,256]{2,1,0:T(8,128)} fusion(f32[256]{0:T(256)S(1)} %multiply_multiply_fusion, f32[16,256]{1,0:T(8,128)S(1)} %broadcast_add_fusion), kind=kLoop, calls=%fused_computation.5 | loop fusion | flops 7340032 | bytes 4211712 | tf_op jit(solution)/shard_map/div | solution.py:435
  17.7 0.7 broadcast_select_fusion.tab_ref
  18.4 4.2 %collective-permute-done.1 = f32[224,128]{1,0:T(8,128)S(1)} collective-permute-done((f32[224,128]{1,0:T(8,128)S(1)}, f32[224,128]{1,0:T(8,128)S(1)}, u32[]{:S(2)}, u32[]{:S(2)}) %collective-permute-start.1) | collective-permute-done | bytes 114720 | tf_op jit(solution)/shard_map/ppermute | solution.py:443
  23.4 1.6 %collective-permute-start.4 = (f32[4,224,128]{2,1,0:T(8,128)S(1)}, f32[4,224,128]{2,1,0:T(8,128)S(1)}, u32[]{:S(2)}, u32[]{:S(2)}) collective-permute-start(f32[4,224,128]{2,1,0:T(8,128)S(1)} %gather_fusion), channel_id=1, source_target_pairs={{0,2},{1,3},{2,0},{3,1},{4,6},{5,7},{6,4},{7,5},{8,10},{9,11},{10,... | collective-permute-start | bytes 1376264 | tf_op jit(solution)/shard_map/ppermute | solution.py:443
  25.8 0.6 and_select_fusion.1.pass_ref
  26.4 14.3 %near_spread.1 = (f32[2,272,16,128]{3,2,1,0:T(8,128)}, f32[8,40,4096]{2,1,0:T(8,128)}) custom-call(s32[256]{0:T(256)} %copy-done.4, s32[256]{0:T(256)} %and_select_fusion.1.pass_ref, f32[9,16,128]{2,1,0:T(8,128)} %broadcast_select_fusion.tab_ref, f32[4,224,128]{2,1,0:T(8,128)} %copy-done, f32[4,224,128]{2,1,0:T(8,128)} %copy-done.3), custom_call_target="tpu_custom_call" | custom-call | flops 19660800000 | bytes 5242880 | tf_op jit(solution)/shard_map/near_spread/pallas_call | solution.py:570
  40.9 1.7 %collective-permute-done.5.refs_1_ = f32[4,224,128]{2,1,0:T(8,128)S(1)} collective-permute-done((f32[4,224,128]{2,1,0:T(8,128)S(1)}, f32[4,224,128]{2,1,0:T(8,128)S(1)}, u32[]{:S(2)}, u32[]{:S(2)}) %collective-permute-start.5) | collective-permute-done | bytes 458784 | tf_op jit(solution)/shard_map/ppermute | solution.py:443
  43.2 0.6 and_select_fusion.pass_ref
  43.8 42.3 %far_spread_filter_sample.1 = (bf16[2,4352,256]{2,1,0:T(8,128)(2,1)}, f32[4,4,4096]{2,1,0:T(4,128)}, f32[4,4,4096]{2,1,0:T(4,128)}) custom-call(s32[256]{0:T(256)} %copy-done.5, s32[256]{0:T(256)} %and_select_fusion.pass_ref, s32[1]{0:T(128)} %bitcast.15.at_ref, f32[9,16,128]{2,1,0:T(8,128)} %broadcast_select_fusion.tab_ref, f32[4,224,128]{2,1,0:T(8,128)} %copy-done.1, ...), custom_call_target="tpu_custom_call" | custom-call | flops 58982400000 | bytes 15728640 | tf_op jit(solution)/shard_map/far_spread_filter_sample/pallas_call | solution.py:597
  86.1 1.6 %collective-permute-start.7 = (f32[4,4,4096]{2,1,0:T(4,128)}, f32[4,4,4096]{2,1,0:T(4,128)S(1)}, u32[]{:S(2)}, u32[]{:S(2)}) collective-permute-start(f32[4,4,4096]{2,1,0:T(4,128)} %get-tuple-element.51), channel_id=1, source_target_pairs={{0,2},{1,3},{2,0},{3,1},{4,6},{5,7},{6,4},{7,5},{8,10},{9,11},{10,... | collective-permute-start | bytes 786440 | tf_op jit(solution)/shard_map/ppermute | solution.py:443
  88.2 13.8 %near_sample.1 = (f32[4,4,4096]{2,1,0:T(4,128)}, f32[4,4,4096]{2,1,0:T(4,128)}) custom-call(s32[256]{0:T(256)} %copy-done.4, s32[256]{0:T(256)} %and_select_fusion.1.pass_ref, f32[8,40,4096]{2,1,0:T(8,128)} %get-tuple-element.39.kept, bf16[2,272,16,256]{3,2,1,0:T(8,128)(2,1)} %bitcast.67), custom_call_target="tpu_custom_call" | custom-call | flops 19660800000 | bytes 5242880 | tf_op jit(solution)/shard_map/near_sample/pallas_call | solution.py:641
  102.0 1.0 add.207
  103.1 1.5 %collective-permute-done.8 = f32[4,4,4096]{2,1,0:T(4,128)S(1)} collective-permute-done((f32[4,4,4096]{2,1,0:T(4,128)S(1)}, f32[4,4,4096]{2,1,0:T(4,128)S(1)}, u32[]{:S(2)}, u32[]{:S(2)}) %collective-permute-start.8) | collective-permute-done | bytes 262176 | tf_op jit(solution)/shard_map/ppermute | solution.py:443
  104.6 1.0 add_add_fusion
  105.6 1.8 %collective-permute-start.11 = (f32[4,4096]{1,0:T(4,128)S(1)}, f32[4,4096]{1,0:T(4,128)S(1)}, u32[]{:S(2)}, u32[]{:S(2)}) collective-permute-start(f32[4,4096]{1,0:T(4,128)S(1)} %get-tuple-element.61), channel_id=1, source_target_pairs={{0,12},{4,0},{8,4},{12,8},{1,13},{5,1},{9,5},{13,9},{2,14},{6,2},{... | collective-permute-start | bytes 196616 | tf_op jit(solution)/shard_map/ppermute | solution.py:443
  107.5 0.8 collective-permute-start.10
  108.2 1.9 %collective-permute-start.9 = (f32[4,4096]{1,0:T(4,128)S(1)}, f32[4,4096]{1,0:T(4,128)S(1)}, u32[]{:S(2)}, u32[]{:S(2)}) collective-permute-start(f32[4,4096]{1,0:T(4,128)S(1)} %get-tuple-element.60), channel_id=1, source_target_pairs={{0,4},{4,8},{8,12},{12,0},{1,5},{5,9},{9,13},{13,1},{2,6},{6,10},{... | collective-permute-start | bytes 196616 | tf_op jit(solution)/shard_map/ppermute | solution.py:443
  110.2 4.8 %collective-permute-done.10 = f32[4,4096]{1,0:T(4,128)S(1)} collective-permute-done((f32[4,4096]{1,0:T(4,128)S(1)}, f32[4,4096]{1,0:T(4,128)S(1)}, u32[]{:S(2)}, u32[]{:S(2)}) %collective-permute-start.10) | collective-permute-done | bytes 65568 | tf_op jit(solution)/shard_map/ppermute | solution.py:443
  115.1 5.6 %sort.85 = (s32[4096]{0:T(1024)}, f32[4096]{0:T(1024)}, f32[4096]{0:T(1024)S(1)}, f32[4096]{0:T(1024)S(1)}, f32[4096]{0:T(1024)S(1)}) sort(s32[4096]{0:T(1024)S(1)} %get-tuple-element.29, f32[4096]{0:T(1024)S(1)} %bitcast.60, f32[4096]{0:T(1024)S(1)} %bitcast.59, f32[4096]{0:T(1024)S(1)} %bitcast.58, f32[4096]{0:T(1024)S(1)} %bitcast.57), dimensions={0}, to_apply=%region_1.2 | sort | flops 49152 | bytes 163840 | tf_op jit(solution)/shard_map/sort | solution.py:664
  120.7 0.7 maximum_negate_fusion
  (70 shorter events, 4.2 us)
Async XLA Ops:
  7.6 10.8 %collective-permute-start.2 = (f32[224,128]{1,0:T(8,128)S(1)}, f32[224,128]{1,0:T(8,128)S(1)}, u32[]{:S(2)}, u32[]{:S(2)}) collective-permute-start(f32[224,128]{1,0:T(8,128)S(1)} %constant_dynamic-update-slice_fusion), channel_id=1, source_target_pairs={{0,12},{4,0},{8,4},{12,8},{1,13},{5,1},{9,5},{13,9},{2,14},{6,2},{... | collective-permute-start | bytes 344072 | tf_op jit(solution)/shard_map/ppermute | solution.py:443
  12.7 10.0 %collective-permute-start.1 = (f32[224,128]{1,0:T(8,128)S(1)}, f32[224,128]{1,0:T(8,128)S(1)}, u32[]{:S(2)}, u32[]{:S(2)}) collective-permute-start(f32[224,128]{1,0:T(8,128)S(1)} %constant_dynamic-update-slice_fusion), channel_id=1, source_target_pairs={{0,8},{4,12},{8,0},{12,4},{1,9},{5,13},{9,1},{13,5},{2,10},{6,14},... | collective-permute-start | bytes 344072 | tf_op jit(solution)/shard_map/ppermute | solution.py:443
  12.7 10.0 %collective-permute-start = (f32[224,128]{1,0:T(8,128)S(1)}, f32[224,128]{1,0:T(8,128)S(1)}, u32[]{:S(2)}, u32[]{:S(2)}) collective-permute-start(f32[224,128]{1,0:T(8,128)S(1)} %constant_dynamic-update-slice_fusion), channel_id=1, source_target_pairs={{0,4},{4,8},{8,12},{12,0},{1,5},{5,9},{9,13},{13,1},{2,6},{6,10},{... | collective-permute-start | bytes 344072 | tf_op jit(solution)/shard_map/ppermute | solution.py:443
  23.3 3.1 %copy-start = (f32[4,224,128]{2,1,0:T(8,128)}, f32[4,224,128]{2,1,0:T(8,128)S(1)}, u32[]{:S(2)}) copy-start(f32[4,224,128]{2,1,0:T(8,128)S(1)} %gather_fusion) | copy-start | bytes 1376260
  23.3 1.9 %collective-permute-start.3 = (f32[4,224,128]{2,1,0:T(8,128)S(1)}, f32[4,224,128]{2,1,0:T(8,128)S(1)}, u32[]{:S(2)}, u32[]{:S(2)}) collective-permute-start(f32[4,224,128]{2,1,0:T(8,128)S(1)} %gather_fusion), channel_id=1, source_target_pairs={{0,1},{1,0},{2,3},{3,2},{4,5},{5,4},{6,7},{7,6},{8,9},{9,8},{10,11... | collective-permute-start | bytes 1376264 | tf_op jit(solution)/shard_map/ppermute | solution.py:443
  23.4 17.3 %collective-permute-start.4 = (f32[4,224,128]{2,1,0:T(8,128)S(1)}, f32[4,224,128]{2,1,0:T(8,128)S(1)}, u32[]{:S(2)}, u32[]{:S(2)}) collective-permute-start(f32[4,224,128]{2,1,0:T(8,128)S(1)} %gather_fusion), channel_id=1, source_target_pairs={{0,2},{1,3},{2,0},{3,1},{4,6},{5,7},{6,4},{7,5},{8,10},{9,11},{10,... | collective-permute-start | bytes 1376264 | tf_op jit(solution)/shard_map/ppermute | solution.py:443
  25.2 1.2 %copy-start.3 = (f32[4,224,128]{2,1,0:T(8,128)}, f32[4,224,128]{2,1,0:T(8,128)S(1)}, u32[]{:S(2)}) copy-start(f32[4,224,128]{2,1,0:T(8,128)S(1)} %collective-permute-done.3.refs_1_) | copy-start | bytes 1376260
  25.7 0.7 copy-start.4
  40.7 3.1 %copy-start.1 = (f32[4,224,128]{2,1,0:T(8,128)}, f32[4,224,128]{2,1,0:T(8,128)S(1)}, u32[]{:S(2)}) copy-start(f32[4,224,128]{2,1,0:T(8,128)S(1)} %collective-permute-done.4.refs_0_) | copy-start | bytes 1376260
  40.7 1.9 %collective-permute-start.5 = (f32[4,224,128]{2,1,0:T(8,128)S(1)}, f32[4,224,128]{2,1,0:T(8,128)S(1)}, u32[]{:S(2)}, u32[]{:S(2)}) collective-permute-start(f32[4,224,128]{2,1,0:T(8,128)S(1)} %collective-permute-done.4.refs_0_), channel_id=1, source_target_pairs={{0,1},{1,0},{2,3},{3,2},{4,5},{5,4},{6,7},{7,6},{8,9},{9,8},{10,11... | collective-permute-start | bytes 1376264 | tf_op jit(solution)/shard_map/ppermute | solution.py:443
  42.6 1.2 %copy-start.2 = (f32[4,224,128]{2,1,0:T(8,128)}, f32[4,224,128]{2,1,0:T(8,128)S(1)}, u32[]{:S(2)}) copy-start(f32[4,224,128]{2,1,0:T(8,128)S(1)} %collective-permute-done.5.refs_1_) | copy-start | bytes 1376260
  43.1 0.7 copy-start.5
  86.1 15.9 %collective-permute-start.7 = (f32[4,4,4096]{2,1,0:T(4,128)}, f32[4,4,4096]{2,1,0:T(4,128)S(1)}, u32[]{:S(2)}, u32[]{:S(2)}) collective-permute-start(f32[4,4,4096]{2,1,0:T(4,128)} %get-tuple-element.51), channel_id=1, source_target_pairs={{0,2},{1,3},{2,0},{3,1},{4,6},{5,7},{6,4},{7,5},{8,10},{9,11},{10,... | collective-permute-start | bytes 786440 | tf_op jit(solution)/shard_map/ppermute | solution.py:443
  87.7 15.4 %collective-permute-start.6 = (f32[4,4,4096]{2,1,0:T(4,128)}, f32[4,4,4096]{2,1,0:T(4,128)S(1)}, u32[]{:S(2)}, u32[]{:S(2)}) collective-permute-start(f32[4,4,4096]{2,1,0:T(4,128)} %get-tuple-element.49), channel_id=1, source_target_pairs={{0,2},{1,3},{2,0},{3,1},{4,6},{5,7},{6,4},{7,5},{8,10},{9,11},{10,... | collective-permute-start | bytes 786440 | tf_op jit(solution)/shard_map/ppermute | solution.py:443
  103.0 1.6 %collective-permute-start.8 = (f32[4,4,4096]{2,1,0:T(4,128)S(1)}, f32[4,4,4096]{2,1,0:T(4,128)S(1)}, u32[]{:S(2)}, u32[]{:S(2)}) collective-permute-start(f32[4,4,4096]{2,1,0:T(4,128)S(1)} %add.207), channel_id=1, source_target_pairs={{0,1},{1,0},{2,3},{3,2},{4,5},{5,4},{6,7},{7,6},{8,9},{9,8},{10,11... | collective-permute-start | bytes 786440 | tf_op jit(solution)/shard_map/ppermute | solution.py:443
  105.6 4.6 %collective-permute-start.11 = (f32[4,4096]{1,0:T(4,128)S(1)}, f32[4,4096]{1,0:T(4,128)S(1)}, u32[]{:S(2)}, u32[]{:S(2)}) collective-permute-start(f32[4,4096]{1,0:T(4,128)S(1)} %get-tuple-element.61), channel_id=1, source_target_pairs={{0,12},{4,0},{8,4},{12,8},{1,13},{5,1},{9,5},{13,9},{2,14},{6,2},{... | collective-permute-start | bytes 196616 | tf_op jit(solution)/shard_map/ppermute | solution.py:443
  107.5 7.6 %collective-permute-start.10 = (f32[4,4096]{1,0:T(4,128)S(1)}, f32[4,4096]{1,0:T(4,128)S(1)}, u32[]{:S(2)}, u32[]{:S(2)}) collective-permute-start(f32[4,4096]{1,0:T(4,128)S(1)} %get-tuple-element.62), channel_id=1, source_target_pairs={{0,8},{4,12},{8,0},{12,4},{1,9},{5,13},{9,1},{13,5},{2,10},{6,14},... | collective-permute-start | bytes 196616 | tf_op jit(solution)/shard_map/ppermute | solution.py:443
  108.2 6.8 %collective-permute-start.9 = (f32[4,4096]{1,0:T(4,128)S(1)}, f32[4,4096]{1,0:T(4,128)S(1)}, u32[]{:S(2)}, u32[]{:S(2)}) collective-permute-start(f32[4,4096]{1,0:T(4,128)S(1)} %get-tuple-element.60), channel_id=1, source_target_pairs={{0,4},{4,8},{8,12},{12,0},{1,5},{5,9},{9,13},{13,1},{2,6},{6,10},{... | collective-permute-start | bytes 196616 | tf_op jit(solution)/shard_map/ppermute | solution.py:443

commit v6 on v5

--- a/solution.py
+++ b/solution.py
@@ -127,13 +127,13 @@
     return load
 
 
-def rounds(unroll, chunks, begin, base_ref, pass_ref, prepare, finish):
+def rounds(unroll, chunks, step, base_ref, last_ref, prepare, finish):
     def some(i, most):
         waiting = []
         for u in range(unroll):
-            index = begin + i * unroll + u
-            most = jnp.maximum(most, pass_ref[index])
-            chunk, start = i * unroll + u, base_ref[index]
+            chunk = i * unroll + u
+            start = base_ref[step, chunk]
+            most = jnp.maximum(most, last_ref[step, chunk] - start)
             waiting.append((chunk, start, prepare(chunk, start, False)))
             if len(waiting) > AHEAD:
                 finish(*waiting.pop(0), False)
@@ -141,17 +141,18 @@
             finish(*item, False)
         return most
 
-    most = lax.fori_loop(0, chunks // unroll, some, jnp.int32(1))
-
-    @pl.when(most > 1)
+    most = lax.fori_loop(0, chunks // unroll, some, jnp.int32(0))
+
+    @pl.when(most + 4 > PLANES)
     def _():
         def one(u, carry):
             def more(p, carry):
-                start = base_ref[begin + u] + p * PLANES
+                start = base_ref[step, u] + p * PLANES
                 finish(u, start, prepare(u, start, True), True)
                 return carry
 
-            return lax.fori_loop(1, pass_ref[begin + u], more, carry)
+            span = last_ref[step, u] - base_ref[step, u] + 4
+            return lax.fori_loop(1, (span + PLANES - 1) // PLANES, more, carry)
 
         lax.fori_loop(0, chunks, one, 0)
 
@@ -166,7 +167,7 @@
     return z, slope_along_z(tab, plus, minus, middle, square) * charge
 
 
-def spread(unroll, chunks, step, base_ref, pass_ref, tab_ref, load, out_ref, kept):
+def spread(unroll, chunks, step, base_ref, last_ref, tab_ref, load, out_ref, kept):
     tab = [tab_ref[m] for m in range(TABLES)]
     cubic = coefficients(SPLINE)
     empty = jnp.zeros((LANES - LINES, LANES), BF16)
@@ -189,7 +190,7 @@
     def finish(chunk, start, total, again):
         out_ref[pl.ds(start, PLANES)] += total.reshape(PLANES, ROWS, LANES)
 
-    rounds(unroll, chunks, step * chunks, base_ref, pass_ref, prepare, finish)
+    rounds(unroll, chunks, step, base_ref, last_ref, prepare, finish)
 
 
 def add_rows(terms):
@@ -203,7 +204,7 @@
     return jnp.concatenate([r[i : i + 1] for i in (0, 2, 4, 6)], axis=0)
 
 
-def sample(unroll, chunks, step, base_ref, pass_ref, tab_ref, load, field_ref, out_ref, kept):
+def sample(unroll, chunks, step, base_ref, last_ref, tab_ref, load, field_ref, out_ref, kept):
     tab = None if tab_ref is None else [tab_ref[m] for m in range(TABLES)]
     cubic, quadratic = coefficients(SPLINE), coefficients(SLOPES)
 
@@ -240,7 +241,7 @@
             total += out_ref[:, place]
         out_ref[:, place] = total
 
-    rounds(unroll, chunks, step * chunks, base_ref, pass_ref, prepare, finish)
+    rounds(unroll, chunks, step, base_ref, last_ref, prepare, finish)
 
 
 MORE = LANES - LINES
@@ -283,7 +284,7 @@
             out_ref[0] = sums[...]
 
 
-def near_kernel(unroll, chunks, n_x, base_ref, pass_ref, tab_ref, *refs):
+def near_kernel(unroll, chunks, n_x, base_ref, last_ref, tab_ref, *refs):
     in_refs, out_ref, kept = refs[:-2], refs[-2], refs[-1]
     step = pl.program_id(0)
 
@@ -292,18 +293,18 @@
         out_ref[...] = jnp.zeros_like(out_ref)
 
     load = loader(in_refs, step, n_x)
-    spread(unroll, chunks, step, base_ref, pass_ref, tab_ref, load, out_ref.at[0], kept.at[0])
+    spread(unroll, chunks, step, base_ref, last_ref, tab_ref, load, out_ref.at[0], kept.at[0])
 
     @pl.when(step % n_x == n_x - 1)
     def _():
         wrap(out_ref.at[0])
 
 
-def far_kernel(longer, unroll, chunks, n_x, turns, base_ref, pass_ref, at_ref, tab_ref, *refs):
-    groups = (len(refs) - 11) // 2
+def far_kernel(longer, unroll, chunks, n_x, at_once, turns, base_ref, last_ref, at_ref, tab_ref, *refs):
+    groups = (len(refs) - 12) // 2
     in_refs = refs[:groups]
-    near_ref, table_ref, lines_ref, back_ref, green_ref = refs[groups : groups + 5]
-    field_ref, out_refs = refs[groups + 5], refs[groups + 6 : -5]
+    near_ref, table_ref, lines_ref, back_ref, flat_ref, own_ref = refs[groups : groups + 6]
+    field_ref, out_refs = refs[groups + 6], refs[groups + 7 : -5]
     mesh, far_field, sums, kept, arrived = refs[-5:]
     keep = kept.shape[0] == groups * n_x
     step = pl.program_id(0)
@@ -327,7 +328,7 @@
         load = loader(in_refs, step, n_x)
         to = mesh.at[at_ref[0] ^ (groups + step // n_x)]
         at_kept = kept.at[step] if keep else None
-        spread(longer, chunks, step, base_ref, pass_ref, tab_ref, load, to, at_kept)
+        spread(longer, chunks, step, base_ref, last_ref, tab_ref, load, to, at_kept)
 
     @pl.when(step == spreads)
     def _():
@@ -350,6 +351,11 @@
             return jnp.dot(table_ref[...], both, preferred_element_type=F32)
 
         first_half = lax.broadcasted_iota(jnp.int32, (N, LANES), 1) < LANES // 2
+
+        def green(k):
+            total = flat_ref[0] + own_ref[0, pl.ds(k, 1), :]
+            rest = flat_ref[1] * own_ref[1, pl.ds(k, 1), :]
+            return jnp.where(total > 0, rest / jnp.where(total > 0, total, F32(1)), F32(0))
 
         def lines_of(own, t):
             before, here, after = [
@@ -357,12 +363,11 @@
             ]
             return here + pltpu.roll(jnp.where(first_half, after, before), LANES // 2, 1)
 
-        at_once = green_ref.shape[0]
-        begin = ROWS + (step - spreads) * at_once
-        owns = [pl.ds(begin + u, N, ROWS) for u in range(at_once)]
+        begin = (step - spreads) * at_once
+        owns = [pl.ds(ROWS + begin + u, N, ROWS) for u in range(at_once)]
         values = [lanes([lines_of(own, t) for t in range(groups)]) for own in owns]
         values = [right(v, lines_ref) for v in values]
-        values = [left(v) * green_ref[u] for u, v in enumerate(values)]
+        values = [left(v) * green(begin + u) for u, v in enumerate(values)]
         values = [left(v) for v in values]
         values = [right(v, back_ref) for v in values]
         for own, value in zip(owns, values):
@@ -388,15 +393,45 @@
         load = loader(in_refs, now, n_x)
         at_field = far_field.at[now // n_x]
         at_kept = kept.at[now] if keep else None
-        sample(unroll, chunks, now, base_ref, pass_ref, tab_ref, load, at_field, sums, at_kept)
+        sample(unroll, chunks, now, base_ref, last_ref, tab_ref, load, at_field, sums, at_kept)
         deliver(now, n_x, sums, out_refs)
 
 
-def last_kernel(unroll, chunks, n_x, base_ref, pass_ref, kept, field_ref, *refs):
+def last_kernel(unroll, chunks, n_x, base_ref, last_ref, kept, field_ref, *refs):
     out_refs, sums = refs[:-1], refs[-1]
     step = pl.program_id(0)
-    sample(unroll, chunks, step, base_ref, pass_ref, None, None, field_ref.at[0], sums, kept.at[0])
+    sample(unroll, chunks, step, base_ref, last_ref, None, None, field_ref.at[0], sums, kept.at[0])
     deliver(step, n_x, sums, out_refs)
+
+
+def order_kernel(rank_ref, *refs):
+    parts, (value_ref, force_ref, source) = refs[:-3], refs[-3:]
+    chunks = rank_ref.shape[0]
+    half = chunks // 2
+    for t in range(half):
+        pair = [sum(p[:, place * LANES : (place + 1) * LANES] for p in parts) for place in (t, t + half)]
+        source[t] = jnp.concatenate(pair, axis=0)
+
+    def one(o):
+        rank = wide(rank_ref[pl.ds(o, 1), :], 8)
+        lane, tile = rank & (LANES - 1), rank // LANES
+        upper = tile >= half
+        tile = jnp.where(upper, tile - half, tile)
+        found = jnp.zeros((8, LANES), F32)
+        for t in range(half):
+            found = jnp.where(tile == t, jnp.take_along_axis(source[t], lane, axis=1), found)
+        result = jnp.where(upper[:4], found[4:], found[:4])
+        value_ref[pl.ds(o, 1), :] = result[:1]
+        force_ref[:, place_of(o)] = -result[1:]
+
+    at_once = 4 if chunks % 4 == 0 else 1
+
+    def some(i, carry):
+        for u in range(at_once):
+            one(i * at_once + u)
+        return carry
+
+    lax.fori_loop(0, chunks // at_once, some, 0)
 
 
 def tables():
@@ -417,24 +452,15 @@
     high, low = halves(table(line, full))
     lines = np.concatenate([high, high, low], axis=0)
     high, low = halves(table(full, line))
-    return left, lines, np.concatenate([high, high, low], axis=0)
+    symbols = (2 * np.sin(np.pi * full / N)) ** 2
+    total = symbols[:, None] + symbols[None, :]
+    shares = np.stack([total, np.exp(-0.5 * total) / float(N * N * N)]).astype(np.float32)
+    return left, lines, np.concatenate([high, high, low], axis=0), shares
 
 
 def symbol(index, size):
     sines = 2.0 * jnp.sin(jnp.pi * index.astype(F32) / size)
     return sines * sines
-
-
-def green_of(freq_a, freq_b, freq_c, grid_size):
-    total = (
-        symbol(freq_a, grid_size)[:, None, None]
-        + symbol(freq_b, grid_size)[None, :, None]
-        + symbol(freq_c, grid_size)[None, None, :]
-    )
-    safe = jnp.where(total > 0, total, F32(1.0))
-    return jnp.where(total > 0, jnp.exp(-0.5 * total) / safe, F32(0.0)) / float(
-        grid_size * grid_size * grid_size
-    )
 
 
 def exchange(value, axis, distance, flip):
@@ -455,13 +481,13 @@
 def scatter_x(value):
     size = lax.axis_size("gx")
     if size > 8:
-        return jnp.sum(lax.all_to_all(value, "gx", split_axis=0, concat_axis=0, tiled=True), axis=0)
+        return [jnp.sum(lax.all_to_all(value, "gx", split_axis=0, concat_axis=0, tiled=True), axis=0)]
     me = lax.axis_index("gx")
-    total = lax.dynamic_index_in_dim(value, me, 0, keepdims=False)
+    parts = [lax.dynamic_index_in_dim(value, me, 0, keepdims=False)]
     for s in range(1, size):
         part = lax.dynamic_index_in_dim(value, (me + s) % size, 0, keepdims=False)
-        total = total + exchange(part, "gx", s, False)
-    return total
+        parts.append(exchange(part, "gx", s, False))
+    return parts
 
 
 def shards(cell_x, cell_y, cell_z, fraction, charge):
@@ -502,11 +528,15 @@
     turn_cos, turn_sin = jnp.cos(turns), jnp.sin(turns)
     tab = jnp.stack([turn_cos + turn_sin] + tab[:6] + [turn_cos - turn_sin] + tab[6:])
     tab = jnp.where((jnp.arange(ROWS) < own)[None, :, None], tab, F32(0.0))
-    full = jnp.arange(N, dtype=jnp.int32)
-    green = green_of(freq[:own], full, full, N)
+    along_own = symbol(freq, N)
+    own_share = jnp.stack([along_own, jnp.exp(-0.5 * along_own)])
+    own_share = jnp.broadcast_to(own_share[:, :, None], (2, ROWS, N))
 
     half = n_y // 2
-    arrived, green, tab = lax.optimization_barrier((gather_x(packed), green, tab))
+    _, rank = lax.sort((order, place), num_keys=1, is_stable=False)
+    rank = rank.reshape(chunks, LANES)
+    ready = (gather_x(packed), own_share, tab, rank)
+    arrived, own_share, tab, rank = lax.optimization_barrier(ready)
     groups = [arrived]
     for s in range(1, half + 1):
         step = s & -s
@@ -522,8 +552,7 @@
 
     def bounds(some):
         planes = jnp.concatenate([g[:, :chunks] for g in some]).astype(jnp.int32)
-        first, last = planes[:, :, 0].reshape(-1), planes[:, :, -1].reshape(-1)
-        return first, (last - first + (3 + PLANES)) // PLANES
+        return planes[:, :, 0], planes[:, :, -1]
 
     def clamp(step, top):
         return jnp.minimum(jnp.maximum(step, 0), top)
@@ -595,7 +624,7 @@
     samples = packs + 2 * half
     keep = steps <= 8
     near_field, *far_sums = pl.pallas_call(
-        functools.partial(far_kernel, longer, unroll, chunks, n_x, turns),
+        functools.partial(far_kernel, longer, unroll, chunks, n_x, at_once, turns),
         grid_spec=pltpu.PrefetchScalarGridSpec(
             num_scalar_prefetch=3,
             grid=(samples + steps,),
@@ -606,7 +635,8 @@
                 whole(N, 3 * N),
                 whole(3 * N, N),
                 whole(3 * N, N),
-                pl.BlockSpec((at_once, N, N), lambda t, *_: (clamp(t - steps, turns - 1), 0, 0)),
+                whole(2, N, N),
+                whole(2, ROWS, N),
             ],
             out_specs=[
                 pl.BlockSpec(
@@ -633,7 +663,7 @@
         *far,
         near_mesh,
         *tables(),
-        green,
+        own_share,
     )
 
     *far_sums, near_field = lax.optimization_barrier((*far_sums, near_field))
@@ -660,11 +690,18 @@
     for s in range(half - 1, 0, -1):
         step = s & -s
         sums[s ^ step] = sums[s ^ step] + exchange(sums[s], "gy", step, True)
-    total = scatter_x(sums[0])
-    _, value, grad_x, grad_y, grad_z = lax.sort(
-        (order, total[0], total[1], total[2], total[3]), num_keys=1, is_stable=False
-    )
-    return (value, -jnp.stack([grad_x, grad_y, grad_z], axis=0))
+    parts = scatter_x(sums[0])
+    value, forces = pl.pallas_call(
+        order_kernel,
+        out_shape=[
+            jax.ShapeDtypeStruct((chunks, LANES), F32),
+            jax.ShapeDtypeStruct((3, count), F32),
+        ],
+        scratch_shapes=[pltpu.VMEM((chunks // 2, 8, LANES), F32)],
+        compiler_params=params,
+        name="order",
+    )(rank, *parts)
+    return (value.reshape(count), forces)
 
 
 def solution(mesh):

time: 122 us -> 120 us (0.984)
  other arithmetic: 19.6 us -> 14.7 us
  waiting for transfers between devices: 12.5 us -> 8.53 us
  Pallas kernels: 70.4 us -> 73.5 us
  local copies, waits for them, and re-layouts: 3.38 us -> 6.07 us
    ppermute x12, waiting for transfers between devices: 12.5 us -> 8.53 us  [exchange(): return lax.ppermute(value, axis, pairs)]
    pallas_call x0 -> x1, Pallas kernels: none -> 2.95 us  [shards(): pl.pallas_call(order_kernel, out_shape=[jax.ShapeDtypeStruct((chunks, LAN...]
    div x1 -> x0, other arithmetic: 2.83 us -> none  [green_of(): jnp.where(total > 0, jnp.exp(-0.5 * total) / safe, F32(0.0))]
  transfers between devices with their start and end apart: 12 -> 12, of which waited for: 5 -> 6; matrix products, arithmetic and copies ran while one was open for 6% -> 8% of each run, Pallas kernels for 23% -> 24%
where the time goes in v6:
time: 120 us; the launch traced here: 119 us
  Pallas kernels  73.5 us (61%)
  starting transfers between devices  15.4 us (13%)
  other arithmetic  14.7 us (12%)
  waiting for transfers between devices  8.53 us (7%)
  local copies, waits for them, and re-layouts  6.07 us (5%)
    pallas_call x1, Pallas kernels, shards(): pl.pallas_call(functools.partial(far_kernel, longer, unroll, chunks, n_x,...  42.5 us
    ppermute x12, starting transfers between devices, exchange(): return lax.ppermute(value, axis, pairs)  15.4 us
    pallas_call x1, Pallas kernels, shards(): pl.pallas_call(functools.partial(near_kernel, longer, chunks, n_x), grid_...  14.2 us
    pallas_call x1, Pallas kernels, shards(): pl.pallas_call(functools.partial(last_kernel, unroll, chunks, n_x), grid_...  13.8 us
    ppermute x12, waiting for transfers between devices, exchange(): return lax.ppermute(value, axis, pairs)  8.53 us
    sort x1, other arithmetic, shards(): lax.sort((cell_x, cell_y, cell_z, fraction[0], fraction[1], fraction[2],...  5.83 us
    sort x1, other arithmetic, shards(): _, rank = lax.sort((order, place), num_keys=1, is_stable=False)  5.57 us
    pallas_call x1, Pallas kernels, shards(): pl.pallas_call(order_kernel, out_shape=[jax.ShapeDtypeStruct((chunks, LAN...  2.95 us
  transfers between devices with their start and end apart: 12, of which 6 were waited for; matrix products, arithmetic and copies ran while one was open for 8% of the time, Pallas kernels for 24%

profile of v6, /device:TPU:0, one launch (start us, length us, event | category | flops | bytes accessed | tf_op | source)
XLA Modules:
  0.0 119.1 jit_solution(6064868409640665136)
XLA Ops:
  0.6 1.0 fusion.14
  1.7 5.8 %sort.66 = (s32[4096]{0:T(1024)S(1)}, s32[4096]{0:T(1024)S(1)}, s32[4096]{0:T(1024)S(1)}, f32[4096]{0:T(1024)S(1)}, f32[4096]{0:T(1024)S(1)}, /*index=5*/f32[4096]{0:T(1024)S(1)}, f32[4096]{0:T(1024)S(1)}, s32[4096]{0:T(1024)S(1)}) sort(s32[4096]{0:T(1024)} %param.9, s32[4096]{0:T(1024)} %param.10, s32[4096]{0:T(1024)} %param.11, f32[4096]{0:T(1024)S(1)} %bitcast.52, ...), dimensions={0}, to_apply=%region_0.0 | sort | flops 49152 | bytes 262144 | tf_op jit(solution)/shard_map/sort | solution.py:503
  7.6 5.1 %collective-permute-start.2 = (f32[224,128]{1,0:T(8,128)S(1)}, f32[224,128]{1,0:T(8,128)S(1)}, u32[]{:S(2)}, u32[]{:S(2)}) collective-permute-start(f32[224,128]{1,0:T(8,128)S(1)} %constant_dynamic-update-slice_fusion), channel_id=1, source_target_pairs={{0,12},{4,0},{8,4},{12,8},{1,13},{5,1},{9,5},{13,9},{2,14},{6,2},{... | collective-permute-start | bytes 344072 | tf_op jit(solution)/shard_map/ppermute | solution.py:469
  12.7 1.0 collective-permute-start
  14.7 0.7 broadcast_select_fusion.tab_ref
  15.5 5.6 %sort.67 = (s32[4096]{0:T(1024)}, s32[4096]{0:T(1024)}) sort(s32[4096]{0:T(1024)S(1)} %get-tuple-element.36, s32[4096]{0:T(1024)S(1)} %iota.34), dimensions={0}, to_apply=%region_1.2 | sort | flops 49152 | bytes 65536 | tf_op jit(solution)/shard_map/sort | solution.py:536
  21.0 1.6 %collective-permute-done.1 = f32[224,128]{1,0:T(8,128)S(1)} collective-permute-done((f32[224,128]{1,0:T(8,128)S(1)}, f32[224,128]{1,0:T(8,128)S(1)}, u32[]{:S(2)}, u32[]{:S(2)}) %collective-permute-start.1) | collective-permute-done | bytes 114720 | tf_op jit(solution)/shard_map/ppermute | solution.py:469
  23.3 0.8 broadcast_in_dim.12.refs_7_
  24.1 1.6 %collective-permute-start.4 = (f32[4,224,128]{2,1,0:T(8,128)S(1)}, f32[4,224,128]{2,1,0:T(8,128)S(1)}, u32[]{:S(2)}, u32[]{:S(2)}) collective-permute-start(f32[4,224,128]{2,1,0:T(8,128)S(1)} %gather_fusion), channel_id=1, source_target_pairs={{0,2},{1,3},{2,0},{3,1},{4,6},{5,7},{6,4},{7,5},{8,10},{9,11},{10,... | collective-permute-start | bytes 1376264 | tf_op jit(solution)/shard_map/ppermute | solution.py:469
  26.8 14.2 %near_spread.1 = (f32[2,272,16,128]{3,2,1,0:T(8,128)}, f32[8,40,4096]{2,1,0:T(8,128)}) custom-call(s32[8,32]{1,0:T(8,128)} %get-tuple-element.59.base_ref, s32[8,32]{1,0:T(8,128)} %get-tuple-element.58.last_ref, f32[9,16,128]{2,1,0:T(8,128)} %broadcast_select_fusion.tab_ref, f32[4,224,128]{2,1,0:T(8,128)} %copy-done, f32[4,224,128]{2,1,0:T(8,128)} %copy-done.6), custom_call_target="tpu_custom_call" | custom-call | flops 19660800000 | bytes 5242880 | tf_op jit(solution)/shard_map/near_spread/pallas_call | solution.py:599
  41.2 1.7 %collective-permute-done.5.refs_1_ = f32[4,224,128]{2,1,0:T(8,128)S(1)} collective-permute-done((f32[4,224,128]{2,1,0:T(8,128)S(1)}, f32[4,224,128]{2,1,0:T(8,128)S(1)}, u32[]{:S(2)}, u32[]{:S(2)}) %collective-permute-start.5) | collective-permute-done | bytes 458784 | tf_op jit(solution)/shard_map/ppermute | solution.py:469
  43.0 1.0 slice_reduce_fusion
  44.0 42.5 %far_spread_filter_sample.1 = (bf16[2,4352,256]{2,1,0:T(8,128)(2,1)}, f32[4,4,4096]{2,1,0:T(4,128)}, f32[4,4,4096]{2,1,0:T(4,128)}) custom-call(s32[8,32]{1,0:T(8,128)} %get-tuple-element.57.base_ref, s32[8,32]{1,0:T(8,128)} %get-tuple-element.56.last_ref, s32[1]{0:T(128)} %bitcast.18.at_ref, f32[9,16,128]{2,1,0:T(8,128)} %broadcast_select_fusion.tab_ref, ...), custom_call_target="tpu_custom_call" | custom-call | flops 58982400000 | bytes 15728640 | tf_op jit(solution)/shard_map/far_spread_filter_sample/pallas_call | solution.py:626
  86.5 1.5 %collective-permute-start.7 = (f32[4,4,4096]{2,1,0:T(4,128)}, f32[4,4,4096]{2,1,0:T(4,128)S(1)}, u32[]{:S(2)}, u32[]{:S(2)}) collective-permute-start(f32[4,4,4096]{2,1,0:T(4,128)} %get-tuple-element.53), channel_id=1, source_target_pairs={{0,2},{1,3},{2,0},{3,1},{4,6},{5,7},{6,4},{7,5},{8,10},{9,11},{10,... | collective-permute-start | bytes 786440 | tf_op jit(solution)/shard_map/ppermute | solution.py:469
  88.6 13.8 %near_sample.1 = (f32[4,4,4096]{2,1,0:T(4,128)}, f32[4,4,4096]{2,1,0:T(4,128)}) custom-call(s32[8,32]{1,0:T(8,128)} %get-tuple-element.59.base_ref, s32[8,32]{1,0:T(8,128)} %get-tuple-element.58.last_ref, f32[8,40,4096]{2,1,0:T(8,128)} %get-tuple-element.41.kept, bf16[2,272,16,256]{3,2,1,0:T(8,128)(2,1)} %bitcast.56), custom_call_target="tpu_custom_call" | custom-call | flops 19660800000 | bytes 5242880 | tf_op jit(solution)/shard_map/near_sample/pallas_call | solution.py:671
  102.4 1.0 add.164
  103.6 1.5 %collective-permute-done.8 = f32[4,4,4096]{2,1,0:T(4,128)S(1)} collective-permute-done((f32[4,4,4096]{2,1,0:T(4,128)S(1)}, f32[4,4,4096]{2,1,0:T(4,128)S(1)}, u32[]{:S(2)}, u32[]{:S(2)}) %collective-permute-start.8) | collective-permute-done | bytes 262176 | tf_op jit(solution)/shard_map/ppermute | solution.py:469
  105.0 1.0 add_add_fusion
  106.7 0.9 collective-permute-start.9
  107.6 1.6 %collective-permute-start.10 = (f32[4,4096]{1,0:T(4,128)S(1)}, f32[4,4096]{1,0:T(4,128)S(1)}, u32[]{:S(2)}, u32[]{:S(2)}) collective-permute-start(f32[4,4096]{1,0:T(4,128)S(1)} %get-tuple-element.61), channel_id=1, source_target_pairs={{0,8},{4,12},{8,0},{12,4},{1,9},{5,13},{9,1},{13,5},{2,10},{6,14},... | collective-permute-start | bytes 196616 | tf_op jit(solution)/shard_map/ppermute | solution.py:469
  109.1 2.9 %collective-permute-start.11 = (f32[4,4096]{1,0:T(4,128)S(1)}, f32[4,4096]{1,0:T(4,128)S(1)}, u32[]{:S(2)}, u32[]{:S(2)}) collective-permute-start(f32[4,4096]{1,0:T(4,128)S(1)} %get-tuple-element.60), channel_id=1, source_target_pairs={{0,12},{4,0},{8,4},{12,8},{1,13},{5,1},{9,5},{13,9},{2,14},{6,2},{... | collective-permute-start | bytes 196616 | tf_op jit(solution)/shard_map/ppermute | solution.py:469
  112.0 1.0 collective-permute-done.9.refs_1_
  113.1 2.4 %collective-permute-done.10.refs_2_ = f32[4,4096]{1,0:T(4,128)S(1)} collective-permute-done((f32[4,4096]{1,0:T(4,128)S(1)}, f32[4,4096]{1,0:T(4,128)S(1)}, u32[]{:S(2)}, u32[]{:S(2)}) %collective-permute-start.10) | collective-permute-done | bytes 65568 | tf_op jit(solution)/shard_map/ppermute | solution.py:469
  116.2 2.9 %order.1 = (f32[32,128]{1,0:T(8,128)}, f32[3,4096]{1,0:T(4,128)}) custom-call(s32[32,128]{1,0:T(8,128)} %bitcast.54, f32[4,4096]{1,0:T(4,128)} %get-tuple-element.63.refs_0_, f32[4,4096]{1,0:T(4,128)} %copy-done.1, f32[4,4096]{1,0:T(4,128)} %copy-done.2, f32[4,4096]{1,0:T(4,128)} %copy-done.3), custom_call_target="tpu_custom_call" | custom-call | tf_op jit(solution)/shard_map/order/pallas_call | solution.py:694
  (66 shorter events, 5.0 us)
Async XLA Ops:
  7.6 13.5 %collective-permute-start.2 = (f32[224,128]{1,0:T(8,128)S(1)}, f32[224,128]{1,0:T(8,128)S(1)}, u32[]{:S(2)}, u32[]{:S(2)}) collective-permute-start(f32[224,128]{1,0:T(8,128)S(1)} %constant_dynamic-update-slice_fusion), channel_id=1, source_target_pairs={{0,12},{4,0},{8,4},{12,8},{1,13},{5,1},{9,5},{13,9},{2,14},{6,2},{... | collective-permute-start | bytes 344072 | tf_op jit(solution)/shard_map/ppermute | solution.py:469
  12.7 10.0 %collective-permute-start.1 = (f32[224,128]{1,0:T(8,128)S(1)}, f32[224,128]{1,0:T(8,128)S(1)}, u32[]{:S(2)}, u32[]{:S(2)}) collective-permute-start(f32[224,128]{1,0:T(8,128)S(1)} %constant_dynamic-update-slice_fusion), channel_id=1, source_target_pairs={{0,8},{4,12},{8,0},{12,4},{1,9},{5,13},{9,1},{13,5},{2,10},{6,14},... | collective-permute-start | bytes 344072 | tf_op jit(solution)/shard_map/ppermute | solution.py:469
  12.7 10.0 %collective-permute-start = (f32[224,128]{1,0:T(8,128)S(1)}, f32[224,128]{1,0:T(8,128)S(1)}, u32[]{:S(2)}, u32[]{:S(2)}) collective-permute-start(f32[224,128]{1,0:T(8,128)S(1)} %constant_dynamic-update-slice_fusion), channel_id=1, source_target_pairs={{0,4},{4,8},{8,12},{12,0},{1,5},{5,9},{9,13},{13,1},{2,6},{6,10},{... | collective-permute-start | bytes 344072 | tf_op jit(solution)/shard_map/ppermute | solution.py:469
  23.3 3.5 %copy-start = (f32[4,224,128]{2,1,0:T(8,128)}, f32[4,224,128]{2,1,0:T(8,128)S(1)}, u32[]{:S(2)}) copy-start(f32[4,224,128]{2,1,0:T(8,128)S(1)} %gather_fusion) | copy-start | bytes 1376260
  24.0 1.8 %collective-permute-start.3 = (f32[4,224,128]{2,1,0:T(8,128)S(1)}, f32[4,224,128]{2,1,0:T(8,128)S(1)}, u32[]{:S(2)}, u32[]{:S(2)}) collective-permute-start(f32[4,224,128]{2,1,0:T(8,128)S(1)} %gather_fusion), channel_id=1, source_target_pairs={{0,1},{1,0},{2,3},{3,2},{4,5},{5,4},{6,7},{7,6},{8,9},{9,8},{10,11... | collective-permute-start | bytes 1376264 | tf_op jit(solution)/shard_map/ppermute | solution.py:469
  24.1 17.0 %collective-permute-start.4 = (f32[4,224,128]{2,1,0:T(8,128)S(1)}, f32[4,224,128]{2,1,0:T(8,128)S(1)}, u32[]{:S(2)}, u32[]{:S(2)}) collective-permute-start(f32[4,224,128]{2,1,0:T(8,128)S(1)} %gather_fusion), channel_id=1, source_target_pairs={{0,2},{1,3},{2,0},{3,1},{4,6},{5,7},{6,4},{7,5},{8,10},{9,11},{10,... | collective-permute-start | bytes 1376264 | tf_op jit(solution)/shard_map/ppermute | solution.py:469
  25.9 0.9 copy-start.6
  41.0 3.0 %copy-start.4 = (f32[4,224,128]{2,1,0:T(8,128)}, f32[4,224,128]{2,1,0:T(8,128)S(1)}, u32[]{:S(2)}) copy-start(f32[4,224,128]{2,1,0:T(8,128)S(1)} %collective-permute-done.4.refs_0_) | copy-start | bytes 1376260
  41.0 1.9 %collective-permute-start.5 = (f32[4,224,128]{2,1,0:T(8,128)S(1)}, f32[4,224,128]{2,1,0:T(8,128)S(1)}, u32[]{:S(2)}, u32[]{:S(2)}) collective-permute-start(f32[4,224,128]{2,1,0:T(8,128)S(1)} %collective-permute-done.4.refs_0_), channel_id=1, source_target_pairs={{0,1},{1,0},{2,3},{3,2},{4,5},{5,4},{6,7},{7,6},{8,9},{9,8},{10,11... | collective-permute-start | bytes 1376264 | tf_op jit(solution)/shard_map/ppermute | solution.py:469
  42.9 1.1 copy-start.5
  86.5 15.9 %collective-permute-start.7 = (f32[4,4,4096]{2,1,0:T(4,128)}, f32[4,4,4096]{2,1,0:T(4,128)S(1)}, u32[]{:S(2)}, u32[]{:S(2)}) collective-permute-start(f32[4,4,4096]{2,1,0:T(4,128)} %get-tuple-element.53), channel_id=1, source_target_pairs={{0,2},{1,3},{2,0},{3,1},{4,6},{5,7},{6,4},{7,5},{8,10},{9,11},{10,... | collective-permute-start | bytes 786440 | tf_op jit(solution)/shard_map/ppermute | solution.py:469
  88.0 15.6 %collective-permute-start.6 = (f32[4,4,4096]{2,1,0:T(4,128)}, f32[4,4,4096]{2,1,0:T(4,128)S(1)}, u32[]{:S(2)}, u32[]{:S(2)}) collective-permute-start(f32[4,4,4096]{2,1,0:T(4,128)} %get-tuple-element.51), channel_id=1, source_target_pairs={{0,2},{1,3},{2,0},{3,1},{4,6},{5,7},{6,4},{7,5},{8,10},{9,11},{10,... | collective-permute-start | bytes 786440 | tf_op jit(solution)/shard_map/ppermute | solution.py:469
  103.4 1.6 %collective-permute-start.8 = (f32[4,4,4096]{2,1,0:T(4,128)S(1)}, f32[4,4,4096]{2,1,0:T(4,128)S(1)}, u32[]{:S(2)}, u32[]{:S(2)}) collective-permute-start(f32[4,4,4096]{2,1,0:T(4,128)S(1)} %add.164), channel_id=1, source_target_pairs={{0,1},{1,0},{2,3},{3,2},{4,5},{5,4},{6,7},{7,6},{8,9},{9,8},{10,11... | collective-permute-start | bytes 786440 | tf_op jit(solution)/shard_map/ppermute | solution.py:469
  106.7 6.4 %collective-permute-start.9 = (f32[4,4096]{1,0:T(4,128)S(1)}, f32[4,4096]{1,0:T(4,128)S(1)}, u32[]{:S(2)}, u32[]{:S(2)}) collective-permute-start(f32[4,4096]{1,0:T(4,128)S(1)} %get-tuple-element.62), channel_id=1, source_target_pairs={{0,4},{4,8},{8,12},{12,0},{1,5},{5,9},{9,13},{13,1},{2,6},{6,10},{... | collective-permute-start | bytes 196616 | tf_op jit(solution)/shard_map/ppermute | solution.py:469
  107.6 8.0 %collective-permute-start.10 = (f32[4,4096]{1,0:T(4,128)S(1)}, f32[4,4096]{1,0:T(4,128)S(1)}, u32[]{:S(2)}, u32[]{:S(2)}) collective-permute-start(f32[4,4096]{1,0:T(4,128)S(1)} %get-tuple-element.61), channel_id=1, source_target_pairs={{0,8},{4,12},{8,0},{12,4},{1,9},{5,13},{9,1},{13,5},{2,10},{6,14},... | collective-permute-start | bytes 196616 | tf_op jit(solution)/shard_map/ppermute | solution.py:469
  109.1 6.4 %collective-permute-start.11 = (f32[4,4096]{1,0:T(4,128)S(1)}, f32[4,4096]{1,0:T(4,128)S(1)}, u32[]{:S(2)}, u32[]{:S(2)}) collective-permute-start(f32[4,4096]{1,0:T(4,128)S(1)} %get-tuple-element.60), channel_id=1, source_target_pairs={{0,12},{4,0},{8,4},{12,8},{1,13},{5,1},{9,5},{13,9},{2,14},{6,2},{... | collective-permute-start | bytes 196616 | tf_op jit(solution)/shard_map/ppermute | solution.py:469
  113.1 2.5 %copy-start.1 = (f32[4,4096]{1,0:T(4,128)}, f32[4,4096]{1,0:T(4,128)S(1)}, u32[]{:S(2)}) copy-start(f32[4,4096]{1,0:T(4,128)S(1)} %collective-permute-done.9.refs_1_) | copy-start | bytes 196612
  115.5 0.6 copy-start.2
  115.5 0.6 copy-start.3

commit v7 on v6

--- a/solution.py
+++ b/solution.py
@@ -15,7 +15,7 @@
 AHEAD = 1
 FIELDS = 7
 KEPT = 2 * ROWS + 8
-TABLES = 9
+TABLES = 11
 PAD = 16
 LINES = 80
 F32 = jnp.float32
@@ -301,10 +301,10 @@
 
 
 def far_kernel(longer, unroll, chunks, n_x, at_once, turns, base_ref, last_ref, at_ref, tab_ref, *refs):
-    groups = (len(refs) - 12) // 2
+    groups = (len(refs) - 11) // 2
     in_refs = refs[:groups]
-    near_ref, table_ref, lines_ref, back_ref, flat_ref, own_ref = refs[groups : groups + 6]
-    field_ref, out_refs = refs[groups + 6], refs[groups + 7 : -5]
+    near_ref, table_ref, lines_ref, back_ref, flat_ref = refs[groups : groups + 5]
+    field_ref, out_refs = refs[groups + 5], refs[groups + 6 : -5]
     mesh, far_field, sums, kept, arrived = refs[-5:]
     keep = kept.shape[0] == groups * n_x
     step = pl.program_id(0)
@@ -353,8 +353,8 @@
         first_half = lax.broadcasted_iota(jnp.int32, (N, LANES), 1) < LANES // 2
 
         def green(k):
-            total = flat_ref[0] + own_ref[0, pl.ds(k, 1), :]
-            rest = flat_ref[1] * own_ref[1, pl.ds(k, 1), :]
+            share = [lanes([tab_ref[m, pl.ds(k, 1), :]] * (N // LANES)) for m in (9, 10)]
+            total, rest = flat_ref[0] + share[0], flat_ref[1] * share[1]
             return jnp.where(total > 0, rest / jnp.where(total > 0, total, F32(1)), F32(0))
 
         def lines_of(own, t):
@@ -513,6 +513,7 @@
     angle = freq.astype(F32) * F32(np.pi / N)
     far_cos, near_cos = jnp.cos(3 * angle), jnp.cos(angle)
     far_sin, near_sin = jnp.sin(3 * angle), jnp.sin(angle)
+    along_own = symbol(freq, N)
     tab = [
         (far_cos + 23 * near_cos) * F32(1 / 24),
         (far_cos - near_cos) * F32(1 / 2),
@@ -521,6 +522,8 @@
         far_cos - near_cos,
         far_sin - 3 * near_sin,
         (freq % 2).astype(F32),
+        along_own,
+        jnp.exp(-0.5 * along_own),
     ]
     tab = [jnp.broadcast_to(t[:, None], (ROWS, LANES)) for t in tab]
     cells = 2 * jnp.arange(LANES, dtype=jnp.int32) + 1
@@ -528,15 +531,11 @@
     turn_cos, turn_sin = jnp.cos(turns), jnp.sin(turns)
     tab = jnp.stack([turn_cos + turn_sin] + tab[:6] + [turn_cos - turn_sin] + tab[6:])
     tab = jnp.where((jnp.arange(ROWS) < own)[None, :, None], tab, F32(0.0))
-    along_own = symbol(freq, N)
-    own_share = jnp.stack([along_own, jnp.exp(-0.5 * along_own)])
-    own_share = jnp.broadcast_to(own_share[:, :, None], (2, ROWS, N))
 
     half = n_y // 2
     _, rank = lax.sort((order, place), num_keys=1, is_stable=False)
     rank = rank.reshape(chunks, LANES)
-    ready = (gather_x(packed), own_share, tab, rank)
-    arrived, own_share, tab, rank = lax.optimization_barrier(ready)
+    arrived, tab, rank = lax.optimization_barrier((gather_x(packed), tab, rank))
     groups = [arrived]
     for s in range(1, half + 1):
         step = s & -s
@@ -636,7 +635,6 @@
                 whole(3 * N, N),
                 whole(3 * N, N),
                 whole(2, N, N),
-                whole(2, ROWS, N),
             ],
             out_specs=[
                 pl.BlockSpec(
@@ -663,7 +661,6 @@
         *far,
         near_mesh,
         *tables(),
-        own_share,
     )
 
     *far_sums, near_field = lax.optimization_barrier((*far_sums, near_field))

time: 120 us -> 119 us (level)
  no operation moved by 1% of the time
where the time goes in v7:
time: 119 us; the launch traced here: 118 us
  Pallas kernels  73.3 us (62%)
  starting transfers between devices  15.5 us (13%)
  other arithmetic  14.8 us (12%)
  waiting for transfers between devices  8.37 us (7%)
  local copies, waits for them, and re-layouts  5.44 us (5%)
    pallas_call x1, Pallas kernels, shards(): pl.pallas_call(functools.partial(far_kernel, longer, unroll, chunks, n_x,...  42.2 us
    ppermute x12, starting transfers between devices, exchange(): return lax.ppermute(value, axis, pairs)  15.5 us
    pallas_call x1, Pallas kernels, shards(): pl.pallas_call(functools.partial(near_kernel, longer, chunks, n_x), grid_...  14.4 us
    pallas_call x1, Pallas kernels, shards(): pl.pallas_call(functools.partial(last_kernel, unroll, chunks, n_x), grid_...  13.8 us
    ppermute x12, waiting for transfers between devices, exchange(): return lax.ppermute(value, axis, pairs)  8.37 us
    sort x1, other arithmetic, shards(): lax.sort((cell_x, cell_y, cell_z, fraction[0], fraction[1], fraction[2],...  5.83 us
    sort x1, other arithmetic, shards(): _, rank = lax.sort((order, place), num_keys=1, is_stable=False)  5.57 us
    pallas_call x1, Pallas kernels, shards(): pl.pallas_call(order_kernel, out_shape=[jax.ShapeDtypeStruct((chunks, LAN...  2.95 us
  transfers between devices with their start and end apart: 12, of which 6 were waited for; matrix products, arithmetic and copies ran while one was open for 8% of the time, Pallas kernels for 24%

profile of v7, /device:TPU:0, one launch (start us, length us, event | category | flops | bytes accessed | tf_op | source)
XLA Modules:
  0.0 118.3 jit_solution(6895719251131279628)
XLA Ops:
  0.6 1.0 fusion.14
  1.7 5.8 %sort.66 = (s32[4096]{0:T(1024)S(1)}, s32[4096]{0:T(1024)S(1)}, s32[4096]{0:T(1024)S(1)}, f32[4096]{0:T(1024)S(1)}, f32[4096]{0:T(1024)S(1)}, /*index=5*/f32[4096]{0:T(1024)S(1)}, f32[4096]{0:T(1024)S(1)}, s32[4096]{0:T(1024)S(1)}) sort(s32[4096]{0:T(1024)} %param.9, s32[4096]{0:T(1024)} %param.10, s32[4096]{0:T(1024)} %param.11, f32[4096]{0:T(1024)S(1)} %bitcast.52, ...), dimensions={0}, to_apply=%region_0.0 | sort | flops 49152 | bytes 262144 | tf_op jit(solution)/shard_map/sort | solution.py:503
  7.6 5.1 %collective-permute-start.2 = (f32[224,128]{1,0:T(8,128)S(1)}, f32[224,128]{1,0:T(8,128)S(1)}, u32[]{:S(2)}, u32[]{:S(2)}) collective-permute-start(f32[224,128]{1,0:T(8,128)S(1)} %constant_dynamic-update-slice_fusion), channel_id=1, source_target_pairs={{0,12},{4,0},{8,4},{12,8},{1,13},{5,1},{9,5},{13,9},{2,14},{6,2},{... | collective-permute-start | bytes 344072 | tf_op jit(solution)/shard_map/ppermute | solution.py:469
  12.7 1.0 collective-permute-start
  14.8 0.7 broadcast_select_fusion.tab_ref
  15.6 5.6 %sort.67 = (s32[4096]{0:T(1024)}, s32[4096]{0:T(1024)}) sort(s32[4096]{0:T(1024)S(1)} %get-tuple-element.35, s32[4096]{0:T(1024)S(1)} %iota.29), dimensions={0}, to_apply=%region_1.2 | sort | flops 49152 | bytes 65536 | tf_op jit(solution)/shard_map/sort | solution.py:536
  21.2 1.5 %collective-permute-done.1 = f32[224,128]{1,0:T(8,128)S(1)} collective-permute-done((f32[224,128]{1,0:T(8,128)S(1)}, f32[224,128]{1,0:T(8,128)S(1)}, u32[]{:S(2)}, u32[]{:S(2)}) %collective-permute-start.1) | collective-permute-done | bytes 114720 | tf_op jit(solution)/shard_map/ppermute | solution.py:469
  23.4 1.6 %collective-permute-start.4 = (f32[4,224,128]{2,1,0:T(8,128)S(1)}, f32[4,224,128]{2,1,0:T(8,128)S(1)}, u32[]{:S(2)}, u32[]{:S(2)}) collective-permute-start(f32[4,224,128]{2,1,0:T(8,128)S(1)} %gather_fusion), channel_id=1, source_target_pairs={{0,2},{1,3},{2,0},{3,1},{4,6},{5,7},{6,4},{7,5},{8,10},{9,11},{10,... | collective-permute-start | bytes 1376264 | tf_op jit(solution)/shard_map/ppermute | solution.py:469
  26.1 14.4 %near_spread.1 = (f32[2,272,16,128]{3,2,1,0:T(8,128)}, f32[8,40,4096]{2,1,0:T(8,128)}) custom-call(s32[8,32]{1,0:T(8,128)} %get-tuple-element.57.base_ref, s32[8,32]{1,0:T(8,128)} %get-tuple-element.56.last_ref, f32[11,16,128]{2,1,0:T(8,128)} %broadcast_select_fusion.tab_ref, f32[4,224,128]{2,1,0:T(8,128)} %copy-done, f32[4,224,128]{2,1,0:T(8,128)} %copy-done.6), custom_call_target="tpu_custom_call" | custom-call | flops 19660800000 | bytes 5242880 | tf_op jit(solution)/shard_map/near_spread/pallas_call | solution.py:598
  40.7 1.7 %collective-permute-done.5.refs_1_ = f32[4,224,128]{2,1,0:T(8,128)S(1)} collective-permute-done((f32[4,224,128]{2,1,0:T(8,128)S(1)}, f32[4,224,128]{2,1,0:T(8,128)S(1)}, u32[]{:S(2)}, u32[]{:S(2)}) %collective-permute-start.5) | collective-permute-done | bytes 458784 | tf_op jit(solution)/shard_map/ppermute | solution.py:469
  42.4 1.0 slice_reduce_fusion
  43.4 42.2 %far_spread_filter_sample.1 = (bf16[2,4352,256]{2,1,0:T(8,128)(2,1)}, f32[4,4,4096]{2,1,0:T(4,128)}, f32[4,4,4096]{2,1,0:T(4,128)}) custom-call(s32[8,32]{1,0:T(8,128)} %get-tuple-element.55.base_ref, s32[8,32]{1,0:T(8,128)} %get-tuple-element.54.last_ref, s32[1]{0:T(128)} %bitcast.18.at_ref, f32[11,16,128]{2,1,0:T(8,128)} %broadcast_select_fusion.tab_ref, ...), custom_call_target="tpu_custom_call" | custom-call | flops 58982400000 | bytes 15728640 | tf_op jit(solution)/shard_map/far_spread_filter_sample/pallas_call | solution.py:625
  85.6 1.6 %collective-permute-start.7 = (f32[4,4,4096]{2,1,0:T(4,128)}, f32[4,4,4096]{2,1,0:T(4,128)S(1)}, u32[]{:S(2)}, u32[]{:S(2)}) collective-permute-start(f32[4,4,4096]{2,1,0:T(4,128)} %get-tuple-element.51), channel_id=1, source_target_pairs={{0,2},{1,3},{2,0},{3,1},{4,6},{5,7},{6,4},{7,5},{8,10},{9,11},{10,... | collective-permute-start | bytes 786440 | tf_op jit(solution)/shard_map/ppermute | solution.py:469
  87.7 13.8 %near_sample.1 = (f32[4,4,4096]{2,1,0:T(4,128)}, f32[4,4,4096]{2,1,0:T(4,128)}) custom-call(s32[8,32]{1,0:T(8,128)} %get-tuple-element.57.base_ref, s32[8,32]{1,0:T(8,128)} %get-tuple-element.56.last_ref, f32[8,40,4096]{2,1,0:T(8,128)} %get-tuple-element.40.kept, bf16[2,272,16,256]{3,2,1,0:T(8,128)(2,1)} %bitcast.56), custom_call_target="tpu_custom_call" | custom-call | flops 19660800000 | bytes 5242880 | tf_op jit(solution)/shard_map/near_sample/pallas_call | solution.py:668
  101.5 1.0 add.147
  102.7 1.5 %collective-permute-done.8 = f32[4,4,4096]{2,1,0:T(4,128)S(1)} collective-permute-done((f32[4,4,4096]{2,1,0:T(4,128)S(1)}, f32[4,4,4096]{2,1,0:T(4,128)S(1)}, u32[]{:S(2)}, u32[]{:S(2)}) %collective-permute-start.8) | collective-permute-done | bytes 262176 | tf_op jit(solution)/shard_map/ppermute | solution.py:469
  104.2 1.0 add_add_fusion
  105.1 0.7 dynamic-slice_bitcast_fusion
  105.8 1.0 collective-permute-start.9
  106.8 1.4 %collective-permute-start.10 = (f32[4,4096]{1,0:T(4,128)S(1)}, f32[4,4096]{1,0:T(4,128)S(1)}, u32[]{:S(2)}, u32[]{:S(2)}) collective-permute-start(f32[4,4096]{1,0:T(4,128)S(1)} %get-tuple-element.59), channel_id=1, source_target_pairs={{0,8},{4,12},{8,0},{12,4},{1,9},{5,13},{9,1},{13,5},{2,10},{6,14},... | collective-permute-start | bytes 196616 | tf_op jit(solution)/shard_map/ppermute | solution.py:469
  108.3 2.9 %collective-permute-start.11 = (f32[4,4096]{1,0:T(4,128)S(1)}, f32[4,4096]{1,0:T(4,128)S(1)}, u32[]{:S(2)}, u32[]{:S(2)}) collective-permute-start(f32[4,4096]{1,0:T(4,128)S(1)} %get-tuple-element.58), channel_id=1, source_target_pairs={{0,12},{4,0},{8,4},{12,8},{1,13},{5,1},{9,5},{13,9},{2,14},{6,2},{... | collective-permute-start | bytes 196616 | tf_op jit(solution)/shard_map/ppermute | solution.py:469
  111.2 1.0 collective-permute-done.9.refs_1_
  112.2 2.5 %collective-permute-done.10.refs_2_ = f32[4,4096]{1,0:T(4,128)S(1)} collective-permute-done((f32[4,4096]{1,0:T(4,128)S(1)}, f32[4,4096]{1,0:T(4,128)S(1)}, u32[]{:S(2)}, u32[]{:S(2)}) %collective-permute-start.10) | collective-permute-done | bytes 65568 | tf_op jit(solution)/shard_map/ppermute | solution.py:469
  115.3 2.9 %order.1 = (f32[32,128]{1,0:T(8,128)}, f32[3,4096]{1,0:T(4,128)}) custom-call(s32[32,128]{1,0:T(8,128)} %bitcast.54, f32[4,4096]{1,0:T(4,128)} %get-tuple-element.61.refs_0_, f32[4,4096]{1,0:T(4,128)} %copy-done.1, f32[4,4096]{1,0:T(4,128)} %copy-done.2, f32[4,4096]{1,0:T(4,128)} %copy-done.3), custom_call_target="tpu_custom_call" | custom-call | tf_op jit(solution)/shard_map/order/pallas_call | solution.py:691
  (66 shorter events, 4.4 us)
Async XLA Ops:
  7.6 13.6 %collective-permute-start.2 = (f32[224,128]{1,0:T(8,128)S(1)}, f32[224,128]{1,0:T(8,128)S(1)}, u32[]{:S(2)}, u32[]{:S(2)}) collective-permute-start(f32[224,128]{1,0:T(8,128)S(1)} %constant_dynamic-update-slice_fusion), channel_id=1, source_target_pairs={{0,12},{4,0},{8,4},{12,8},{1,13},{5,1},{9,5},{13,9},{2,14},{6,2},{... | collective-permute-start | bytes 344072 | tf_op jit(solution)/shard_map/ppermute | solution.py:469
  12.7 10.0 %collective-permute-start.1 = (f32[224,128]{1,0:T(8,128)S(1)}, f32[224,128]{1,0:T(8,128)S(1)}, u32[]{:S(2)}, u32[]{:S(2)}) collective-permute-start(f32[224,128]{1,0:T(8,128)S(1)} %constant_dynamic-update-slice_fusion), channel_id=1, source_target_pairs={{0,8},{4,12},{8,0},{12,4},{1,9},{5,13},{9,1},{13,5},{2,10},{6,14},... | collective-permute-start | bytes 344072 | tf_op jit(solution)/shard_map/ppermute | solution.py:469
  12.7 10.0 %collective-permute-start = (f32[224,128]{1,0:T(8,128)S(1)}, f32[224,128]{1,0:T(8,128)S(1)}, u32[]{:S(2)}, u32[]{:S(2)}) collective-permute-start(f32[224,128]{1,0:T(8,128)S(1)} %constant_dynamic-update-slice_fusion), channel_id=1, source_target_pairs={{0,4},{4,8},{8,12},{12,0},{1,5},{5,9},{9,13},{13,1},{2,6},{6,10},{... | collective-permute-start | bytes 344072 | tf_op jit(solution)/shard_map/ppermute | solution.py:469
  23.3 2.8 %copy-start = (f32[4,224,128]{2,1,0:T(8,128)}, f32[4,224,128]{2,1,0:T(8,128)S(1)}, u32[]{:S(2)}) copy-start(f32[4,224,128]{2,1,0:T(8,128)S(1)} %gather_fusion) | copy-start | bytes 1376260
  23.3 1.9 %collective-permute-start.3 = (f32[4,224,128]{2,1,0:T(8,128)S(1)}, f32[4,224,128]{2,1,0:T(8,128)S(1)}, u32[]{:S(2)}, u32[]{:S(2)}) collective-permute-start(f32[4,224,128]{2,1,0:T(8,128)S(1)} %gather_fusion), channel_id=1, source_target_pairs={{0,1},{1,0},{2,3},{3,2},{4,5},{5,4},{6,7},{7,6},{8,9},{9,8},{10,11... | collective-permute-start | bytes 1376264 | tf_op jit(solution)/shard_map/ppermute | solution.py:469
  23.4 17.1 %collective-permute-start.4 = (f32[4,224,128]{2,1,0:T(8,128)S(1)}, f32[4,224,128]{2,1,0:T(8,128)S(1)}, u32[]{:S(2)}, u32[]{:S(2)}) collective-permute-start(f32[4,224,128]{2,1,0:T(8,128)S(1)} %gather_fusion), channel_id=1, source_target_pairs={{0,2},{1,3},{2,0},{3,1},{4,6},{5,7},{6,4},{7,5},{8,10},{9,11},{10,... | collective-permute-start | bytes 1376264 | tf_op jit(solution)/shard_map/ppermute | solution.py:469
  25.2 0.9 copy-start.6
  40.5 3.0 %copy-start.4 = (f32[4,224,128]{2,1,0:T(8,128)}, f32[4,224,128]{2,1,0:T(8,128)S(1)}, u32[]{:S(2)}) copy-start(f32[4,224,128]{2,1,0:T(8,128)S(1)} %collective-permute-done.4.refs_0_) | copy-start | bytes 1376260
  40.5 1.9 %collective-permute-start.5 = (f32[4,224,128]{2,1,0:T(8,128)S(1)}, f32[4,224,128]{2,1,0:T(8,128)S(1)}, u32[]{:S(2)}, u32[]{:S(2)}) collective-permute-start(f32[4,224,128]{2,1,0:T(8,128)S(1)} %collective-permute-done.4.refs_0_), channel_id=1, source_target_pairs={{0,1},{1,0},{2,3},{3,2},{4,5},{5,4},{6,7},{7,6},{8,9},{9,8},{10,11... | collective-permute-start | bytes 1376264 | tf_op jit(solution)/shard_map/ppermute | solution.py:469
  42.3 1.1 copy-start.5
  85.6 15.9 %collective-permute-start.7 = (f32[4,4,4096]{2,1,0:T(4,128)}, f32[4,4,4096]{2,1,0:T(4,128)S(1)}, u32[]{:S(2)}, u32[]{:S(2)}) collective-permute-start(f32[4,4,4096]{2,1,0:T(4,128)} %get-tuple-element.51), channel_id=1, source_target_pairs={{0,2},{1,3},{2,0},{3,1},{4,6},{5,7},{6,4},{7,5},{8,10},{9,11},{10,... | collective-permute-start | bytes 786440 | tf_op jit(solution)/shard_map/ppermute | solution.py:469
  87.2 15.5 %collective-permute-start.6 = (f32[4,4,4096]{2,1,0:T(4,128)}, f32[4,4,4096]{2,1,0:T(4,128)S(1)}, u32[]{:S(2)}, u32[]{:S(2)}) collective-permute-start(f32[4,4,4096]{2,1,0:T(4,128)} %get-tuple-element.49), channel_id=1, source_target_pairs={{0,2},{1,3},{2,0},{3,1},{4,6},{5,7},{6,4},{7,5},{8,10},{9,11},{10,... | collective-permute-start | bytes 786440 | tf_op jit(solution)/shard_map/ppermute | solution.py:469
  102.6 1.6 %collective-permute-start.8 = (f32[4,4,4096]{2,1,0:T(4,128)S(1)}, f32[4,4,4096]{2,1,0:T(4,128)S(1)}, u32[]{:S(2)}, u32[]{:S(2)}) collective-permute-start(f32[4,4,4096]{2,1,0:T(4,128)S(1)} %add.147), channel_id=1, source_target_pairs={{0,1},{1,0},{2,3},{3,2},{4,5},{5,4},{6,7},{7,6},{8,9},{9,8},{10,11... | collective-permute-start | bytes 786440 | tf_op jit(solution)/shard_map/ppermute | solution.py:469
  105.8 6.4 %collective-permute-start.9 = (f32[4,4096]{1,0:T(4,128)S(1)}, f32[4,4096]{1,0:T(4,128)S(1)}, u32[]{:S(2)}, u32[]{:S(2)}) collective-permute-start(f32[4,4096]{1,0:T(4,128)S(1)} %get-tuple-element.60), channel_id=1, source_target_pairs={{0,4},{4,8},{8,12},{12,0},{1,5},{5,9},{9,13},{13,1},{2,6},{6,10},{... | collective-permute-start | bytes 196616 | tf_op jit(solution)/shard_map/ppermute | solution.py:469
  106.8 7.8 %collective-permute-start.10 = (f32[4,4096]{1,0:T(4,128)S(1)}, f32[4,4096]{1,0:T(4,128)S(1)}, u32[]{:S(2)}, u32[]{:S(2)}) collective-permute-start(f32[4,4096]{1,0:T(4,128)S(1)} %get-tuple-element.59), channel_id=1, source_target_pairs={{0,8},{4,12},{8,0},{12,4},{1,9},{5,13},{9,1},{13,5},{2,10},{6,14},... | collective-permute-start | bytes 196616 | tf_op jit(solution)/shard_map/ppermute | solution.py:469
  108.3 6.4 %collective-permute-start.11 = (f32[4,4096]{1,0:T(4,128)S(1)}, f32[4,4096]{1,0:T(4,128)S(1)}, u32[]{:S(2)}, u32[]{:S(2)}) collective-permute-start(f32[4,4096]{1,0:T(4,128)S(1)} %get-tuple-element.58), channel_id=1, source_target_pairs={{0,12},{4,0},{8,4},{12,8},{1,13},{5,1},{9,5},{13,9},{2,14},{6,2},{... | collective-permute-start | bytes 196616 | tf_op jit(solution)/shard_map/ppermute | solution.py:469
  112.2 2.5 %copy-start.1 = (f32[4,4096]{1,0:T(4,128)}, f32[4,4096]{1,0:T(4,128)S(1)}, u32[]{:S(2)}) copy-start(f32[4,4096]{1,0:T(4,128)S(1)} %collective-permute-done.9.refs_1_) | copy-start | bytes 196612
  114.7 0.6 copy-start.2
  114.7 0.6 copy-start.3

commit v8 on v7

--- a/solution.py
+++ b/solution.py
@@ -310,7 +310,7 @@
     step = pl.program_id(0)
     spreads = groups * n_x
     packs = spreads + turns
-    samples = packs + 2 * groups
+    samples = packs + 1 + groups
     slots = [at_ref[0] ^ s for s in range(2 * groups)]
     copies = [
         pltpu.make_async_copy(near_ref.at[g], mesh.at[slots[g]], arrived.at[g]) for g in range(groups)
@@ -379,13 +379,14 @@
 
     far_flat = far_field.reshape(groups, (N + PAD) * ROWS, N)
 
-    @pl.when((step >= packs) & (step < packs + groups))
-    def _():
-        pack(flat.at[at_ref[0] ^ (groups + step - packs)], far_flat.at[step - packs])
-
-    @pl.when((step >= packs + groups) & (step < samples))
-    def _():
-        pack(flat.at[at_ref[0] ^ (step - packs - groups)], field_ref.at[0])
+    @pl.when(step == packs)
+    def _():
+        for g in range(groups):
+            pack(flat.at[slots[groups + g]], far_flat.at[g])
+
+    @pl.when((step > packs) & (step < samples))
+    def _():
+        pack(flat.at[at_ref[0] ^ (step - packs - 1)], field_ref.at[0])
 
     @pl.when(step >= samples)
     def _():
@@ -424,7 +425,7 @@
         value_ref[pl.ds(o, 1), :] = result[:1]
         force_ref[:, place_of(o)] = -result[1:]
 
-    at_once = 4 if chunks % 4 == 0 else 1
+    at_once = 8 if chunks % 8 == 0 else 1
 
     def some(i, carry):
         for u in range(at_once):
@@ -545,7 +546,7 @@
     longer = 32 if chunks % 32 == 0 else unroll
     size = N + PAD
     steps = half * n_x
-    at_once = 4 if own % 4 == 0 else 1
+    at_once = 8 if own % 8 == 0 else 1
     turns = own // at_once
     params = pltpu.CompilerParams(vmem_limit_bytes=56 * 1024 * 1024)
 
@@ -620,7 +621,7 @@
     far_bounds = bounds(far)
 
     packs = steps + turns
-    samples = packs + 2 * half
+    samples = packs + 1 + half
     keep = steps <= 8
     near_field, *far_sums = pl.pallas_call(
         functools.partial(far_kernel, longer, unroll, chunks, n_x, at_once, turns),
@@ -638,7 +639,7 @@
             ],
             out_specs=[
                 pl.BlockSpec(
-                    (1, size * ROWS, N), lambda t, *_: (clamp(t - packs - half, half - 1), 0, 0)
+                    (1, size * ROWS, N), lambda t, *_: (clamp(t - packs - 1, half - 1), 0, 0)
                 ),
             ]
             + results(samples),

time: 119 us -> 118 us (level)
  no operation moved by 1% of the time
where the time goes in v8:
time: 118 us
  Pallas kernels  72.6 us (62%)
  starting transfers between devices  15.5 us (13%)
  other arithmetic  14.8 us (13%)
  waiting for transfers between devices  8.36 us (7%)
  local copies, waits for them, and re-layouts  5.44 us (5%)
    pallas_call x1, Pallas kernels, shards(): pl.pallas_call(functools.partial(far_kernel, longer, unroll, chunks, n_x,...  41.6 us
    ppermute x12, starting transfers between devices, exchange(): return lax.ppermute(value, axis, pairs)  15.5 us
    pallas_call x1, Pallas kernels, shards(): pl.pallas_call(functools.partial(near_kernel, longer, chunks, n_x), grid_...  14.5 us
    pallas_call x1, Pallas kernels, shards(): pl.pallas_call(functools.partial(last_kernel, unroll, chunks, n_x), grid_...  13.8 us
    ppermute x12, waiting for transfers between devices, exchange(): return lax.ppermute(value, axis, pairs)  8.36 us
    sort x1, other arithmetic, shards(): lax.sort((cell_x, cell_y, cell_z, fraction[0], fraction[1], fraction[2],...  5.83 us
    sort x1, other arithmetic, shards(): _, rank = lax.sort((order, place), num_keys=1, is_stable=False)  5.57 us
    pallas_call x1, Pallas kernels, shards(): pl.pallas_call(order_kernel, out_shape=[jax.ShapeDtypeStruct((chunks, LAN...  2.6 us
  transfers between devices with their start and end apart: 12, of which 6 were waited for; matrix products, arithmetic and copies ran while one was open for 8% of the time, Pallas kernels for 24%

profile of v8, /device:TPU:0, one launch (start us, length us, event | category | flops | bytes accessed | tf_op | source)
XLA Modules:
  0.0 117.5 jit_solution(4617345697675761018)
XLA Ops:
  0.6 1.0 fusion.14
  1.7 5.8 %sort.66 = (s32[4096]{0:T(1024)S(1)}, s32[4096]{0:T(1024)S(1)}, s32[4096]{0:T(1024)S(1)}, f32[4096]{0:T(1024)S(1)}, f32[4096]{0:T(1024)S(1)}, /*index=5*/f32[4096]{0:T(1024)S(1)}, f32[4096]{0:T(1024)S(1)}, s32[4096]{0:T(1024)S(1)}) sort(s32[4096]{0:T(1024)} %param.9, s32[4096]{0:T(1024)} %param.10, s32[4096]{0:T(1024)} %param.11, f32[4096]{0:T(1024)S(1)} %bitcast.52, ...), dimensions={0}, to_apply=%region_0.0 | sort | flops 49152 | bytes 262144 | tf_op jit(solution)/shard_map/sort | solution.py:504
  7.6 5.1 %collective-permute-start.2 = (f32[224,128]{1,0:T(8,128)S(1)}, f32[224,128]{1,0:T(8,128)S(1)}, u32[]{:S(2)}, u32[]{:S(2)}) collective-permute-start(f32[224,128]{1,0:T(8,128)S(1)} %constant_dynamic-update-slice_fusion), channel_id=1, source_target_pairs={{0,12},{4,0},{8,4},{12,8},{1,13},{5,1},{9,5},{13,9},{2,14},{6,2},{... | collective-permute-start | bytes 344072 | tf_op jit(solution)/shard_map/ppermute | solution.py:470
  12.7 1.0 collective-permute-start
  14.8 0.7 broadcast_select_fusion.tab_ref
  15.6 5.6 %sort.67 = (s32[4096]{0:T(1024)}, s32[4096]{0:T(1024)}) sort(s32[4096]{0:T(1024)S(1)} %get-tuple-element.35, s32[4096]{0:T(1024)S(1)} %iota.29), dimensions={0}, to_apply=%region_1.2 | sort | flops 49152 | bytes 65536 | tf_op jit(solution)/shard_map/sort | solution.py:537
  21.2 1.5 %collective-permute-done.1 = f32[224,128]{1,0:T(8,128)S(1)} collective-permute-done((f32[224,128]{1,0:T(8,128)S(1)}, f32[224,128]{1,0:T(8,128)S(1)}, u32[]{:S(2)}, u32[]{:S(2)}) %collective-permute-start.1) | collective-permute-done | bytes 114720 | tf_op jit(solution)/shard_map/ppermute | solution.py:470
  23.4 1.6 %collective-permute-start.4 = (f32[4,224,128]{2,1,0:T(8,128)S(1)}, f32[4,224,128]{2,1,0:T(8,128)S(1)}, u32[]{:S(2)}, u32[]{:S(2)}) collective-permute-start(f32[4,224,128]{2,1,0:T(8,128)S(1)} %gather_fusion), channel_id=1, source_target_pairs={{0,2},{1,3},{2,0},{3,1},{4,6},{5,7},{6,4},{7,5},{8,10},{9,11},{10,... | collective-permute-start | bytes 1376264 | tf_op jit(solution)/shard_map/ppermute | solution.py:470
  26.1 14.5 %near_spread.1 = (f32[2,272,16,128]{3,2,1,0:T(8,128)}, f32[8,40,4096]{2,1,0:T(8,128)}) custom-call(s32[8,32]{1,0:T(8,128)} %get-tuple-element.57.base_ref, s32[8,32]{1,0:T(8,128)} %get-tuple-element.56.last_ref, f32[11,16,128]{2,1,0:T(8,128)} %broadcast_select_fusion.tab_ref, f32[4,224,128]{2,1,0:T(8,128)} %copy-done, f32[4,224,128]{2,1,0:T(8,128)} %copy-done.6), custom_call_target="tpu_custom_call" | custom-call | flops 19660800000 | bytes 5242880 | tf_op jit(solution)/shard_map/near_spread/pallas_call | solution.py:599
  40.8 1.7 %collective-permute-done.5.refs_1_ = f32[4,224,128]{2,1,0:T(8,128)S(1)} collective-permute-done((f32[4,224,128]{2,1,0:T(8,128)S(1)}, f32[4,224,128]{2,1,0:T(8,128)S(1)}, u32[]{:S(2)}, u32[]{:S(2)}) %collective-permute-start.5) | collective-permute-done | bytes 458784 | tf_op jit(solution)/shard_map/ppermute | solution.py:470
  42.5 1.0 slice_reduce_fusion
  43.6 41.6 %far_spread_filter_sample.1 = (bf16[2,4352,256]{2,1,0:T(8,128)(2,1)}, f32[4,4,4096]{2,1,0:T(4,128)}, f32[4,4,4096]{2,1,0:T(4,128)}) custom-call(s32[8,32]{1,0:T(8,128)} %get-tuple-element.55.base_ref, s32[8,32]{1,0:T(8,128)} %get-tuple-element.54.last_ref, s32[1]{0:T(128)} %bitcast.18.at_ref, f32[11,16,128]{2,1,0:T(8,128)} %broadcast_select_fusion.tab_ref, ...), custom_call_target="tpu_custom_call" | custom-call | flops 58982400000 | bytes 15728640 | tf_op jit(solution)/shard_map/far_spread_filter_sample/pallas_call | solution.py:626
  85.2 1.5 %collective-permute-start.7 = (f32[4,4,4096]{2,1,0:T(4,128)}, f32[4,4,4096]{2,1,0:T(4,128)S(1)}, u32[]{:S(2)}, u32[]{:S(2)}) collective-permute-start(f32[4,4,4096]{2,1,0:T(4,128)} %get-tuple-element.51), channel_id=1, source_target_pairs={{0,2},{1,3},{2,0},{3,1},{4,6},{5,7},{6,4},{7,5},{8,10},{9,11},{10,... | collective-permute-start | bytes 786440 | tf_op jit(solution)/shard_map/ppermute | solution.py:470
  87.3 13.8 %near_sample.1 = (f32[4,4,4096]{2,1,0:T(4,128)}, f32[4,4,4096]{2,1,0:T(4,128)}) custom-call(s32[8,32]{1,0:T(8,128)} %get-tuple-element.57.base_ref, s32[8,32]{1,0:T(8,128)} %get-tuple-element.56.last_ref, f32[8,40,4096]{2,1,0:T(8,128)} %get-tuple-element.40.kept, bf16[2,272,16,256]{3,2,1,0:T(8,128)(2,1)} %bitcast.56), custom_call_target="tpu_custom_call" | custom-call | flops 19660800000 | bytes 5242880 | tf_op jit(solution)/shard_map/near_sample/pallas_call | solution.py:669
  101.1 1.0 add.147
  102.3 1.5 %collective-permute-done.8 = f32[4,4,4096]{2,1,0:T(4,128)S(1)} collective-permute-done((f32[4,4,4096]{2,1,0:T(4,128)S(1)}, f32[4,4,4096]{2,1,0:T(4,128)S(1)}, u32[]{:S(2)}, u32[]{:S(2)}) %collective-permute-start.8) | collective-permute-done | bytes 262176 | tf_op jit(solution)/shard_map/ppermute | solution.py:470
  103.8 1.0 add_add_fusion
  104.8 0.7 dynamic-slice_bitcast_fusion
  105.4 1.0 collective-permute-start.9
  106.4 1.4 %collective-permute-start.10 = (f32[4,4096]{1,0:T(4,128)S(1)}, f32[4,4096]{1,0:T(4,128)S(1)}, u32[]{:S(2)}, u32[]{:S(2)}) collective-permute-start(f32[4,4096]{1,0:T(4,128)S(1)} %get-tuple-element.59), channel_id=1, source_target_pairs={{0,8},{4,12},{8,0},{12,4},{1,9},{5,13},{9,1},{13,5},{2,10},{6,14},... | collective-permute-start | bytes 196616 | tf_op jit(solution)/shard_map/ppermute | solution.py:470
  107.9 2.9 %collective-permute-start.11 = (f32[4,4096]{1,0:T(4,128)S(1)}, f32[4,4096]{1,0:T(4,128)S(1)}, u32[]{:S(2)}, u32[]{:S(2)}) collective-permute-start(f32[4,4096]{1,0:T(4,128)S(1)} %get-tuple-element.58), channel_id=1, source_target_pairs={{0,12},{4,0},{8,4},{12,8},{1,13},{5,1},{9,5},{13,9},{2,14},{6,2},{... | collective-permute-start | bytes 196616 | tf_op jit(solution)/shard_map/ppermute | solution.py:470
  110.8 1.0 collective-permute-done.9.refs_1_
  111.8 2.5 %collective-permute-done.10.refs_2_ = f32[4,4096]{1,0:T(4,128)S(1)} collective-permute-done((f32[4,4096]{1,0:T(4,128)S(1)}, f32[4,4096]{1,0:T(4,128)S(1)}, u32[]{:S(2)}, u32[]{:S(2)}) %collective-permute-start.10) | collective-permute-done | bytes 65568 | tf_op jit(solution)/shard_map/ppermute | solution.py:470
  114.9 2.6 %order.1 = (f32[32,128]{1,0:T(8,128)}, f32[3,4096]{1,0:T(4,128)}) custom-call(s32[32,128]{1,0:T(8,128)} %bitcast.54, f32[4,4096]{1,0:T(4,128)} %get-tuple-element.61.refs_0_, f32[4,4096]{1,0:T(4,128)} %copy-done.1, f32[4,4096]{1,0:T(4,128)} %copy-done.2, f32[4,4096]{1,0:T(4,128)} %copy-done.3), custom_call_target="tpu_custom_call" | custom-call | tf_op jit(solution)/shard_map/order/pallas_call | solution.py:692
  (66 shorter events, 4.5 us)
Async XLA Ops:
  7.6 13.6 %collective-permute-start.2 = (f32[224,128]{1,0:T(8,128)S(1)}, f32[224,128]{1,0:T(8,128)S(1)}, u32[]{:S(2)}, u32[]{:S(2)}) collective-permute-start(f32[224,128]{1,0:T(8,128)S(1)} %constant_dynamic-update-slice_fusion), channel_id=1, source_target_pairs={{0,12},{4,0},{8,4},{12,8},{1,13},{5,1},{9,5},{13,9},{2,14},{6,2},{... | collective-permute-start | bytes 344072 | tf_op jit(solution)/shard_map/ppermute | solution.py:470
  12.7 10.0 %collective-permute-start.1 = (f32[224,128]{1,0:T(8,128)S(1)}, f32[224,128]{1,0:T(8,128)S(1)}, u32[]{:S(2)}, u32[]{:S(2)}) collective-permute-start(f32[224,128]{1,0:T(8,128)S(1)} %constant_dynamic-update-slice_fusion), channel_id=1, source_target_pairs={{0,8},{4,12},{8,0},{12,4},{1,9},{5,13},{9,1},{13,5},{2,10},{6,14},... | collective-permute-start | bytes 344072 | tf_op jit(solution)/shard_map/ppermute | solution.py:470
  12.7 10.0 %collective-permute-start = (f32[224,128]{1,0:T(8,128)S(1)}, f32[224,128]{1,0:T(8,128)S(1)}, u32[]{:S(2)}, u32[]{:S(2)}) collective-permute-start(f32[224,128]{1,0:T(8,128)S(1)} %constant_dynamic-update-slice_fusion), channel_id=1, source_target_pairs={{0,4},{4,8},{8,12},{12,0},{1,5},{5,9},{9,13},{13,1},{2,6},{6,10},{... | collective-permute-start | bytes 344072 | tf_op jit(solution)/shard_map/ppermute | solution.py:470
  23.3 2.8 %copy-start = (f32[4,224,128]{2,1,0:T(8,128)}, f32[4,224,128]{2,1,0:T(8,128)S(1)}, u32[]{:S(2)}) copy-start(f32[4,224,128]{2,1,0:T(8,128)S(1)} %gather_fusion) | copy-start | bytes 1376260
  23.3 1.9 %collective-permute-start.3 = (f32[4,224,128]{2,1,0:T(8,128)S(1)}, f32[4,224,128]{2,1,0:T(8,128)S(1)}, u32[]{:S(2)}, u32[]{:S(2)}) collective-permute-start(f32[4,224,128]{2,1,0:T(8,128)S(1)} %gather_fusion), channel_id=1, source_target_pairs={{0,1},{1,0},{2,3},{3,2},{4,5},{5,4},{6,7},{7,6},{8,9},{9,8},{10,11... | collective-permute-start | bytes 1376264 | tf_op jit(solution)/shard_map/ppermute | solution.py:470
  23.4 17.2 %collective-permute-start.4 = (f32[4,224,128]{2,1,0:T(8,128)S(1)}, f32[4,224,128]{2,1,0:T(8,128)S(1)}, u32[]{:S(2)}, u32[]{:S(2)}) collective-permute-start(f32[4,224,128]{2,1,0:T(8,128)S(1)} %gather_fusion), channel_id=1, source_target_pairs={{0,2},{1,3},{2,0},{3,1},{4,6},{5,7},{6,4},{7,5},{8,10},{9,11},{10,... | collective-permute-start | bytes 1376264 | tf_op jit(solution)/shard_map/ppermute | solution.py:470
  25.2 0.9 copy-start.6
  40.6 3.0 %copy-start.4 = (f32[4,224,128]{2,1,0:T(8,128)}, f32[4,224,128]{2,1,0:T(8,128)S(1)}, u32[]{:S(2)}) copy-start(f32[4,224,128]{2,1,0:T(8,128)S(1)} %collective-permute-done.4.refs_0_) | copy-start | bytes 1376260
  40.6 1.9 %collective-permute-start.5 = (f32[4,224,128]{2,1,0:T(8,128)S(1)}, f32[4,224,128]{2,1,0:T(8,128)S(1)}, u32[]{:S(2)}, u32[]{:S(2)}) collective-permute-start(f32[4,224,128]{2,1,0:T(8,128)S(1)} %collective-permute-done.4.refs_0_), channel_id=1, source_target_pairs={{0,1},{1,0},{2,3},{3,2},{4,5},{5,4},{6,7},{7,6},{8,9},{9,8},{10,11... | collective-permute-start | bytes 1376264 | tf_op jit(solution)/shard_map/ppermute | solution.py:470
  42.5 1.1 copy-start.5
  85.2 15.9 %collective-permute-start.7 = (f32[4,4,4096]{2,1,0:T(4,128)}, f32[4,4,4096]{2,1,0:T(4,128)S(1)}, u32[]{:S(2)}, u32[]{:S(2)}) collective-permute-start(f32[4,4,4096]{2,1,0:T(4,128)} %get-tuple-element.51), channel_id=1, source_target_pairs={{0,2},{1,3},{2,0},{3,1},{4,6},{5,7},{6,4},{7,5},{8,10},{9,11},{10,... | collective-permute-start | bytes 786440 | tf_op jit(solution)/shard_map/ppermute | solution.py:470
  86.7 15.5 %collective-permute-start.6 = (f32[4,4,4096]{2,1,0:T(4,128)}, f32[4,4,4096]{2,1,0:T(4,128)S(1)}, u32[]{:S(2)}, u32[]{:S(2)}) collective-permute-start(f32[4,4,4096]{2,1,0:T(4,128)} %get-tuple-element.49), channel_id=1, source_target_pairs={{0,2},{1,3},{2,0},{3,1},{4,6},{5,7},{6,4},{7,5},{8,10},{9,11},{10,... | collective-permute-start | bytes 786440 | tf_op jit(solution)/shard_map/ppermute | solution.py:470
  102.2 1.6 %collective-permute-start.8 = (f32[4,4,4096]{2,1,0:T(4,128)S(1)}, f32[4,4,4096]{2,1,0:T(4,128)S(1)}, u32[]{:S(2)}, u32[]{:S(2)}) collective-permute-start(f32[4,4,4096]{2,1,0:T(4,128)S(1)} %add.147), channel_id=1, source_target_pairs={{0,1},{1,0},{2,3},{3,2},{4,5},{5,4},{6,7},{7,6},{8,9},{9,8},{10,11... | collective-permute-start | bytes 786440 | tf_op jit(solution)/shard_map/ppermute | solution.py:470
  105.4 6.4 %collective-permute-start.9 = (f32[4,4096]{1,0:T(4,128)S(1)}, f32[4,4096]{1,0:T(4,128)S(1)}, u32[]{:S(2)}, u32[]{:S(2)}) collective-permute-start(f32[4,4096]{1,0:T(4,128)S(1)} %get-tuple-element.60), channel_id=1, source_target_pairs={{0,4},{4,8},{8,12},{12,0},{1,5},{5,9},{9,13},{13,1},{2,6},{6,10},{... | collective-permute-start | bytes 196616 | tf_op jit(solution)/shard_map/ppermute | solution.py:470
  106.4 7.8 %collective-permute-start.10 = (f32[4,4096]{1,0:T(4,128)S(1)}, f32[4,4096]{1,0:T(4,128)S(1)}, u32[]{:S(2)}, u32[]{:S(2)}) collective-permute-start(f32[4,4096]{1,0:T(4,128)S(1)} %get-tuple-element.59), channel_id=1, source_target_pairs={{0,8},{4,12},{8,0},{12,4},{1,9},{5,13},{9,1},{13,5},{2,10},{6,14},... | collective-permute-start | bytes 196616 | tf_op jit(solution)/shard_map/ppermute | solution.py:470
  107.9 6.4 %collective-permute-start.11 = (f32[4,4096]{1,0:T(4,128)S(1)}, f32[4,4096]{1,0:T(4,128)S(1)}, u32[]{:S(2)}, u32[]{:S(2)}) collective-permute-start(f32[4,4096]{1,0:T(4,128)S(1)} %get-tuple-element.58), channel_id=1, source_target_pairs={{0,12},{4,0},{8,4},{12,8},{1,13},{5,1},{9,5},{13,9},{2,14},{6,2},{... | collective-permute-start | bytes 196616 | tf_op jit(solution)/shard_map/ppermute | solution.py:470
  111.8 2.5 %copy-start.1 = (f32[4,4096]{1,0:T(4,128)}, f32[4,4096]{1,0:T(4,128)S(1)}, u32[]{:S(2)}) copy-start(f32[4,4096]{1,0:T(4,128)S(1)} %collective-permute-done.9.refs_1_) | copy-start | bytes 196612
  114.3 0.6 copy-start.2
  114.3 0.6 copy-start.3
